TPU v7x, 512 devices: a whole 4x8x8 slice. The times are simulated.
512 devices in a mesh: tile: 128 (over y_lo, x, z, core), chan: 4 (over y_hi).
Axes of the slice: x: 4, y: 8 (y_hi: 4, y_lo: 2; y = y_hi * 2 + y_lo), z: 8, core: 2. Of those that a mesh axis runs over, the one named last changes fastest.
Arguments:
- fields: bfloat16 [384, 256, 144], P('tile', 'chan'), may hold values from -6 to 6
- seam_table: int32 [384, 4, 3], replicated, may hold values from 0 to 383, as said below
- w_first: bfloat16 [9, 256, 256], P(None, 'chan'), may hold values from -0.125 to 0.125
- w_down: bfloat16 [9, 256, 256], P(None, 'chan'), may hold values from -0.125 to 0.125
- cotangent: bfloat16 [384, 256, 36], P('tile', 'chan'), may hold values from -6 to 6
Outputs:
- coarse: bfloat16 [384, 256, 36], P('tile', 'chan')
- grad_first: float32 [9, 256, 256], P(None, 'chan')
- grad_down: float32 [9, 256, 256], P(None, 'chan')
- grad_pre: bfloat16 [384, 256, 144], P('tile', 'chan')
Inputs may be any that keep to these rules, and one draw needn't show every extreme that they name: seam_table[t, e] = (n, f, r): the tiles tile the six faces of a cube, each face an equal square grid of tiles, and tile t is held by the device at position t // 3 along tile; tile n lies across edge e of tile t, f is its edge on the shared seam, r is 1 where the two edges run in opposite directions and 0 else; the matching is symmetric, seam_table[n, f] = (t, e, r). Columns 1 and 2 hold 0 to 3 and 0 to 1.
All inputs are finite; a program needn't handle non-finite values.
Results may differ from a plain program's by a relative error of at most 0.023.
Values may be sent and summed in bfloat16 or wider, within the bound.
No kernel may reach another device: no remote copies, remote signals or barrier semaphores. Data moves between devices by JAX's collectives and lax.ppermute only.
A program may use at most 64 MiB of HBM per device.

v0:
```python
import jax
import jax.numpy as jnp
from jax import lax
from jax.sharding import PartitionSpec as P

S = 12
HALF = 6


def edge_strips(values):
    return jnp.stack(
        [values[:, :, 0, :], values[:, :, -1, :], values[:, :, :, 0], values[:, :, :, -1]], axis=1
    )


def flip_where(picked, flipped):
    return jnp.where(flipped[:, :, None, None] == 1, picked[..., ::-1], picked)


def frame_tile(values, picked):
    left_col = picked[:, 2][..., None]
    right_col = picked[:, 3][..., None]
    middle = jnp.concatenate([left_col, values, right_col], axis=3)
    zero_cell = jnp.zeros(values.shape[:2] + (1,), values.dtype)
    top_line = jnp.concatenate([zero_cell, picked[:, 0], zero_cell], axis=2)[:, :, None, :]
    low_line = jnp.concatenate([zero_cell, picked[:, 1], zero_cell], axis=2)[:, :, None, :]
    return jnp.concatenate([top_line, middle, low_line], axis=2)


def pad_tiles(values, own_table):
    gathered = lax.all_gather(edge_strips(values), "tile", axis=0, tiled=True)
    picked = gathered[own_table[:, :, 0], own_table[:, :, 1]]
    return frame_tile(values, flip_where(picked, own_table[:, :, 2]))


def conv_local(padded, weight, stride):
    kernel = weight.reshape(3, 3, weight.shape[1], weight.shape[2])
    return lax.conv_general_dilated(
        padded,
        kernel,
        (stride, stride),
        "VALID",
        dimension_numbers=("NCHW", "HWIO", "NCHW"),
        preferred_element_type=jnp.float32,
    )


def reduce_channels(partial_value):
    return lax.psum_scatter(
        partial_value.astype(jnp.bfloat16), "chan", scatter_dimension=1, tiled=True
    ).astype(jnp.float32)


def gather_channels(values):
    return lax.all_gather(values, "chan", axis=1, tiled=True)


def shards(fields, seam_table, w_first, w_down, cotangent):
    tiles_here, chan_here, cell_count = fields.shape
    total_tiles = lax.axis_size("tile") * tiles_here
    own_table = lax.dynamic_slice_in_dim(
        seam_table, lax.axis_index("tile") * tiles_here, tiles_here, 0
    )
    inputs = fields.reshape(tiles_here, chan_here, S, S)
    padded_in = pad_tiles(inputs, own_table)
    preact = reduce_channels(conv_local(padded_in, w_first, 1))
    hidden = jax.nn.gelu(preact, approximate=True).astype(jnp.bfloat16)
    padded_hid = pad_tiles(hidden, own_table)
    coarse = reduce_channels(conv_local(padded_hid, w_down, 2)).astype(jnp.bfloat16)
    coarse = coarse.reshape(tiles_here, chan_here, HALF * HALF)
    upstream = gather_channels(cotangent)
    down_windows = jnp.stack(
        [
            padded_hid[:, :, tap // 3 : tap // 3 + S : 2, tap % 3 : tap % 3 + S : 2].reshape(
                tiles_here, chan_here, HALF * HALF
            )
            for tap in range(9)
        ],
        0,
    )
    grad_down = jnp.einsum(
        "ktip,top->kio", down_windows, upstream, preferred_element_type=jnp.float32
    ) * float(total_tiles * HALF * HALF) ** (-0.5)
    backward_taps = jnp.einsum(
        "kio,top->ktip", w_down, upstream, preferred_element_type=jnp.float32
    )
    spread = jnp.zeros((tiles_here, chan_here, S + 2, S + 2), jnp.float32)
    for tap in range(9):
        row_at, col_at = (tap // 3, tap % 3)
        spread = spread.at[:, :, row_at : row_at + S : 2, col_at : col_at + S : 2].add(
            backward_taps[tap].reshape(tiles_here, chan_here, HALF, HALF)
        )
    rims = jnp.stack([spread[:, :, 0, 1:-1], spread[:, :, 1:-1, 0]], axis=1).astype(jnp.bfloat16)
    gathered_rims = lax.all_gather(rims, "tile", axis=0, tiled=True)
    facing = own_table[:, :, 1]
    rim_slot = jnp.where(facing == 2, 1, 0)
    rim_keep = jnp.logical_or(facing == 0, facing == 2).astype(jnp.float32)
    picked = (
        gathered_rims[own_table[:, :, 0], rim_slot].astype(jnp.float32) * rim_keep[:, :, None, None]
    )
    picked = flip_where(picked, own_table[:, :, 2])
    grad_hidden = spread[:, :, 1:-1, 1:-1]
    grad_hidden = grad_hidden.at[:, :, 0, :].add(picked[:, 0])
    grad_hidden = grad_hidden.at[:, :, -1, :].add(picked[:, 1])
    grad_hidden = grad_hidden.at[:, :, :, 0].add(picked[:, 2])
    grad_hidden = grad_hidden.at[:, :, :, -1].add(picked[:, 3])
    unused, gelu_back = jax.vjp(lambda value: jax.nn.gelu(value, approximate=True), preact)
    grad_pre = (
        gelu_back(grad_hidden)[0].astype(jnp.bfloat16).reshape(tiles_here, chan_here, cell_count)
    )
    grad_all = gather_channels(grad_pre)
    first_windows = jnp.stack(
        [
            padded_in[:, :, tap // 3 : tap // 3 + S, tap % 3 : tap % 3 + S].reshape(
                tiles_here, chan_here, cell_count
            )
            for tap in range(9)
        ],
        0,
    )
    grad_first = jnp.einsum(
        "ktip,top->kio", first_windows, grad_all, preferred_element_type=jnp.float32
    ) * float(total_tiles * S * S) ** (-0.5)
    grad_first, grad_down = lax.psum((grad_first, grad_down), "tile")
    return (coarse, grad_first, grad_down, grad_pre)


def solution(mesh):
    return jax.shard_map(
        shards,
        mesh=mesh,
        in_specs=(
            P("tile", "chan", None),
            P(),
            P(None, "chan", None),
            P(None, "chan", None),
            P("tile", "chan", None),
        ),
        out_specs=(
            P("tile", "chan", None),
            P(None, "chan", None),
            P(None, "chan", None),
            P("tile", "chan", None),
        ),
        check_vma=False,
    )
```

profile of v0, /device:TPU:1, one launch (start us, length us, event | category | flops | bytes accessed | tf_op | source)
XLA Modules:
  0.0 1914.5 jit_solution(16360569517298930785)
XLA Ops:
  8.3 15.5 all_gather.17
  26.5 2.9 scatter_fusion
  29.4 2.9 scatter_fusion.1
  32.2 2.9 scatter_fusion.2
  35.1 2.9 scatter_fusion.3
  38.0 2.9 scatter_fusion.4
  40.9 2.9 scatter_fusion.5
  43.8 2.9 scatter_fusion.6
  46.6 2.9 scatter_fusion.7
  57.4 217.0 %all-gather.8.cloned.1.call-done = bf16[384,2,64,12]{2,1,3,0:T(2,128)(2,1)} async-done(((bf16[3,2,64,12]{2,1,3,0:T(2,128)(2,1)}), bf16[384,2,64,12]{2,1,3,0:T(2,128)(2,1)}) %all-gather.8.cloned.1.call-update) | async-done | bytes 1179664 | tf_op jit(solution)/shard_map/all_gather | solution.py:94
  279.4 217.6 %all-gather.4.cloned.1.call-done = bf16[384,4,64,12]{2,1,3,0:T(4,128)(2,1)} async-done(((bf16[3,4,64,12]{2,1,3,0:T(4,128)(2,1)}), bf16[384,4,64,12]{2,1,3,0:T(4,128)(2,1)}) %all-gather.4.cloned.1.call-update) | async-done | bytes 2359312 | tf_op jit(solution)/shard_map/all_gather | solution.py:31
  496.9 6.9 copy.307
  503.8 3.4 gather_fusion
  508.7 18.0 copy.389
  526.8 13.5 reshape.280
  545.5 20.0 %reduce-scatter.7.cloned.1.call-done = bf16[64,432]{1,0:T(8,128)(2,1)} async-done(((bf16[256,432]{1,0:T(8,128)(2,1)}), bf16[64,432]{1,0:T(8,128)(2,1)}) %reduce-scatter.7.cloned.1.call-update) | async-done | bytes 55312
  565.5 4.7 reshape.281
  570.1 5.9 copy.316
  585.4 14.5 all_gather.19
  601.1 198.0 %all-gather.6.cloned.1.call-done = bf16[384,4,64,12]{2,1,3,0:T(4,128)(2,1)} async-done(((bf16[3,4,64,12]{2,1,3,0:T(4,128)(2,1)}), bf16[384,4,64,12]{2,1,3,0:T(4,128)(2,1)}) %all-gather.6.cloned.1.call-update) | async-done | bytes 2359312 | tf_op jit(solution)/shard_map/all_gather | solution.py:31
  799.1 6.9 copy.321
  806.0 3.4 gather_fusion.1
  809.8 5.4 slice.328
  815.2 5.4 slice.329
  821.2 5.4 slice.331
  826.6 5.4 slice.333
  832.0 5.4 slice.334
  837.4 5.3 slice.335
  842.8 5.4 slice.336
  849.1 3.8 copy.391
  863.4 17.1 reduce-scatter.9.cloned.1.call-done
  883.0 1020.8 %all-reduce.3.cloned.1.call-done = (f32[9,64,256]{2,1,0:T(8,128)}, f32[9,64,256]{2,1,0:T(8,128)}) async-done(((f32[9,64,256]{2,1,0:T(8,128)}, f32[9,64,256]{2,1,0:T(8,128)}), (f32[9,64,256]{2,1,0:T(8,128)}, f32[9,64,256]{2,1,0:T(8,128)})) %all-reduce.3.cloned.1.call-update) | async-done | bytes 1179664 | tf_op jit(solution)/shard_map/psum | solution.py:124
  (193 shorter events, 51.8 us)
Async XLA Ops:
  7.2 500.4 %copy-start = (bf16[9,64,256]{2,1,0:T(8,128)(2,1)S(1)}, bf16[9,64,256]{2,1,0:T(8,128)(2,1)}, u32[]{:S(2)}) copy-start(bf16[9,64,256]{2,1,0:T(8,128)(2,1)} %param.15) | copy-start | bytes 884740
  7.2 267.2 %all-gather.8.cloned.1.call-start = ((), (), s32[]{:S(2)}) async-start(), calls=%async_computation.4 | async-start | bytes 2377728 | tf_op jit(solution)/shard_map/all_gather | solution.py:94
  23.8 1.5 copy-start.1
  40.9 12.3 copy-start.4
  53.2 443.8 %all-gather.4.cloned.1.call-start = ((), (), s32[]{:S(2)}) async-start(), calls=%async_computation.2 | async-start | bytes 4755456 | tf_op jit(solution)/shard_map/all_gather | solution.py:31
  53.4 4.0 copy-start.2
  54.2 511.3 %reduce-scatter.7.cloned.1.call-start = ((), (), s32[]{:S(2)}) async-start(), calls=%async_computation.5 | async-start | bytes 327680
  56.3 450.9 %copy-start.14 = (pred[3,4,1]{1,0,2:T(4,128)(4,1)}, pred[3,4,1]{1,0,2:T(4,128)(4,1)S(1)}, u32[]{:S(2)}) copy-start(pred[3,4,1]{1,0,2:T(4,128)(4,1)S(1)} %copy.302) | copy-start | bytes 40
  279.4 228.7 %copy-start.3 = (bf16[3,64,144]{1,0,2:T(4,128)(2,1)S(1)}, bf16[3,64,144]{1,0,2:T(4,128)(2,1)}, u32[]{:S(2)}) copy-start(bf16[3,64,144]{1,0,2:T(4,128)(2,1)} %copy-done.2) | copy-start | bytes 165892
  507.5 0.6 copy-start.12
  507.5 19.3 %copy-start.10 = (bf16[3,64,1,14]{1,0,3,2:T(4,128)(2,1)}, bf16[3,64,1,14]{1,0,3,2:T(4,128)(2,1)S(1)}, u32[]{:S(2)}) copy-start(bf16[3,64,1,14]{1,0,3,2:T(4,128)(2,1)S(1)} %copy.314) | copy-start | bytes 16132
  507.5 19.2 %copy-start.11 = (bf16[3,64,1,14]{1,0,3,2:T(4,128)(2,1)}, bf16[3,64,1,14]{1,0,3,2:T(4,128)(2,1)S(1)}, u32[]{:S(2)}) copy-start(bf16[3,64,1,14]{1,0,3,2:T(4,128)(2,1)S(1)} %copy.313) | copy-start | bytes 16132
  507.6 19.2 %copy-start.9 = (bf16[3,64,12,1]{1,0,3,2:T(4,128)(2,1)}, bf16[3,64,12,1]{1,0,3,2:T(4,128)(2,1)S(1)}, u32[]{:S(2)}) copy-start(bf16[3,64,12,1]{1,0,3,2:T(4,128)(2,1)S(1)} %get-tuple-element.145) | copy-start | bytes 13828
  540.3 258.8 %all-gather.6.cloned.1.call-start = ((), (), s32[]{:S(2)}) async-start(), calls=%async_computation.3 | async-start | bytes 4755456 | tf_op jit(solution)/shard_map/all_gather | solution.py:31
  570.1 13.9 copy-start.5
  578.1 302.3 %reduce-scatter.9.cloned.1.call-start = ((), (), s32[]{:S(2)}) async-start(), calls=%async_computation.6 | async-start | bytes 81920
  584.7 221.3 %copy-start.6 = (bf16[3,64,144]{2,1,0:T(8,128)(2,1)}, bf16[3,64,144]{2,1,0:T(8,128)(2,1)S(1)}, u32[]{:S(2)}) copy-start(bf16[3,64,144]{2,1,0:T(8,128)(2,1)S(1)} %copy.363) | copy-start | bytes 165892
  601.1 208.3 %copy-start.15 = (pred[3,4,1]{1,0,2:T(4,128)(4,1)S(1)}, pred[3,4,1]{1,0,2:T(4,128)(4,1)}, u32[]{:S(2)}) copy-start(pred[3,4,1]{1,0,2:T(4,128)(4,1)} %copy-done.14) | copy-start | bytes 40
  601.1 208.5 %copy-start.13 = (bf16[3,64,1]{1,2,0:T(2,128)(2,1)S(1)}, bf16[3,64,1]{1,2,0:T(2,128)(2,1)}, u32[]{:S(2)}) copy-start(bf16[3,64,1]{1,2,0:T(2,128)(2,1)} %copy-done.12) | copy-start | bytes 1156
  601.1 247.0 %copy-start.7 = (bf16[9,64,256]{2,1,0:T(8,128)(2,1)S(1)}, bf16[9,64,256]{2,1,0:T(8,128)(2,1)}, u32[]{:S(2)}) copy-start(bf16[9,64,256]{2,1,0:T(8,128)(2,1)} %param.16) | copy-start | bytes 884740
  809.7 52.6 %copy-start.8 = (bf16[3,256,36]{1,2,0:T(8,128)(2,1)S(1)}, bf16[3,256,36]{1,2,0:T(8,128)(2,1)}, u32[]{:S(2)}) copy-start(bf16[3,256,36]{1,2,0:T(8,128)(2,1)} %copy.364) | copy-start | bytes 165892
  855.7 1048.1 %all-reduce.3.cloned.1.call-start = ((), (), s32[]{:S(2)}) async-start(), calls=%async_computation.7 | async-start | bytes 2359296 | tf_op jit(solution)/shard_map/psum | solution.py:124
Sparse Core Ops, SparseCore 0:
  53.3 221.0 all-gather.7
  277.1 219.7 all-gather.3
  540.4 25.0 reduce-scatter.6
  578.2 220.8 all-gather.5
  855.8 24.5 reduce-scatter.8
  883.9 1019.9 all-reduce.2
where the time goes:
time: 1920 us; the launch traced here: 1910 us
  waiting for transfers between devices  1690 us (88%)
  local copies, waits for them, and re-layouts  137 us (7%)
  other arithmetic  36 us (2%)
  blocking collectives  30 us (2%)
    psum x1, waiting for transfers between devices, shards(): grad_first, grad_down = lax.psum((grad_first, grad_down), 'tile')  1020 us
    all_gather x2, waiting for transfers between devices, pad_tiles(): gathered = lax.all_gather(edge_strips(values), 'tile', axis=0, tiled=True)  416 us
    all_gather x1, waiting for transfers between devices, shards(): gathered_rims = lax.all_gather(rims, 'tile', axis=0, tiled=True)  217 us
    unnamed x66, local copies, waits for them, and re-layouts  52.4 us
    slice x9, local copies, waits for them, and re-layouts, shards(): padded_hid[:, :, tap // 3:tap // 3 + S:2, tap % 3:tap % 3 + S:2]  38.7 us
  transfers between devices with their start and end apart: 6, of which 6 were waited for; matrix products, arithmetic and copies ran while one was open for 2% of the time, Pallas kernels for 0%

commit v1 on v0

v1 whole, which is shorter than its diff:
```python
import numpy as np
import jax
import jax.numpy as jnp
from jax import lax
from jax.experimental import pallas as pl
from jax.experimental.pallas import tpu as pltpu
from jax.sharding import Mesh, PartitionSpec as P

S = 12
HALF = 6
CELLS = 144
COARSE = 36
TILES_HERE = 3
CH = 64
C = 256
YLO, NX, NZ, CORE, CHAN = 2, 4, 8, 2, 4
PLANE = NX * NZ
QUAD = YLO * CORE
TILE_AXES = ("ylo", "x", "z", "core")
BF = jnp.bfloat16
F32 = jnp.float32

EDGE_ROWS = (0, 28, 14, 34)
FIELD_ROWS = 40
BLOCK_ROWS = 52
SEND_ROWS = 160
OWN_ROWS = 72
X_HALF = OWN_ROWS + FIELD_ROWS
C_OWN = 18
C_HALF = 32
PAY_ROWS = X_HALF + C_HALF
PACK_ROWS = 96
UNIT = 16
PRE_ROWS = 176
DOWN_ROWS = 48
SPREAD_ROWS = 192


def strip_cells(edge, depth):
    if edge == 0:
        return [depth * S + i for i in range(S)]
    if edge == 1:
        return [(S - 1 - depth) * S + i for i in range(S)]
    if edge == 2:
        return [i * S + depth for i in range(S)]
    return [i * S + S - 1 - depth for i in range(S)]


def pack_selectors():
    rows = PACK_ROWS + 4 * UNIT
    fields = np.zeros((2, rows, CELLS), np.float32)
    coarse = np.zeros((2, rows, COARSE), np.float32)
    for half in range(2):
        for row in range(OWN_ROWS):
            fields[half, row, 2 * row + half] = 1
        for row in range(C_OWN):
            coarse[half, OWN_ROWS + row, 2 * row + half] = 1
        for edge in range(4):
            base = PACK_ROWS + edge * UNIT
            near, far = strip_cells(edge, 0), strip_cells(edge, 1)
            for row in range(6):
                fields[half, base + row, near[2 * row + half]] = 1
                fields[half, base + 9 + row, far[2 * row + half]] = 1
            for row in range(3):
                at = 2 * row + half
                if edge == 0:
                    coarse[half, base + 6 + row, at] = 1
                if edge == 2:
                    coarse[half, base + 6 + row, at * HALF] = 1
            fields[half, base + 15, near[11 - half]] = 1
    return fields, coarse


def own_at(cell):
    return cell // 2 + X_HALF * (cell % 2)


def near_at(edge, along, depth):
    row = OWN_ROWS + EDGE_ROWS[edge] + 6 * depth
    if along < 0:
        return OWN_ROWS + EDGE_ROWS[edge] + 12 + X_HALF * depth
    if along >= S:
        return OWN_ROWS + EDGE_ROWS[edge] + 13 + X_HALF * depth
    return row + along // 2 + X_HALF * (along % 2)


def window_index():
    fixed = np.zeros((9, PRE_ROWS), np.float32)
    varied = np.zeros((4, 4, 2, 9, PRE_ROWS), np.float32)
    for k in range(9):
        a, b = k // 3, k % 3
        for cell in range(CELLS):
            row, col = cell // S + a, cell % S + b
            inner_row, inner_col = 1 <= row <= S, 1 <= col <= S
            if inner_row and inner_col:
                fixed[k, cell] = 1 + own_at((row - 1) * S + col - 1)
            elif inner_row or inner_col:
                edge = (2 if col == 0 else 3) if inner_row else (0 if row == 0 else 1)
                at = row - 1 if inner_row else col - 1
                for flip in range(2):
                    varied[edge, :, flip, k, cell] = 1 + near_at(edge, 11 - at if flip else at, 0)
        for slot, edge in enumerate((0, 2)):
            own = strip_cells(edge, 0)
            for facing in range(4):
                depth = (a - 1, 1 - a, b - 1, 1 - b)[facing]
                shift = (b - 1, b - 1, a - 1, a - 1)[facing]
                for flip in range(2):
                    for j in range(S):
                        along = (11 - j if flip else j) + shift
                        if depth >= 0:
                            at = near_at(edge, along, depth)
                        elif 0 <= along < S:
                            at = own_at(own[11 - along if flip else along])
                        else:
                            continue
                        varied[edge, facing, flip, k, CELLS + 16 * slot + j] = 1 + at
    return fixed.reshape(-1), varied.reshape(32, -1)


def spread_index():
    fixed = np.zeros((9, SPREAD_ROWS), np.float32)
    varied = np.zeros((4, 4, 2, 9, SPREAD_ROWS), np.float32)
    for k in range(9):
        a, b = k // 3, k % 3
        for cell in range(CELLS):
            row, col = cell // S + 1 - a, cell % S + 1 - b
            if row % 2 == 0 and col % 2 == 0 and 0 <= row < S and 0 <= col < S:
                at = (row // 2) * HALF + col // 2
                fixed[k, cell] = 1 + at // 2 + C_HALF * (at % 2)
        for edge in range(4):
            for flip in range(2):
                for j in range(S):
                    for facing, live, tap in ((0, a == 0, b), (2, b == 0, a)):
                        at = (11 - j if flip else j) + 1 - tap
                        if live and at % 2 == 0 and 0 <= at < S:
                            at //= 2
                            varied[edge, facing, flip, k, CELLS + edge * S + j] = (
                                1 + C_OWN + 3 * edge + at // 2 + C_HALF * (at % 2)
                            )
    return fixed.reshape(-1), varied.reshape(32, -1)


def down_selector():
    chosen = np.zeros((9, DOWN_ROWS, PRE_ROWS), np.float32)
    for k in range(9):
        for cell in range(COARSE):
            row, col = 2 * (cell // HALF) + k // 3, 2 * (cell % HALF) + k % 3
            if row == 0 and col == 0:
                continue
            if row == 0:
                at = CELLS + col - 1
            elif col == 0:
                at = CELLS + 16 + row - 1
            else:
                at = (row - 1) * S + col - 1
            chosen[k, cell, at] = 1
    return chosen.reshape(9 * DOWN_ROWS, PRE_ROWS)


def rim_selector():
    chosen = np.zeros((CELLS, 4 * S), np.float32)
    for edge in range(4):
        for j, cell in enumerate(strip_cells(edge, 0)):
            chosen[cell, edge * S + j] = 1
    return chosen


def order_selector():
    chosen = np.zeros((DOWN_ROWS, 2 * C_HALF), np.float32)
    for cell in range(COARSE):
        chosen[cell, cell // 2 + C_HALF * (cell % 2)] = 1
    return chosen


def dot_nn(left, right):
    return lax.dot_general(left, right, (((1,), (0,)), ((), ())), preferred_element_type=F32)


def dot_nt(left, right):
    return lax.dot_general(left, right, (((1,), (1,)), ((), ())), preferred_element_type=F32)


def pack_kernel(fields_ref, cot_ref, self_ref, selc_ref, own_ref, unit_ref):
    for t in range(TILES_HERE):
        halves = [
            (dot_nt(self_ref[h], fields_ref[t]) + dot_nt(selc_ref[h], cot_ref[t])).astype(BF)
            for h in range(2)
        ]
        for h in range(2):
            own_ref[t, :, h * CH : (h + 1) * CH] = halves[h][:PACK_ROWS]
            unit_ref[t * 4 * UNIT : (t + 1) * 4 * UNIT, h * CH : (h + 1) * CH] = halves[h][PACK_ROWS:]


def edge_row(edge):
    return jnp.where(edge < 2, edge * 28, 14 + (edge - 2) * 20)


def place_kernel(table_ref, me_ref, unit_ref, out_ref, source, sent):
    ylo, x, z, core = me_ref[0], me_ref[1], me_ref[2], me_ref[3]
    for s in range(QUAD):
        source[s * 192 : (s + 1) * 192, :] = unit_ref[s].astype(F32)
    sent[...] = jnp.zeros_like(sent)

    def target(tile, wanted):
        device = tile // TILES_HERE
        slot = tile - device * TILES_HERE
        mine = jnp.logical_and(device % CORE == core, device // (CORE * PLANE) == ylo)
        place = jnp.where(jnp.logical_and(mine, wanted), (device // CORE) % PLANE, PLANE)
        return place, slot * BLOCK_ROWS

    def body(i, carry):
        s = i // 12
        device = (((s // CORE) * NX + x) * NZ + z) * CORE + s % CORE
        at = (device * TILES_HERE * 4 + i % 12) * 3
        n, p, r = table_ref[at], table_ref[at + 1], table_ref[at + 2]
        base = pl.multiple_of(i * UNIT, UNIT)
        place, rows = target(n, True)
        sent[place, pl.ds(rows + edge_row(p), 6), :] = source[pl.ds(base, 6), :]
        sent[place, pl.ds(rows + FIELD_ROWS + 3 * p, 3), :] = source[pl.ds(base + 6, 3), :]
        deep = jnp.where(p % 2 == 0, place, PLANE)
        sent[deep, pl.ds(rows + edge_row(p) + 6, 6), :] = source[pl.ds(base + 9, 6), :]
        for last in range(2):
            f = jnp.where(p >= 2, 0, 2) + last
            beyond = (n * 4 + f) * 3
            t2, e2 = table_ref[beyond], table_ref[beyond + 1]
            place2, rows2 = target(t2, e2 % 2 == 0)
            end = base + jnp.where(r == last, 0, 15)
            sent[place2, pl.ds(rows2 + edge_row(e2) + 12 + p % 2, 1), :] = source[pl.ds(end, 1), :]
        return carry

    lax.fori_loop(0, QUAD * 12, body, 0)
    out_ref[...] = sent[:PLANE].astype(BF)


def join_kernel(got_ref, own_ref, out_ref, rows):
    total = got_ref[0].astype(F32)
    for q in range(1, PLANE):
        total = total + got_ref[q].astype(F32)
    for t in range(TILES_HERE):
        base, block = t * PAY_ROWS, t * BLOCK_ROWS
        own = own_ref[t].astype(F32)
        rows[base : base + OWN_ROWS, :] = own[:OWN_ROWS]
        rows[base + OWN_ROWS : base + X_HALF, :] = total[block : block + FIELD_ROWS]
        rows[base + X_HALF : base + X_HALF + C_OWN, :] = own[OWN_ROWS : OWN_ROWS + C_OWN]
        rows[base + X_HALF + C_OWN : base + PAY_ROWS - 2, :] = total[block + FIELD_ROWS : block + BLOCK_ROWS]
        rows[base + PAY_ROWS - 2 : base + PAY_ROWS, :] = jnp.zeros((2, 128), F32)
    whole = rows[...].astype(BF)
    for c in range(CHAN):
        out_ref[c] = whole


def main_kernel(
    me_ref, pay_ref, window_ref, lift_ref, down_ref, rim_ref, order_ref, wf_ref, wd_ref,
    coarse_ref, gp_ref, grads_ref, xs, cs, wf, wd, wins, lifts,
):
    chan = me_ref[4]
    pick = jnp.where(
        lax.broadcasted_iota(jnp.int32, (CH, C), 1) == lax.broadcasted_iota(jnp.int32, (CH, C), 0) + chan * CH, 1.0, 0.0
    ).astype(BF)
    for c in range(CHAN):
        for k in range(9):
            wf[k, c * CH : (c + 1) * CH, :] = wf_ref[c, k]
            wd[k, c * CH : (c + 1) * CH, :] = wd_ref[c, k]
        for t in range(TILES_HERE):
            base = t * PAY_ROWS
            for h in range(2):
                lanes = slice(h * CH, (h + 1) * CH)
                xs[t, h * X_HALF : (h + 1) * X_HALF, c * CH : (c + 1) * CH] = pay_ref[c, base : base + X_HALF, lanes]
                cs[t, h * C_HALF : (h + 1) * C_HALF, c * CH : (c + 1) * CH] = pay_ref[
                    c, base + X_HALF : base + PAY_ROWS, lanes
                ]
    for t in range(TILES_HERE):
        xs[t, 2 * X_HALF :, :] = jnp.zeros((C - 2 * X_HALF, C), BF)
    for k in range(9):
        for t in range(TILES_HERE):
            wins[k, t * PRE_ROWS : (t + 1) * PRE_ROWS, :] = dot_nn(
                window_ref[t, k * PRE_ROWS : (k + 1) * PRE_ROWS, :], xs[t]
            ).astype(BF)
            lifts[k, t * SPREAD_ROWS : (t + 1) * SPREAD_ROWS, :] = dot_nn(
                lift_ref[t, k * SPREAD_ROWS : (k + 1) * SPREAD_ROWS, :], cs[t]
            ).astype(BF)
    pre = dot_nn(wins[0], wf[0])
    back = dot_nt(lifts[0], wd[0])
    for k in range(1, 9):
        pre = pre + dot_nn(wins[k], wf[k])
        back = back + dot_nt(lifts[k], wd[k])
    scale = np.float32(np.sqrt(2 / np.pi))
    squared = pre * pre
    bent = jnp.tanh(scale * (pre + np.float32(0.044715) * squared * pre))
    gate = 0.5 * (1.0 + bent)
    hidden = (pre * gate).astype(BF)
    slope = gate + 0.5 * pre * (1.0 - bent * bent) * scale * (1.0 + np.float32(3 * 0.044715) * squared)

    down = [None] * TILES_HERE
    first_sum = None
    down_sum = None
    for t in range(TILES_HERE):
        own_hidden = hidden[t * PRE_ROWS : (t + 1) * PRE_ROWS]
        coarse = None
        windows = dot_nn(down_ref[...], own_hidden).astype(BF)
        for k in range(9):
            part = dot_nn(windows[k * DOWN_ROWS : (k + 1) * DOWN_ROWS], wd[k])
            coarse = part if coarse is None else coarse + part
        coarse_ref[t] = dot_nt(pick, coarse.astype(BF))[:, :COARSE].astype(BF)

        rows = back[t * SPREAD_ROWS : (t + 1) * SPREAD_ROWS]
        rims = rows[CELLS:].astype(BF)
        grad_hidden = rows[:CELLS] + dot_nn(rim_ref[...], rims)
        grad_pre = (grad_hidden * slope[t * PRE_ROWS : t * PRE_ROWS + CELLS]).astype(BF)
        gp_ref[t] = dot_nt(pick, grad_pre).astype(BF)

        x_own = dot_nt(pick, xs[t]).astype(BF)
        h_own = dot_nt(pick, own_hidden).astype(BF)
        up = dot_nn(order_ref[...], cs[t]).astype(BF)
        first_parts, down_parts = [], []
        for k in range(9):
            first_parts.append(
                dot_nt(x_own, window_ref[t, k * PRE_ROWS : k * PRE_ROWS + CELLS, :]).astype(BF)
            )
            down_parts.append(
                dot_nt(h_own, down_ref[k * DOWN_ROWS : (k + 1) * DOWN_ROWS, :]).astype(BF)
            )
        first = dot_nn(jnp.concatenate(first_parts, axis=0), grad_pre)
        first_sum = first if first_sum is None else first_sum + first
        part = dot_nn(jnp.concatenate(down_parts, axis=0), up)
        down_sum = part if down_sum is None else down_sum + part
    grads_ref[: 9 * CH, :] = first_sum.astype(BF)
    grads_ref[9 * CH :, :] = down_sum.astype(BF)


def vmem(count):
    return [pl.BlockSpec(memory_space=pltpu.VMEM)] * count


def smem(count):
    return [pl.BlockSpec(memory_space=pltpu.SMEM)] * count


LIMIT = pltpu.CompilerParams(vmem_limit_bytes=48 * 1024 * 1024)


def shards(fields, seam_table, w_first, w_down, cotangent):
    coords = [lax.axis_index(axis) for axis in ("ylo", "x", "z", "core", "chan")]
    me = jnp.stack(coords).astype(jnp.int32)
    all_first = lax.all_gather(w_first, "chan", axis=0, tiled=False)
    all_down = lax.all_gather(w_down, "chan", axis=0, tiled=False)

    sel_fields, sel_coarse = pack_selectors()
    own, units = pl.pallas_call(
        pack_kernel,
        out_shape=(
            jax.ShapeDtypeStruct((TILES_HERE, PACK_ROWS, 128), BF),
            jax.ShapeDtypeStruct((TILES_HERE * 4 * UNIT, 128), BF),
        ),
        in_specs=vmem(4),
        out_specs=tuple(vmem(2)),
        compiler_params=LIMIT,
        name="pack",
    )(fields, cotangent, jnp.asarray(sel_fields, BF), jnp.asarray(sel_coarse, BF))
    quad = lax.all_gather(units, ("ylo", "core"), axis=0, tiled=False)
    table = seam_table.reshape(-1)
    sends = pl.pallas_call(
        place_kernel,
        out_shape=jax.ShapeDtypeStruct((PLANE, SEND_ROWS, 128), BF),
        in_specs=smem(2) + vmem(1),
        out_specs=vmem(1)[0],
        scratch_shapes=[pltpu.VMEM((QUAD * 192, 128), F32), pltpu.VMEM((PLANE + 1, SEND_ROWS, 128), F32)],
        compiler_params=LIMIT,
        name="place",
    )(table, me, quad)
    got = lax.all_to_all(sends, ("x", "z"), 0, 0)
    joined = pl.pallas_call(
        join_kernel,
        out_shape=jax.ShapeDtypeStruct((CHAN, TILES_HERE * PAY_ROWS, 128), BF),
        in_specs=vmem(2),
        out_specs=vmem(1)[0],
        scratch_shapes=[pltpu.VMEM((TILES_HERE * PAY_ROWS, 128), F32)],
        compiler_params=LIMIT,
        name="join",
    )(got, own)
    payload = lax.all_to_all(joined, "chan", 0, 0)

    tile_at = ((coords[0] * NX + coords[1]) * NZ + coords[2]) * CORE + coords[3]
    own_table = lax.dynamic_slice_in_dim(seam_table, tile_at * TILES_HERE, TILES_HERE, 0)
    code = own_table[:, :, 1] * 2 + own_table[:, :, 2]
    chosen = (code[:, :, None] == jnp.arange(8, dtype=jnp.int32)).astype(BF).reshape(TILES_HERE, 32)
    one_hots = []
    for (fixed, varied), depth in ((window_index(), C), (spread_index(), 2 * C_HALF)):
        at = jnp.dot(chosen, jnp.asarray(varied, BF), preferred_element_type=F32) + jnp.asarray(fixed, F32)
        one_hots.append((at[:, :, None] == jnp.arange(1, depth + 1, dtype=jnp.int32).astype(F32)).astype(BF))

    coarse, grad_pre, grads = pl.pallas_call(
        main_kernel,
        out_shape=(
            jax.ShapeDtypeStruct((TILES_HERE, CH, COARSE), BF),
            jax.ShapeDtypeStruct((TILES_HERE, CH, CELLS), BF),
            jax.ShapeDtypeStruct((18 * CH, C), BF),
        ),
        in_specs=smem(1) + vmem(8),
        out_specs=tuple(vmem(3)),
        scratch_shapes=[
            pltpu.VMEM((TILES_HERE, C, C), BF),
            pltpu.VMEM((TILES_HERE, 2 * C_HALF, C), BF),
            pltpu.VMEM((9, C, C), BF),
            pltpu.VMEM((9, C, C), BF),
            pltpu.VMEM((9, TILES_HERE * PRE_ROWS, C), BF),
            pltpu.VMEM((9, TILES_HERE * SPREAD_ROWS, C), BF),
        ],
        compiler_params=LIMIT,
        name="tiles",
    )(
        me, payload, one_hots[0], one_hots[1], jnp.asarray(down_selector(), BF), jnp.asarray(rim_selector(), BF),
        jnp.asarray(order_selector(), BF), all_first, all_down,
    )

    part = lax.all_to_all(grads.reshape(QUAD, 18 * CH // QUAD, C), ("ylo", "core"), 0, 0)
    part = part.astype(F32).sum(0).astype(BF).reshape(PLANE, 18, 128)
    part = lax.all_to_all(part, ("x", "z"), 0, 0)
    part = part.astype(F32).sum(0).astype(BF)
    part = lax.all_to_all(jnp.broadcast_to(part[None], (PLANE, 18, 128)), ("x", "z"), 0, 0)
    whole = lax.all_gather(part.reshape(18 * CH // QUAD, C), ("ylo", "core"), axis=0, tiled=True)
    whole = whole.astype(F32).reshape(2, 9, CH, C)
    tiles = TILES_HERE * PLANE * QUAD
    return (
        coarse,
        whole[0] * float(tiles * CELLS) ** (-0.5),
        whole[1] * float(tiles * COARSE) ** (-0.5),
        grad_pre,
    )


def solution(mesh):
    fine = Mesh(mesh.devices.reshape(YLO, NX, NZ, CORE, CHAN), ("ylo", "x", "z", "core", "chan"))
    return jax.shard_map(
        shards,
        mesh=fine,
        in_specs=(
            P(TILE_AXES, "chan", None),
            P(),
            P(None, "chan", None),
            P(None, "chan", None),
            P(TILE_AXES, "chan", None),
        ),
        out_specs=(
            P(TILE_AXES, "chan", None),
            P(None, "chan", None),
            P(None, "chan", None),
            P(TILE_AXES, "chan", None),
        ),
        check_vma=False,
    )
```

time: 1920 us -> 179 us (0.09)
  waiting for transfers between devices: 1690 us -> 62.5 us
  local copies, waits for them, and re-layouts: 137 us -> 7.29 us
  other arithmetic: 36 us -> 4.88 us
  blocking collectives: 30 us -> 52.5 us
  starting transfers between devices: 0.43 us -> 19.9 us
    psum x1 -> x0, waiting for transfers between devices: 1020 us -> none  [shards(): grad_first, grad_down = lax.psum((grad_first, grad_down), 'tile')]
    all_gather x3 -> x2, waiting for transfers between devices: 633 us -> 23.6 us  [the longest x1 23.6 us: shards(): all_down = lax.all_gather(w_down, 'chan', axis=0, tiled=False)]
    unnamed x66 -> x27, local copies, waits for them, and re-layouts: 52.4 us -> 5.22 us
    slice x17 -> x0, local copies, waits for them, and re-layouts: 39.2 us -> none  [the longest x9 38.7 us: shards(): padded_hid[:, :, tap // 3:tap // 3 + S:2, tap % 3:tap % 3 + S:2]]
    all_to_all x0 -> x3, waiting for transfers between devices: none -> 37.5 us  [the longest x1 28.8 us: shards(): got = lax.all_to_all(sends, ('x', 'z'), 0, 0)]
    unnamed x8 -> x2, waiting for transfers between devices: 37.1 us -> 1.38 us
    all_to_all x0 -> x2, blocking collectives: none -> 30.7 us  [the longest x1 18.6 us: shards(): part = lax.all_to_all(part, ('x', 'z'), 0, 0)]
    scatter-add x11 -> x0, other arithmetic: 27.8 us -> none  [the longest x9 25.8 us: shards(): spread.at[:, :, row_at:row_at + S:2, col_at:col_at + S:2]]
  transfers between devices with their start and end apart: 6 -> 5, of which waited for: 6 -> 3; matrix products, arithmetic and copies ran while one was open for 2% -> 4% of each run, Pallas kernels for 0% -> 5%
where the time goes in v1:
time: 179 us
  waiting for transfers between devices  62.5 us (35%)
  blocking collectives  52.5 us (29%)
  starting transfers between devices  19.9 us (11%)
  Pallas kernels  17.3 us (10%)
  between operations  14.2 us (8%)
  local copies, waits for them, and re-layouts  7.29 us (4%)
  other arithmetic  4.88 us (3%)
    all_to_all x1, waiting for transfers between devices, shards(): got = lax.all_to_all(sends, ('x', 'z'), 0, 0)  28.8 us
    all_gather x1, waiting for transfers between devices, shards(): all_down = lax.all_gather(w_down, 'chan', axis=0, tiled=False)  23.6 us
    all_to_all x1, blocking collectives, shards(): part = lax.all_to_all(part, ('x', 'z'), 0, 0)  18.6 us
    all_gather x1, blocking collectives, shards(): quad = lax.all_gather(units, ('ylo', 'core'), axis=0, tiled=False)  12.3 us
    all_to_all x1, blocking collectives, shards(): lax.all_to_all(grads.reshape(QUAD, 18 * CH // QUAD, C), ('ylo', 'core'),...  12 us
    all_gather x1, blocking collectives, shards(): lax.all_gather(part.reshape(18 * CH // QUAD, C), ('ylo', 'core'), axis=0,...  9.52 us
    all_to_all x1, waiting for transfers between devices, shards(): lax.all_to_all(jnp.broadcast_to(part[None], (PLANE, 18, 128)), ('x', 'z')...  8.67 us
    pallas_call x1, Pallas kernels, shards(): pl.pallas_call(main_kernel, out_shape=(jax.ShapeDtypeStruct((TILES_HERE,...  8.6 us
  transfers between devices with their start and end apart: 5, of which 3 were waited for; matrix products, arithmetic and copies ran while one was open for 4% of the time, Pallas kernels for 5%

profile of v1, /device:TPU:1, one launch (start us, length us, event | category | flops | bytes accessed | tf_op | source)
XLA Modules:
  0.0 178.8 jit_solution(8840169497102636478)
XLA Ops:
  7.2 0.7 all-gather.6.cloned.1.call-update
  7.9 0.9 copy.26.cot_ref
  8.8 1.1 copy.25
  9.9 0.8 reshape.47.table_ref
  10.6 0.4 pack.1
  11.1 12.3 %all-gather = bf16[768,128]{1,0:T(8,128)(2,1)S(1)} all-gather(bf16[192,128]{1,0:T(8,128)(2,1)S(1)} %get-tuple-element.9), channel_id=2, replica_groups=mesh['ylo'=2,'x'=4,'z'=8,'core'=2,'chan'=4] {'ylo','core'}, dimensions={0}, use_global_device_ids=true | all-gather | bytes 245760 | tf_op jit(solution)/shard_map/all_gather | solution.py:360
  23.4 7.3 %place.1 = bf16[32,160,128]{2,1,0:T(8,128)(2,1)} custom-call(s32[4608]{0:T(1024)S(1)} %reshape.47.table_ref, s32[5]{0:T(128)S(1)} %stack.23.me_ref, bf16[4,192,128]{2,1,0:T(8,128)(2,1)S(1)} %bitcast.18), custom_call_target="tpu_custom_call" | custom-call | tf_op jit(solution)/shard_map/place/pallas_call | solution.py:362
  30.8 7.6 %all-to-all-start = ((bf16[32,160,128]{2,1,0:T(8,128)(2,1)}), bf16[32,160,128]{2,1,0:T(8,128)(2,1)S(1)}, u32[]{:S(2)}, u32[]{:S(2)}) async-start(bf16[32,160,128]{2,1,0:T(8,128)(2,1)} %place.1), calls=%async_computation | async-start | bytes 2621440 | tf_op jit(solution)/shard_map/all_to_all | solution.py:371
  38.5 0.7 all-gather.8.cloned.1.call-update
  39.2 0.8 dynamic-slice_add_fusion
  40.0 0.1 copy.27
  40.3 0.1 convolution_add_fusion.1
  40.5 0.9 compare_convert_fusion.1.lift_ref
  41.4 28.8 %all-to-all-done.got_ref = bf16[32,160,128]{2,1,0:T(8,128)(2,1)S(1)} async-done(((bf16[32,160,128]{2,1,0:T(8,128)(2,1)}), bf16[32,160,128]{2,1,0:T(8,128)(2,1)S(1)}, u32[]{:S(2)}, u32[]{:S(2)}) %all-to-all-start) | async-done | bytes 1310752 | tf_op jit(solution)/shard_map/all_to_all | solution.py:371
  70.2 0.9 join.1
  71.1 6.8 %all-to-all-start.1 = ((bf16[4,432,128]{2,1,0:T(8,128)(2,1)}), bf16[4,432,128]{2,1,0:T(8,128)(2,1)S(1)}, u32[]{:S(2)}, u32[]{:S(2)}) async-start(bf16[4,432,128]{2,1,0:T(8,128)(2,1)} %join.1), calls=%async_computation.1 | async-start | bytes 884736 | tf_op jit(solution)/shard_map/all_to_all | solution.py:381
  78.0 0.1 convolution_add_fusion
  78.1 1.9 %compare_convert_fusion.window_ref = bf16[3,1584,256]{2,1,0:T(8,128)(2,1)} fusion(f32[256]{0:T(256)S(1)} %add_convert_fusion, f32[3,1584]{1,0:T(4,128)S(1)} %convolution_add_fusion), kind=kLoop, calls=%fused_computation | loop fusion | flops 2433024 | bytes 2453056 | tf_op jit(solution)/shard_map/convert_element_type | solution.py:390
  80.0 23.6 %all-gather.8.cloned.1.call-done = bf16[36,64,256]{2,1,0:T(8,128)(2,1)} async-done(((bf16[9,64,256]{2,1,0:T(8,128)(2,1)}), bf16[36,64,256]{2,1,0:T(8,128)(2,1)}) %all-gather.8.cloned.1.call-update) | async-done | bytes 1179664 | tf_op jit(solution)/shard_map/all_gather | solution.py:346
  103.6 1.3 copy-done
  104.9 1.3 copy-done.1
  106.2 8.6 %tiles.1 = (bf16[3,64,36]{2,1,0:T(8,128)(2,1)S(1)}, bf16[3,64,144]{2,1,0:T(8,128)(2,1)}, bf16[1152,256]{1,0:T(8,128)(2,1)S(1)}) custom-call(s32[5]{0:T(128)S(1)} %stack.23.me_ref, bf16[4,432,128]{2,1,0:T(8,128)(2,1)S(1)} %all-to-all-done.1.pay_ref, bf16[3,1584,256]{2,1,0:T(8,128)(2,1)} %compare_convert_fusion.window_ref, ...), custom_call_target="tpu_custom_call" | custom-call | tf_op jit(solution)/shard_map/tiles/pallas_call | solution.py:392
  114.8 12.0 %all_to_all.25 = bf16[4,288,256]{2,1,0:T(8,128)(2,1)S(1)} all-to-all(bf16[4,288,256]{2,1,0:T(8,128)(2,1)S(1)} %bitcast.19), channel_id=1, replica_groups=mesh['ylo'=2,'x'=4,'z'=8,'core'=2,'chan'=4] {'ylo','core'}, dimensions={0} | all-to-all | bytes 1179648 | tf_op jit(solution)/shard_map/all_to_all | solution.py:416
  126.9 0.1 reshape.49
  127.0 18.6 %all_to_all.26 = bf16[32,18,128]{2,1,0:T(8,128)(2,1)S(1)} all-to-all(bf16[32,18,128]{2,1,0:T(8,128)(2,1)S(1)} %reshape.49), channel_id=1, replica_groups=mesh['ylo'=2,'x'=4,'z'=8,'core'=2,'chan'=4] {'x','z'}, dimensions={0} | all-to-all | bytes 294912 | tf_op jit(solution)/shard_map/all_to_all | solution.py:418
  145.7 0.7 broadcast_in_dim.2
  146.4 5.4 %all-to-all-start.4 = ((bf16[32,18,128]{2,1,0:T(8,128)(2,1)}), bf16[32,18,128]{2,1,0:T(8,128)(2,1)S(1)}, u32[]{:S(2)}, u32[]{:S(2)}) async-start(bf16[32,18,128]{2,1,0:T(8,128)(2,1)} %broadcast_in_dim.2), calls=%async_computation.4 | async-start | bytes 393216 | tf_op jit(solution)/shard_map/all_to_all | solution.py:420
  151.8 0.7 copy.28
  152.5 8.7 %all-to-all-done.4 = bf16[32,18,128]{2,1,0:T(8,128)(2,1)S(1)} async-done(((bf16[32,18,128]{2,1,0:T(8,128)(2,1)}), bf16[32,18,128]{2,1,0:T(8,128)(2,1)S(1)}, u32[]{:S(2)}, u32[]{:S(2)}) %all-to-all-start.4) | async-done | bytes 147488 | tf_op jit(solution)/shard_map/all_to_all | solution.py:420
  161.1 0.1 reshape.50
  161.2 9.5 %all_gather.27 = bf16[1152,256]{1,0:T(8,128)(2,1)S(1)} all-gather(bf16[288,256]{1,0:T(8,128)(2,1)S(1)} %reshape.50), channel_id=1, replica_groups=mesh['ylo'=2,'x'=4,'z'=8,'core'=2,'chan'=4] {'ylo','core'}, dimensions={0}, use_global_device_ids=true | all-gather | bytes 737280 | tf_op jit(solution)/shard_map/all_gather | solution.py:421
  170.8 1.1 slice_multiply_fusion
  (37 shorter events, 0.7 us)
Async XLA Ops:
  7.2 3.5 %copy-start.5 = (bf16[2,160,36]{2,1,0:T(8,128)(2,1)S(1)}, bf16[2,160,36]{2,1,0:T(8,128)(2,1)}, u32[]{:S(2)}) copy-start(bf16[2,160,36]{2,1,0:T(8,128)(2,1)} %constant.64.clone.selc_ref) | copy-start | bytes 69124
  7.2 3.5 %copy-start.3 = (bf16[2,160,144]{2,1,0:T(8,128)(2,1)S(1)}, bf16[2,160,144]{2,1,0:T(8,128)(2,1)}, u32[]{:S(2)}) copy-start(bf16[2,160,144]{2,1,0:T(8,128)(2,1)} %constant.63.clone.self_ref) | copy-start | bytes 276484
  7.2 3.5 %copy-start.4 = (bf16[3,64,144]{2,1,0:T(8,128)(2,1)S(1)}, bf16[3,64,144]{2,1,0:T(8,128)(2,1)}, u32[]{:S(2)}) copy-start(bf16[3,64,144]{2,1,0:T(8,128)(2,1)} %fields_ref.1) | copy-start | bytes 165892
  7.2 72.8 %all-gather.6.cloned.1.call-start = ((), (), s32[]{:S(2)}) async-start(), calls=%async_computation.5 | async-start | bytes 1474560 | tf_op jit(solution)/shard_map/all_gather | solution.py:345
  30.8 9.6 %copy-start.8 = (bf16[32,1728]{1,0:T(8,128)(2,1)S(1)}, bf16[32,1728]{1,0:T(8,128)(2,1)}, u32[]{:S(2)}) copy-start(bf16[32,1728]{1,0:T(8,128)(2,1)} %constant.67.clone) | copy-start | bytes 331780
  30.8 9.6 %copy-start.11 = (f32[1728]{0:T(1024)S(1)}, f32[1728]{0:T(1024)}, u32[]{:S(2)}) copy-start(f32[1728]{0:T(1024)} %constant.68.clone) | copy-start | bytes 20740
  30.8 39.4 %all-to-all-start = ((bf16[32,160,128]{2,1,0:T(8,128)(2,1)}), bf16[32,160,128]{2,1,0:T(8,128)(2,1)S(1)}, u32[]{:S(2)}, u32[]{:S(2)}) async-start(bf16[32,160,128]{2,1,0:T(8,128)(2,1)} %place.1), calls=%async_computation | async-start | bytes 2621440 | tf_op jit(solution)/shard_map/all_to_all | solution.py:371
  38.4 65.2 %all-gather.8.cloned.1.call-start = ((), (), s32[]{:S(2)}) async-start(), calls=%async_computation.6 | async-start | bytes 1474560 | tf_op jit(solution)/shard_map/all_gather | solution.py:346
  70.2 7.8 %copy-start.9 = (bf16[32,1584]{1,0:T(8,128)(2,1)S(1)}, bf16[32,1584]{1,0:T(8,128)(2,1)}, u32[]{:S(2)}) copy-start(bf16[32,1584]{1,0:T(8,128)(2,1)} %constant.65.clone) | copy-start | bytes 304132
  70.2 7.8 %copy-start.10 = (f32[1584]{0:T(1024)S(1)}, f32[1584]{0:T(1024)}, u32[]{:S(2)}) copy-start(f32[1584]{0:T(1024)} %constant.66.clone) | copy-start | bytes 19012
  71.1 32.5 %all-to-all-start.1 = ((bf16[4,432,128]{2,1,0:T(8,128)(2,1)}), bf16[4,432,128]{2,1,0:T(8,128)(2,1)S(1)}, u32[]{:S(2)}, u32[]{:S(2)}) async-start(bf16[4,432,128]{2,1,0:T(8,128)(2,1)} %join.1), calls=%async_computation.1 | async-start | bytes 884736 | tf_op jit(solution)/shard_map/all_to_all | solution.py:381
  77.9 25.7 %copy-start.2 = (bf16[432,176]{1,0:T(8,128)(2,1)S(1)}, bf16[432,176]{1,0:T(8,128)(2,1)}, u32[]{:S(2)}) copy-start(bf16[432,176]{1,0:T(8,128)(2,1)} %constant.69.clone.down_ref) | copy-start | bytes 456196
  78.0 25.7 %copy-start.6 = (bf16[144,48]{1,0:T(8,128)(2,1)S(1)}, bf16[144,48]{1,0:T(8,128)(2,1)}, u32[]{:S(2)}) copy-start(bf16[144,48]{1,0:T(8,128)(2,1)} %constant.70.clone.rim_ref) | copy-start | bytes 41476
  78.0 25.7 %copy-start.7 = (bf16[48,64]{1,0:T(8,128)(2,1)S(1)}, bf16[48,64]{1,0:T(8,128)(2,1)}, u32[]{:S(2)}) copy-start(bf16[48,64]{1,0:T(8,128)(2,1)} %constant.71.clone.order_ref) | copy-start | bytes 18436
  103.6 1.3 copy-start
  104.9 1.3 copy-start.1
  146.4 14.8 %all-to-all-start.4 = ((bf16[32,18,128]{2,1,0:T(8,128)(2,1)}), bf16[32,18,128]{2,1,0:T(8,128)(2,1)S(1)}, u32[]{:S(2)}, u32[]{:S(2)}) async-start(bf16[32,18,128]{2,1,0:T(8,128)(2,1)} %broadcast_in_dim.2), calls=%async_computation.4 | async-start | bytes 393216 | tf_op jit(solution)/shard_map/all_to_all | solution.py:420
Sparse Core Ops, SparseCore 0:
  10.1 44.8 all-gather.5
  57.1 46.4 all-gather.7

commit v2 on v1

--- a/solution.py
+++ b/solution.py
@@ -14,8 +14,9 @@
 CH = 64
 C = 256
 YLO, NX, NZ, CORE, CHAN = 2, 4, 8, 2, 4
-PLANE = NX * NZ
-QUAD = YLO * CORE
+YX = YLO * NX
+NEAR = YX * CORE
+PLANE = YX * NZ
 TILE_AXES = ("ylo", "x", "z", "core")
 BF = jnp.bfloat16
 F32 = jnp.float32
@@ -188,53 +189,57 @@
         ]
         for h in range(2):
             own_ref[t, :, h * CH : (h + 1) * CH] = halves[h][:PACK_ROWS]
-            unit_ref[t * 4 * UNIT : (t + 1) * 4 * UNIT, h * CH : (h + 1) * CH] = halves[h][PACK_ROWS:]
-
-
-def edge_row(edge):
-    return jnp.where(edge < 2, edge * 28, 14 + (edge - 2) * 20)
-
-
-def place_kernel(table_ref, me_ref, unit_ref, out_ref, source, sent):
+            for copy in range(YX):
+                unit_ref[copy, t * 4 * UNIT : (t + 1) * 4 * UNIT, h * CH : (h + 1) * CH] = halves[h][PACK_ROWS:]
+
+
+def edge_words(seam_table):
+    n, f, r = seam_table[:, :, 0], seam_table[:, :, 1], seam_table[:, :, 2]
+    device = n // TILES_HERE
+    group = (device % CORE) * YX + device // (NZ * CORE)
+    unit = (group * TILES_HERE + n % TILES_HERE) * 4 + f
+    z = (device // CORE) % NZ
+    word = unit + r * 256 + z * 512
+    beyond = (n * 4 + jnp.where(f < 2, 2, 0)) * 2 + f % 2
+    return word.reshape(-1), beyond.reshape(-1)
+
+
+def place_kernel(word_ref, beyond_ref, me_ref, unit_ref, out_ref, sent):
     ylo, x, z, core = me_ref[0], me_ref[1], me_ref[2], me_ref[3]
-    for s in range(QUAD):
-        source[s * 192 : (s + 1) * 192, :] = unit_ref[s].astype(F32)
-    sent[...] = jnp.zeros_like(sent)
-
-    def target(tile, wanted):
-        device = tile // TILES_HERE
-        slot = tile - device * TILES_HERE
-        mine = jnp.logical_and(device % CORE == core, device // (CORE * PLANE) == ylo)
-        place = jnp.where(jnp.logical_and(mine, wanted), (device // CORE) % PLANE, PLANE)
-        return place, slot * BLOCK_ROWS
-
-    def body(i, carry):
-        s = i // 12
-        device = (((s // CORE) * NX + x) * NZ + z) * CORE + s % CORE
-        at = (device * TILES_HERE * 4 + i % 12) * 3
-        n, p, r = table_ref[at], table_ref[at + 1], table_ref[at + 2]
-        base = pl.multiple_of(i * UNIT, UNIT)
-        place, rows = target(n, True)
-        sent[place, pl.ds(rows + edge_row(p), 6), :] = source[pl.ds(base, 6), :]
-        sent[place, pl.ds(rows + FIELD_ROWS + 3 * p, 3), :] = source[pl.ds(base + 6, 3), :]
-        deep = jnp.where(p % 2 == 0, place, PLANE)
-        sent[deep, pl.ds(rows + edge_row(p) + 6, 6), :] = source[pl.ds(base + 9, 6), :]
-        for last in range(2):
-            f = jnp.where(p >= 2, 0, 2) + last
-            beyond = (n * 4 + f) * 3
-            t2, e2 = table_ref[beyond], table_ref[beyond + 1]
-            place2, rows2 = target(t2, e2 % 2 == 0)
-            end = base + jnp.where(r == last, 0, 15)
-            sent[place2, pl.ds(rows2 + edge_row(e2) + 12 + p % 2, 1), :] = source[pl.ds(end, 1), :]
+
+    def unit_at(word):
+        keep = jnp.where(word // 512 == z, 1.0, 0.0).astype(F32)
+        at = pl.multiple_of((word % 256) * UNIT, UNIT)
+        return unit_ref[pl.ds(at, UNIT), :].astype(F32) * keep
+
+    def body(z_to, carry):
+        device = ((ylo * NX + x) * NZ + z_to) * CORE + core
+        for t in range(TILES_HERE):
+            for edge in range(4):
+                at = (device * TILES_HERE + t) * 4 + edge
+                unit = unit_at(word_ref[at])
+                row = t * BLOCK_ROWS + EDGE_ROWS[edge]
+                cot = t * BLOCK_ROWS + FIELD_ROWS + 3 * edge
+                sent[z_to, row : row + 6, :] = unit[0:6]
+                sent[z_to, cot : cot + 3, :] = unit[6:9]
+                if edge % 2 == 0:
+                    sent[z_to, row + 6 : row + 12, :] = unit[9:15]
+                    beyond = beyond_ref[at]
+                    for last in range(2):
+                        word = word_ref[beyond // 2 + last]
+                        end = unit_at(word)
+                        low = (beyond + word // 256) % 2 == 0
+                        sent[z_to, row + 12 + last : row + 13 + last, :] = jnp.where(low, end[0:1], end[15:16])
+        sent[z_to, TILES_HERE * BLOCK_ROWS :, :] = jnp.zeros((SEND_ROWS - TILES_HERE * BLOCK_ROWS, 128), F32)
         return carry
 
-    lax.fori_loop(0, QUAD * 12, body, 0)
-    out_ref[...] = sent[:PLANE].astype(BF)
+    lax.fori_loop(0, NZ, body, 0)
+    out_ref[...] = sent[...].astype(BF)
 
 
 def join_kernel(got_ref, own_ref, out_ref, rows):
     total = got_ref[0].astype(F32)
-    for q in range(1, PLANE):
+    for q in range(1, NZ):
         total = total + got_ref[q].astype(F32)
     for t in range(TILES_HERE):
         base, block = t * PAY_ROWS, t * BLOCK_ROWS
@@ -250,7 +255,7 @@
 
 
 def main_kernel(
-    me_ref, pay_ref, window_ref, lift_ref, down_ref, rim_ref, order_ref, wf_ref, wd_ref,
+    me_ref, pay_ref, window_ref, lift_ref, down_ref, rim_ref, order_ref, weights_ref,
     coarse_ref, gp_ref, grads_ref, xs, cs, wf, wd, wins, lifts,
 ):
     chan = me_ref[4]
@@ -259,8 +264,8 @@
     ).astype(BF)
     for c in range(CHAN):
         for k in range(9):
-            wf[k, c * CH : (c + 1) * CH, :] = wf_ref[c, k]
-            wd[k, c * CH : (c + 1) * CH, :] = wd_ref[c, k]
+            wf[k, c * CH : (c + 1) * CH, :] = weights_ref[2 * c, k]
+            wd[k, c * CH : (c + 1) * CH, :] = weights_ref[2 * c + 1, k]
         for t in range(TILES_HERE):
             base = t * PAY_ROWS
             for h in range(2):
@@ -324,8 +329,9 @@
         first_sum = first if first_sum is None else first_sum + first
         part = dot_nn(jnp.concatenate(down_parts, axis=0), up)
         down_sum = part if down_sum is None else down_sum + part
-    grads_ref[: 9 * CH, :] = first_sum.astype(BF)
-    grads_ref[9 * CH :, :] = down_sum.astype(BF)
+    for h in range(CORE):
+        grads_ref[h, : 9 * CH, :] = first_sum[:, h * 128 : (h + 1) * 128].astype(BF)
+        grads_ref[h, 9 * CH :, :] = down_sum[:, h * 128 : (h + 1) * 128].astype(BF)
 
 
 def vmem(count):
@@ -342,33 +348,34 @@
 def shards(fields, seam_table, w_first, w_down, cotangent):
     coords = [lax.axis_index(axis) for axis in ("ylo", "x", "z", "core", "chan")]
     me = jnp.stack(coords).astype(jnp.int32)
-    all_first = lax.all_gather(w_first, "chan", axis=0, tiled=False)
-    all_down = lax.all_gather(w_down, "chan", axis=0, tiled=False)
+    half = jnp.where(coords[3] == 0, w_first, w_down)
+    weights = lax.all_gather(half, ("chan", "core"), axis=0, tiled=False)
 
     sel_fields, sel_coarse = pack_selectors()
     own, units = pl.pallas_call(
         pack_kernel,
         out_shape=(
             jax.ShapeDtypeStruct((TILES_HERE, PACK_ROWS, 128), BF),
-            jax.ShapeDtypeStruct((TILES_HERE * 4 * UNIT, 128), BF),
+            jax.ShapeDtypeStruct((YX, TILES_HERE * 4 * UNIT, 128), BF),
         ),
         in_specs=vmem(4),
         out_specs=tuple(vmem(2)),
         compiler_params=LIMIT,
         name="pack",
     )(fields, cotangent, jnp.asarray(sel_fields, BF), jnp.asarray(sel_coarse, BF))
-    quad = lax.all_gather(units, ("ylo", "core"), axis=0, tiled=False)
-    table = seam_table.reshape(-1)
+    units = lax.all_to_all(units, ("ylo", "x"), 0, 0).reshape(-1, 128)
+    units = lax.all_gather(units, "core", axis=0, tiled=True)
+    words, beyond = edge_words(seam_table)
     sends = pl.pallas_call(
         place_kernel,
-        out_shape=jax.ShapeDtypeStruct((PLANE, SEND_ROWS, 128), BF),
-        in_specs=smem(2) + vmem(1),
+        out_shape=jax.ShapeDtypeStruct((NZ, SEND_ROWS, 128), BF),
+        in_specs=smem(3) + vmem(1),
         out_specs=vmem(1)[0],
-        scratch_shapes=[pltpu.VMEM((QUAD * 192, 128), F32), pltpu.VMEM((PLANE + 1, SEND_ROWS, 128), F32)],
+        scratch_shapes=[pltpu.VMEM((NZ, SEND_ROWS, 128), F32)],
         compiler_params=LIMIT,
         name="place",
-    )(table, me, quad)
-    got = lax.all_to_all(sends, ("x", "z"), 0, 0)
+    )(words, beyond, me, units)
+    got = lax.all_to_all(sends, "z", 0, 0)
     joined = pl.pallas_call(
         join_kernel,
         out_shape=jax.ShapeDtypeStruct((CHAN, TILES_HERE * PAY_ROWS, 128), BF),
@@ -394,9 +401,9 @@
         out_shape=(
             jax.ShapeDtypeStruct((TILES_HERE, CH, COARSE), BF),
             jax.ShapeDtypeStruct((TILES_HERE, CH, CELLS), BF),
-            jax.ShapeDtypeStruct((18 * CH, C), BF),
+            jax.ShapeDtypeStruct((CORE, 18 * CH, 128), BF),
         ),
-        in_specs=smem(1) + vmem(8),
+        in_specs=smem(1) + vmem(7),
         out_specs=tuple(vmem(3)),
         scratch_shapes=[
             pltpu.VMEM((TILES_HERE, C, C), BF),
@@ -410,17 +417,17 @@
         name="tiles",
     )(
         me, payload, one_hots[0], one_hots[1], jnp.asarray(down_selector(), BF), jnp.asarray(rim_selector(), BF),
-        jnp.asarray(order_selector(), BF), all_first, all_down,
+        jnp.asarray(order_selector(), BF), weights,
     )
 
-    part = lax.all_to_all(grads.reshape(QUAD, 18 * CH // QUAD, C), ("ylo", "core"), 0, 0)
-    part = part.astype(F32).sum(0).astype(BF).reshape(PLANE, 18, 128)
-    part = lax.all_to_all(part, ("x", "z"), 0, 0)
+    part = lax.all_to_all(grads, "core", 0, 0)
+    part = (part[0].astype(F32) + part[1].astype(F32)).astype(BF).reshape(PLANE, 18, 128)
+    part = lax.all_to_all(part, ("ylo", "x", "z"), 0, 0)
     part = part.astype(F32).sum(0).astype(BF)
-    part = lax.all_to_all(jnp.broadcast_to(part[None], (PLANE, 18, 128)), ("x", "z"), 0, 0)
-    whole = lax.all_gather(part.reshape(18 * CH // QUAD, C), ("ylo", "core"), axis=0, tiled=True)
-    whole = whole.astype(F32).reshape(2, 9, CH, C)
-    tiles = TILES_HERE * PLANE * QUAD
+    part = lax.all_to_all(jnp.broadcast_to(part[None], (PLANE, 18, 128)), ("ylo", "x", "z"), 0, 0)
+    whole = lax.all_gather(part.reshape(18 * CH, 128), "core", axis=0, tiled=False)
+    whole = jnp.concatenate([whole[0], whole[1]], axis=1).astype(F32).reshape(2, 9, CH, C)
+    tiles = TILES_HERE * PLANE * CORE
     return (
         coarse,
         whole[0] * float(tiles * CELLS) ** (-0.5),

time: 179 us -> 146 us (0.82)
  waiting for transfers between devices: 62.5 us -> 41 us
  blocking collectives: 52.5 us -> 37.3 us
  starting transfers between devices: 19.9 us -> 25.3 us
  Pallas kernels: 17.3 us -> 14.5 us
    all_gather x2 -> x1, waiting for transfers between devices: 23.6 us -> 0.01 us  [shards(): weights = lax.all_gather(half, ('chan', 'core'), axis=0, tiled=False)]
    all_to_all x1, waiting for transfers between devices: 0.01 us -> 10.2 us  [shards(): payload = lax.all_to_all(joined, 'chan', 0, 0)]
    all_gather x2, blocking collectives: 21.8 us -> 11.9 us  [the longest x1 7.54 us: shards(): units = lax.all_gather(units, 'core', axis=0, tiled=True)]
    all_to_all x2 -> x3, waiting for transfers between devices: 37.5 us -> 30.8 us  [the longest x1 14 us: shards(): lax.all_to_all(jnp.broadcast_to(part[None], (PLANE, 18, 128)), ('ylo', 'x...]
    all_to_all x2 -> x3, starting transfers between devices: 13 us -> 19.3 us  [the longest x1 7.53 us: shards(): got = lax.all_to_all(sends, 'z', 0, 0)]
    all_to_all x2, blocking collectives: 30.7 us -> 25.4 us  [the longest x1 19 us: shards(): part = lax.all_to_all(part, ('ylo', 'x', 'z'), 0, 0)]
    pallas_call x1, Pallas kernels: 7.31 us -> 3.95 us  [shards(): pl.pallas_call(place_kernel, out_shape=jax.ShapeDtypeStruct((NZ, SEND_ROW...]
    unnamed x27 -> x26, local copies, waits for them, and re-layouts: 5.22 us -> 3.31 us
  transfers between devices with their start and end apart: 5 -> 5, of which waited for: 3 -> 4; matrix products, arithmetic and copies ran while one was open for 4% -> 5% of each run, Pallas kernels for 5% -> 4%
where the time goes in v2:
time: 146 us; the launch traced here: 145 us
  waiting for transfers between devices  41 us (28%)
  blocking collectives  37.3 us (26%)
  starting transfers between devices  25.3 us (17%)
  Pallas kernels  14.5 us (10%)
  between operations  14.4 us (10%)
  local copies, waits for them, and re-layouts  6.51 us (4%)
  other arithmetic  6.07 us (4%)
    all_to_all x1, blocking collectives, shards(): part = lax.all_to_all(part, ('ylo', 'x', 'z'), 0, 0)  19 us
    all_to_all x1, waiting for transfers between devices, shards(): lax.all_to_all(jnp.broadcast_to(part[None], (PLANE, 18, 128)), ('ylo', 'x...  14 us
    all_to_all x1, waiting for transfers between devices, shards(): got = lax.all_to_all(sends, 'z', 0, 0)  12.8 us
    all_to_all x1, waiting for transfers between devices, shards(): payload = lax.all_to_all(joined, 'chan', 0, 0)  10.2 us
    pallas_call x1, Pallas kernels, shards(): pl.pallas_call(main_kernel, out_shape=(jax.ShapeDtypeStruct((TILES_HERE,...  8.59 us
    all_gather x1, blocking collectives, shards(): units = lax.all_gather(units, 'core', axis=0, tiled=True)  7.54 us
    all_to_all x1, starting transfers between devices, shards(): got = lax.all_to_all(sends, 'z', 0, 0)  7.53 us
    all_to_all x1, blocking collectives, shards(): part = lax.all_to_all(grads, 'core', 0, 0)  6.43 us
  transfers between devices with their start and end apart: 5, of which 4 were waited for; matrix products, arithmetic and copies ran while one was open for 5% of the time, Pallas kernels for 4%

profile of v2, /device:TPU:1, one launch (start us, length us, event | category | flops | bytes accessed | tf_op | source)
XLA Modules:
  0.0 145.3 jit_solution(3262883290291298180)
XLA Ops:
  7.3 1.8 %broadcast_select_fusion = bf16[9,64,256]{2,1,0:T(8,128)(2,1)} fusion(bf16[9,64,256]{2,1,0:T(8,128)(2,1)} %param.16, bf16[9,64,256]{2,1,0:T(8,128)(2,1)} %param.17, pred[]{:T(512)S(6)} %eq.69), kind=kLoop, calls=%fused_computation.10 | loop fusion | flops 147456 | bytes 884737 | tf_op jit(solution)/shard_map/jit(_where)/select_n | solution.py:351
  9.1 0.9 copy.36.cot_ref
  10.0 1.2 pack.1
  11.1 5.9 %all-to-all-start = ((bf16[8,192,128]{2,1,0:T(8,128)(2,1)}), bf16[8,192,128]{2,1,0:T(8,128)(2,1)S(1)}, u32[]{:S(2)}, u32[]{:S(2)}) async-start(bf16[8,192,128]{2,1,0:T(8,128)(2,1)} %get-tuple-element.9), calls=%async_computation | async-start | bytes 786432 | tf_op jit(solution)/shard_map/all_to_all | solution.py:366
  17.5 0.2 copy.30
  17.7 0.2 ne.70
  17.9 0.1 copy.35
  18.0 0.1 mul.88
  18.3 0.1 div.31
  18.6 0.1 rem.82
  18.9 0.1 squeeze.6
  19.2 0.1 mul.84
  19.6 4.0 %all-to-all-done = bf16[8,192,128]{2,1,0:T(8,128)(2,1)S(1)} async-done(((bf16[8,192,128]{2,1,0:T(8,128)(2,1)}), bf16[8,192,128]{2,1,0:T(8,128)(2,1)S(1)}, u32[]{:S(2)}, u32[]{:S(2)}) %all-to-all-start) | async-done | bytes 393248 | tf_op jit(solution)/shard_map/all_to_all | solution.py:366
  23.6 7.5 %all_gather.12.unit_ref = bf16[3072,128]{1,0:T(8,128)(2,1)S(1)} all-gather(bf16[1536,128]{1,0:T(8,128)(2,1)S(1)} %bitcast.31), channel_id=1, replica_groups=mesh['ylo'=2,'x'=4,'z'=8,'core'=2,'chan'=4] {'core'}, dimensions={0}, use_global_device_ids=true | all-gather | bytes 1179648 | tf_op jit(solution)/shard_map/all_gather | solution.py:367
  31.1 3.9 %place.1 = bf16[8,160,128]{2,1,0:T(8,128)(2,1)} custom-call(s32[1536]{0:T(1024)S(1)} %get-tuple-element.36.word_ref, s32[1536]{0:T(1024)S(1)} %get-tuple-element.35.beyond_ref, s32[5]{0:T(128)S(1)} %stack.23.me_ref, bf16[3072,128]{1,0:T(8,128)(2,1)S(1)} %all_gather.12.unit_ref), custom_call_target="tpu_custom_call" | custom-call | tf_op jit(solution)/shard_map/place/pallas_call | solution.py:369
  35.1 7.5 %all-to-all-start.1 = ((bf16[8,160,128]{2,1,0:T(8,128)(2,1)}), bf16[8,160,128]{2,1,0:T(8,128)(2,1)S(1)}, u32[]{:S(2)}, u32[]{:S(2)}) async-start(bf16[8,160,128]{2,1,0:T(8,128)(2,1)} %place.1), calls=%async_computation.1 | async-start | bytes 655360 | tf_op jit(solution)/shard_map/all_to_all | solution.py:378
  42.7 0.9 compare_convert_fusion.1.lift_ref
  43.5 12.8 %all-to-all-done.1.got_ref = bf16[8,160,128]{2,1,0:T(8,128)(2,1)S(1)} async-done(((bf16[8,160,128]{2,1,0:T(8,128)(2,1)}), bf16[8,160,128]{2,1,0:T(8,128)(2,1)S(1)}, u32[]{:S(2)}, u32[]{:S(2)}) %all-to-all-start.1) | async-done | bytes 327712 | tf_op jit(solution)/shard_map/all_to_all | solution.py:378
  56.4 0.8 join.1
  57.2 5.9 %all-to-all-start.2 = ((bf16[4,432,128]{2,1,0:T(8,128)(2,1)}), bf16[4,432,128]{2,1,0:T(8,128)(2,1)S(1)}, u32[]{:S(2)}, u32[]{:S(2)}) async-start(bf16[4,432,128]{2,1,0:T(8,128)(2,1)} %join.1), calls=%async_computation.2 | async-start | bytes 884736 | tf_op jit(solution)/shard_map/all_to_all | solution.py:388
  63.3 1.9 %compare_convert_fusion.window_ref = bf16[3,1584,256]{2,1,0:T(8,128)(2,1)} fusion(f32[256]{0:T(256)S(1)} %add_convert_fusion.1, f32[3,1584]{1,0:T(4,128)S(1)} %convolution_add_fusion), kind=kLoop, calls=%fused_computation | loop fusion | flops 2433024 | bytes 2453056 | tf_op jit(solution)/shard_map/convert_element_type | solution.py:397
  65.2 10.2 %all-to-all-done.2.pay_ref = bf16[4,432,128]{2,1,0:T(8,128)(2,1)S(1)} async-done(((bf16[4,432,128]{2,1,0:T(8,128)(2,1)}), bf16[4,432,128]{2,1,0:T(8,128)(2,1)S(1)}, u32[]{:S(2)}, u32[]{:S(2)}) %all-to-all-start.2) | async-done | bytes 442400 | tf_op jit(solution)/shard_map/all_to_all | solution.py:388
  75.3 1.7 %copy-done = bf16[72,64,256]{2,1,0:T(8,128)(2,1)S(1)} copy-done((bf16[72,64,256]{2,1,0:T(8,128)(2,1)S(1)}, bf16[72,64,256]{2,1,0:T(8,128)(2,1)}, u32[]{:S(2)}) %copy-start) | copy-done | bytes 2359320
  77.0 8.6 %tiles.1 = (bf16[3,64,36]{2,1,0:T(8,128)(2,1)S(1)}, bf16[3,64,144]{2,1,0:T(8,128)(2,1)}, bf16[2,1152,128]{2,1,0:T(8,128)(2,1)S(1)}) custom-call(s32[5]{0:T(128)S(1)} %stack.23.me_ref, bf16[4,432,128]{2,1,0:T(8,128)(2,1)S(1)} %all-to-all-done.2.pay_ref, bf16[3,1584,256]{2,1,0:T(8,128)(2,1)} %compare_convert_fusion.window_ref, ...), custom_call_target="tpu_custom_call" | custom-call | tf_op jit(solution)/shard_map/tiles/pallas_call | solution.py:399
  85.6 6.4 %all_to_all.30 = bf16[2,1152,128]{2,1,0:T(8,128)(2,1)S(1)} all-to-all(bf16[2,1152,128]{2,1,0:T(8,128)(2,1)S(1)} %get-tuple-element.12), channel_id=1, replica_groups=mesh['ylo'=2,'x'=4,'z'=8,'core'=2,'chan'=4] {'core'}, dimensions={0} | all-to-all | bytes 1179648 | tf_op jit(solution)/shard_map/all_to_all | solution.py:423
  92.2 19.0 %all_to_all.31 = bf16[64,18,128]{2,1,0:T(8,128)(2,1)S(1)} all-to-all(bf16[64,18,128]{2,1,0:T(8,128)(2,1)S(1)} %convert_element_type.50), channel_id=1, replica_groups=mesh['ylo'=2,'x'=4,'z'=8,'core'=2,'chan'=4] {'ylo','x','z'}, dimensions={0} | all-to-all | bytes 589824 | tf_op jit(solution)/shard_map/all_to_all | solution.py:425
  111.3 0.8 broadcast_in_dim.6
  112.1 5.9 %all-to-all-start.5 = ((bf16[64,18,128]{2,1,0:T(8,128)(2,1)}), bf16[64,18,128]{2,1,0:T(8,128)(2,1)S(1)}, u32[]{:S(2)}, u32[]{:S(2)}) async-start(bf16[64,18,128]{2,1,0:T(8,128)(2,1)} %broadcast_in_dim.6), calls=%async_computation.5 | async-start | bytes 786432 | tf_op jit(solution)/shard_map/all_to_all | solution.py:427
  118.0 0.7 copy.38
  118.8 14.0 %all-to-all-done.5 = bf16[64,18,128]{2,1,0:T(8,128)(2,1)S(1)} async-done(((bf16[64,18,128]{2,1,0:T(8,128)(2,1)}), bf16[64,18,128]{2,1,0:T(8,128)(2,1)S(1)}, u32[]{:S(2)}, u32[]{:S(2)}) %all-to-all-start.5) | async-done | bytes 294944 | tf_op jit(solution)/shard_map/all_to_all | solution.py:427
  132.9 4.3 %all_gather.15 = bf16[2,1152,128]{2,1,0:T(8,128)(2,1)S(1)} all-gather(bf16[1,1152,128]{2,1,0:T(8,128)(2,1)S(1)} %all_gather_reshape.3), channel_id=1, replica_groups=mesh['ylo'=2,'x'=4,'z'=8,'core'=2,'chan'=4] {'core'}, dimensions={0}, use_global_device_ids=true | all-gather | bytes 884736 | tf_op jit(solution)/shard_map/all_gather | solution.py:428
  137.3 1.1 slice_multiply_fusion
  (51 shorter events, 2.0 us)
Async XLA Ops:
  7.2 2.8 %copy-start.4 = (bf16[2,160,36]{2,1,0:T(8,128)(2,1)S(1)}, bf16[2,160,36]{2,1,0:T(8,128)(2,1)}, u32[]{:S(2)}) copy-start(bf16[2,160,36]{2,1,0:T(8,128)(2,1)} %constant.127.clone.selc_ref) | copy-start | bytes 69124
  7.2 2.8 %copy-start.2 = (bf16[2,160,144]{2,1,0:T(8,128)(2,1)S(1)}, bf16[2,160,144]{2,1,0:T(8,128)(2,1)}, u32[]{:S(2)}) copy-start(bf16[2,160,144]{2,1,0:T(8,128)(2,1)} %constant.126.clone.self_ref) | copy-start | bytes 276484
  7.2 2.8 %copy-start.3 = (bf16[3,64,144]{2,1,0:T(8,128)(2,1)S(1)}, bf16[3,64,144]{2,1,0:T(8,128)(2,1)}, u32[]{:S(2)}) copy-start(bf16[3,64,144]{2,1,0:T(8,128)(2,1)} %fields_ref.1) | copy-start | bytes 165892
  7.2 9.8 %copy-start.9 = (s32[384,4,3]{0,1,2:T(4,128)S(1)}, s32[384,4,3]{0,1,2:T(4,128)}, u32[]{:S(2)}) copy-start(s32[384,4,3]{0,1,2:T(4,128)} %param.15) | copy-start | bytes 55300
  7.2 68.1 %all-gather.3.cloned.1.call-start = ((), (), s32[]{:S(2)}) async-start(), calls=%async_computation.6 | async-start | bytes 2654208 | tf_op jit(solution)/shard_map/all_gather | solution.py:352
  11.1 12.5 %all-to-all-start = ((bf16[8,192,128]{2,1,0:T(8,128)(2,1)}), bf16[8,192,128]{2,1,0:T(8,128)(2,1)S(1)}, u32[]{:S(2)}, u32[]{:S(2)}) async-start(bf16[8,192,128]{2,1,0:T(8,128)(2,1)} %get-tuple-element.9), calls=%async_computation | async-start | bytes 786432 | tf_op jit(solution)/shard_map/all_to_all | solution.py:366
  17.0 2.4 %copy-start.7 = (bf16[32,1728]{1,0:T(8,128)(2,1)S(1)}, bf16[32,1728]{1,0:T(8,128)(2,1)}, u32[]{:S(2)}) copy-start(bf16[32,1728]{1,0:T(8,128)(2,1)} %constant.130.clone) | copy-start | bytes 331780
  17.0 2.5 %copy-start.11 = (f32[1728]{0:T(1024)S(1)}, f32[1728]{0:T(1024)}, u32[]{:S(2)}) copy-start(f32[1728]{0:T(1024)} %constant.131.clone) | copy-start | bytes 20740
  35.1 21.3 %all-to-all-start.1 = ((bf16[8,160,128]{2,1,0:T(8,128)(2,1)}), bf16[8,160,128]{2,1,0:T(8,128)(2,1)S(1)}, u32[]{:S(2)}, u32[]{:S(2)}) async-start(bf16[8,160,128]{2,1,0:T(8,128)(2,1)} %place.1), calls=%async_computation.1 | async-start | bytes 655360 | tf_op jit(solution)/shard_map/all_to_all | solution.py:378
  42.6 20.5 %copy-start.8 = (bf16[32,1584]{1,0:T(8,128)(2,1)S(1)}, bf16[32,1584]{1,0:T(8,128)(2,1)}, u32[]{:S(2)}) copy-start(bf16[32,1584]{1,0:T(8,128)(2,1)} %constant.128.clone) | copy-start | bytes 304132
  42.6 20.5 %copy-start.10 = (f32[1584]{0:T(1024)S(1)}, f32[1584]{0:T(1024)}, u32[]{:S(2)}) copy-start(f32[1584]{0:T(1024)} %constant.129.clone) | copy-start | bytes 19012
  57.2 18.2 %all-to-all-start.2 = ((bf16[4,432,128]{2,1,0:T(8,128)(2,1)}), bf16[4,432,128]{2,1,0:T(8,128)(2,1)S(1)}, u32[]{:S(2)}, u32[]{:S(2)}) async-start(bf16[4,432,128]{2,1,0:T(8,128)(2,1)} %join.1), calls=%async_computation.2 | async-start | bytes 884736 | tf_op jit(solution)/shard_map/all_to_all | solution.py:388
  63.1 12.2 %copy-start.1 = (bf16[432,176]{1,0:T(8,128)(2,1)S(1)}, bf16[432,176]{1,0:T(8,128)(2,1)}, u32[]{:S(2)}) copy-start(bf16[432,176]{1,0:T(8,128)(2,1)} %constant.132.clone.down_ref) | copy-start | bytes 456196
  63.1 12.2 %copy-start.5 = (bf16[144,48]{1,0:T(8,128)(2,1)S(1)}, bf16[144,48]{1,0:T(8,128)(2,1)}, u32[]{:S(2)}) copy-start(bf16[144,48]{1,0:T(8,128)(2,1)} %constant.133.clone.rim_ref) | copy-start | bytes 41476
  63.1 12.2 %copy-start.6 = (bf16[48,64]{1,0:T(8,128)(2,1)S(1)}, bf16[48,64]{1,0:T(8,128)(2,1)}, u32[]{:S(2)}) copy-start(bf16[48,64]{1,0:T(8,128)(2,1)} %constant.134.clone.order_ref) | copy-start | bytes 18436
  75.3 1.7 %copy-start = (bf16[72,64,256]{2,1,0:T(8,128)(2,1)S(1)}, bf16[72,64,256]{2,1,0:T(8,128)(2,1)}, u32[]{:S(2)}) copy-start(bf16[72,64,256]{2,1,0:T(8,128)(2,1)} %all-gather.3.cloned.1.call-done) | copy-start | bytes 7077892
  112.1 20.7 %all-to-all-start.5 = ((bf16[64,18,128]{2,1,0:T(8,128)(2,1)}), bf16[64,18,128]{2,1,0:T(8,128)(2,1)S(1)}, u32[]{:S(2)}, u32[]{:S(2)}) async-start(bf16[64,18,128]{2,1,0:T(8,128)(2,1)} %broadcast_in_dim.6), calls=%async_computation.5 | async-start | bytes 786432 | tf_op jit(solution)/shard_map/all_to_all | solution.py:427
Sparse Core Ops, SparseCore 0:
  10.7 46.5 all-gather.2

commit v3 on v2

--- a/solution.py
+++ b/solution.py
@@ -181,16 +181,25 @@
     return lax.dot_general(left, right, (((1,), (1,)), ((), ())), preferred_element_type=F32)
 
 
-def pack_kernel(fields_ref, cot_ref, self_ref, selc_ref, own_ref, unit_ref):
+def pack_kernel(me_ref, fields_ref, cot_ref, self_ref, selc_ref, first_ref, down_ref, own_ref, unit_ref, half_ref, sem):
+    @pl.when(me_ref[3] == 0)
+    def _():
+        pltpu.make_async_copy(first_ref, half_ref, sem).start()
+
+    @pl.when(me_ref[3] == 1)
+    def _():
+        pltpu.make_async_copy(down_ref, half_ref, sem).start()
+
     for t in range(TILES_HERE):
         halves = [
-            (dot_nt(self_ref[h], fields_ref[t]) + dot_nt(selc_ref[h], cot_ref[t])).astype(BF)
+            (dot_nt(self_ref[h], fields_ref[t]) + dot_nn(selc_ref[h], cot_ref[t])).astype(BF)
             for h in range(2)
         ]
         for h in range(2):
             own_ref[t, :, h * CH : (h + 1) * CH] = halves[h][:PACK_ROWS]
             for copy in range(YX):
                 unit_ref[copy, t * 4 * UNIT : (t + 1) * 4 * UNIT, h * CH : (h + 1) * CH] = halves[h][PACK_ROWS:]
+    pltpu.make_async_copy(first_ref, half_ref, sem).wait()
 
 
 def edge_words(seam_table):
@@ -208,8 +217,8 @@
     ylo, x, z, core = me_ref[0], me_ref[1], me_ref[2], me_ref[3]
 
     def unit_at(word):
-        keep = jnp.where(word // 512 == z, 1.0, 0.0).astype(F32)
-        at = pl.multiple_of((word % 256) * UNIT, UNIT)
+        keep = jnp.where((word >> 9) == z, 1.0, 0.0).astype(F32)
+        at = pl.multiple_of((word & 255) * UNIT, UNIT)
         return unit_ref[pl.ds(at, UNIT), :].astype(F32) * keep
 
     def body(z_to, carry):
@@ -226,9 +235,9 @@
                     sent[z_to, row + 6 : row + 12, :] = unit[9:15]
                     beyond = beyond_ref[at]
                     for last in range(2):
-                        word = word_ref[beyond // 2 + last]
+                        word = word_ref[(beyond >> 1) + last]
                         end = unit_at(word)
-                        low = (beyond + word // 256) % 2 == 0
+                        low = ((beyond + (word >> 8)) & 1) == 0
                         sent[z_to, row + 12 + last : row + 13 + last, :] = jnp.where(low, end[0:1], end[15:16])
         sent[z_to, TILES_HERE * BLOCK_ROWS :, :] = jnp.zeros((SEND_ROWS - TILES_HERE * BLOCK_ROWS, 128), F32)
         return carry
@@ -256,16 +265,23 @@
 
 def main_kernel(
     me_ref, pay_ref, window_ref, lift_ref, down_ref, rim_ref, order_ref, weights_ref,
-    coarse_ref, gp_ref, grads_ref, xs, cs, wf, wd, wins, lifts,
+    coarse_ref, gp_ref, grads_ref, xs, cs, wf, wd, wins, lifts, sems,
 ):
+    copies = []
+    for c in range(CHAN):
+        for which, held in enumerate((wf, wd)):
+            copies.append(
+                pltpu.make_async_copy(
+                    weights_ref.at[2 * c + which], held.at[:, pl.ds(c * CH, CH), :], sems.at[2 * c + which]
+                )
+            )
+    for copy in copies:
+        copy.start()
     chan = me_ref[4]
     pick = jnp.where(
         lax.broadcasted_iota(jnp.int32, (CH, C), 1) == lax.broadcasted_iota(jnp.int32, (CH, C), 0) + chan * CH, 1.0, 0.0
     ).astype(BF)
     for c in range(CHAN):
-        for k in range(9):
-            wf[k, c * CH : (c + 1) * CH, :] = weights_ref[2 * c, k]
-            wd[k, c * CH : (c + 1) * CH, :] = weights_ref[2 * c + 1, k]
         for t in range(TILES_HERE):
             base = t * PAY_ROWS
             for h in range(2):
@@ -284,6 +300,8 @@
             lifts[k, t * SPREAD_ROWS : (t + 1) * SPREAD_ROWS, :] = dot_nn(
                 lift_ref[t, k * SPREAD_ROWS : (k + 1) * SPREAD_ROWS, :], cs[t]
             ).astype(BF)
+    for copy in copies:
+        copy.wait()
     pre = dot_nn(wins[0], wf[0])
     back = dot_nt(lifts[0], wd[0])
     for k in range(1, 9):
@@ -306,7 +324,7 @@
         for k in range(9):
             part = dot_nn(windows[k * DOWN_ROWS : (k + 1) * DOWN_ROWS], wd[k])
             coarse = part if coarse is None else coarse + part
-        coarse_ref[t] = dot_nt(pick, coarse.astype(BF))[:, :COARSE].astype(BF)
+        coarse_ref[t] = dot_nt(coarse.astype(BF), pick)[:COARSE].astype(BF)
 
         rows = back[t * SPREAD_ROWS : (t + 1) * SPREAD_ROWS]
         rims = rows[CELLS:].astype(BF)
@@ -338,6 +356,10 @@
     return [pl.BlockSpec(memory_space=pltpu.VMEM)] * count
 
 
+def anywhere(count):
+    return [pl.BlockSpec(memory_space=pl.ANY)] * count
+
+
 def smem(count):
     return [pl.BlockSpec(memory_space=pltpu.SMEM)] * count
 
@@ -348,21 +370,24 @@
 def shards(fields, seam_table, w_first, w_down, cotangent):
     coords = [lax.axis_index(axis) for axis in ("ylo", "x", "z", "core", "chan")]
     me = jnp.stack(coords).astype(jnp.int32)
-    half = jnp.where(coords[3] == 0, w_first, w_down)
-    weights = lax.all_gather(half, ("chan", "core"), axis=0, tiled=False)
-
     sel_fields, sel_coarse = pack_selectors()
-    own, units = pl.pallas_call(
+    own, units, half = pl.pallas_call(
         pack_kernel,
         out_shape=(
             jax.ShapeDtypeStruct((TILES_HERE, PACK_ROWS, 128), BF),
             jax.ShapeDtypeStruct((YX, TILES_HERE * 4 * UNIT, 128), BF),
+            jax.ShapeDtypeStruct(w_first.shape, BF),
         ),
-        in_specs=vmem(4),
-        out_specs=tuple(vmem(2)),
+        in_specs=smem(1) + vmem(4) + anywhere(2),
+        out_specs=tuple(vmem(2) + anywhere(1)),
+        scratch_shapes=[pltpu.SemaphoreType.DMA],
         compiler_params=LIMIT,
         name="pack",
-    )(fields, cotangent, jnp.asarray(sel_fields, BF), jnp.asarray(sel_coarse, BF))
+    )(
+        me, fields, jnp.swapaxes(cotangent, 1, 2), jnp.asarray(sel_fields, BF), jnp.asarray(sel_coarse, BF),
+        w_first, w_down,
+    )
+    weights = lax.all_gather(half, ("chan", "core"), axis=0, tiled=False)
     units = lax.all_to_all(units, ("ylo", "x"), 0, 0).reshape(-1, 128)
     units = lax.all_gather(units, "core", axis=0, tiled=True)
     words, beyond = edge_words(seam_table)
@@ -399,11 +424,11 @@
     coarse, grad_pre, grads = pl.pallas_call(
         main_kernel,
         out_shape=(
-            jax.ShapeDtypeStruct((TILES_HERE, CH, COARSE), BF),
+            jax.ShapeDtypeStruct((TILES_HERE, COARSE, CH), BF),
             jax.ShapeDtypeStruct((TILES_HERE, CH, CELLS), BF),
             jax.ShapeDtypeStruct((CORE, 18 * CH, 128), BF),
         ),
-        in_specs=smem(1) + vmem(7),
+        in_specs=smem(1) + vmem(6) + anywhere(1),
         out_specs=tuple(vmem(3)),
         scratch_shapes=[
             pltpu.VMEM((TILES_HERE, C, C), BF),
@@ -412,6 +437,7 @@
             pltpu.VMEM((9, C, C), BF),
             pltpu.VMEM((9, TILES_HERE * PRE_ROWS, C), BF),
             pltpu.VMEM((9, TILES_HERE * SPREAD_ROWS, C), BF),
+            pltpu.SemaphoreType.DMA((2 * CHAN,)),
         ],
         compiler_params=LIMIT,
         name="tiles",
@@ -421,15 +447,17 @@
     )
 
     part = lax.all_to_all(grads, "core", 0, 0)
-    part = (part[0].astype(F32) + part[1].astype(F32)).astype(BF).reshape(PLANE, 18, 128)
-    part = lax.all_to_all(part, ("ylo", "x", "z"), 0, 0)
+    part = (part[0].astype(F32) + part[1].astype(F32)).astype(BF).reshape(NX * NZ, 36, 128)
+    part = lax.all_to_all(part, ("x", "z"), 0, 0)
     part = part.astype(F32).sum(0).astype(BF)
-    part = lax.all_to_all(jnp.broadcast_to(part[None], (PLANE, 18, 128)), ("ylo", "x", "z"), 0, 0)
+    part = lax.all_gather(part, "ylo", axis=0, tiled=False)
+    part = (part[0].astype(F32) + part[1].astype(F32)).astype(BF)
+    part = lax.all_to_all(jnp.broadcast_to(part[None], (NX * NZ, 36, 128)), ("x", "z"), 0, 0)
     whole = lax.all_gather(part.reshape(18 * CH, 128), "core", axis=0, tiled=False)
     whole = jnp.concatenate([whole[0], whole[1]], axis=1).astype(F32).reshape(2, 9, CH, C)
     tiles = TILES_HERE * PLANE * CORE
     return (
-        coarse,
+        jnp.swapaxes(coarse, 1, 2),
         whole[0] * float(tiles * CELLS) ** (-0.5),
         whole[1] * float(tiles * COARSE) ** (-0.5),
         grad_pre,

time: 146 us -> 144 us (0.986)
  blocking collectives: 37.3 us -> 55.3 us
  waiting for transfers between devices: 41 us -> 26.1 us
  starting transfers between devices: 25.3 us -> 19.3 us
  local copies, waits for them, and re-layouts: 6.51 us -> 9.45 us
  other arithmetic: 6.07 us -> 4.25 us
    all_to_all x1 -> x0, waiting for transfers between devices: 14 us -> none  [shards(): lax.all_to_all(jnp.broadcast_to(part[None], (PLANE, 18, 128)), ('ylo', 'x...]
    all_to_all x1 -> x2, blocking collectives: 19 us -> 30.8 us  [the longest x1 16.9 us: shards(): lax.all_to_all(jnp.broadcast_to(part[None], (NX * NZ, 36, 128)), ('x', 'z...]
    all_to_all x1 -> x0, starting transfers between devices: 5.94 us -> none  [shards(): lax.all_to_all(jnp.broadcast_to(part[None], (PLANE, 18, 128)), ('ylo', 'x...]
    unnamed x26 -> x30, local copies, waits for them, and re-layouts: 3.31 us -> 7.07 us
    all_gather x0 -> x1, blocking collectives: none -> 3.38 us  [shards(): part = lax.all_gather(part, 'ylo', axis=0, tiled=False)]
    all_gather x1, blocking collectives: 4.32 us -> 6.26 us  [shards(): lax.all_gather(part.reshape(18 * CH, 128), 'core', axis=0, tiled=False)]
    select_n x1 -> x0, other arithmetic: 1.79 us -> none  [shards(): half = jnp.where(coords[3] == 0, w_first, w_down)]
    pallas_call x1, Pallas kernels: 3.95 us -> 2.33 us  [shards(): pl.pallas_call(place_kernel, out_shape=jax.ShapeDtypeStruct((NZ, SEND_ROW...]
  transfers between devices with their start and end apart: 5 -> 4, of which waited for: 4 -> 3; matrix products, arithmetic and copies ran while one was open for 5% -> 4% of each run, Pallas kernels for 4% -> 2%
where the time goes in v3:
time: 144 us
  blocking collectives  55.3 us (38%)
  waiting for transfers between devices  26.1 us (18%)
  starting transfers between devices  19.3 us (13%)
  Pallas kernels  14.6 us (10%)
  between operations  14.3 us (10%)
  local copies, waits for them, and re-layouts  9.45 us (7%)
  other arithmetic  4.25 us (3%)
    all_to_all x1, blocking collectives, shards(): lax.all_to_all(jnp.broadcast_to(part[None], (NX * NZ, 36, 128)), ('x', 'z...  16.9 us
    all_to_all x1, blocking collectives, shards(): part = lax.all_to_all(part, ('x', 'z'), 0, 0)  13.9 us
    all_to_all x1, waiting for transfers between devices, shards(): got = lax.all_to_all(sends, 'z', 0, 0)  12.7 us
    pallas_call x1, Pallas kernels, shards(): pl.pallas_call(main_kernel, out_shape=(jax.ShapeDtypeStruct((TILES_HERE,...  9.3 us
    all_to_all x1, waiting for transfers between devices, shards(): payload = lax.all_to_all(joined, 'chan', 0, 0)  9.25 us
    all_to_all x1, starting transfers between devices, shards(): got = lax.all_to_all(sends, 'z', 0, 0)  7.85 us
    all_to_all x1, blocking collectives, shards(): part = lax.all_to_all(grads, 'core', 0, 0)  7.53 us
    all_gather x1, blocking collectives, shards(): units = lax.all_gather(units, 'core', axis=0, tiled=True)  7.39 us
  transfers between devices with their start and end apart: 4, of which 3 were waited for; matrix products, arithmetic and copies ran while one was open for 4% of the time, Pallas kernels for 2%

profile of v3, /device:TPU:1, one launch (start us, length us, event | category | flops | bytes accessed | tf_op | source)
XLA Modules:
  0.0 143.5 jit_solution(1794017931479378283)
XLA Ops:
  7.3 1.0 copy-done.1
  8.3 1.0 copy-done.2
  9.2 0.9 copy-done.4
  10.2 0.9 copy-done.5
  11.1 0.9 copy-done.6
  11.9 0.8 copy-done.8
  12.7 2.2 %pack.1 = (bf16[3,96,128]{2,1,0:T(8,128)(2,1)S(1)}, bf16[8,192,128]{2,1,0:T(8,128)(2,1)}, bf16[9,64,256]{2,1,0:T(8,128)(2,1)}) custom-call(s32[5]{0:T(128)S(1)} %stack.23.me_ref, bf16[3,64,144]{2,1,0:T(8,128)(2,1)S(1)} %copy-done.5, bf16[3,36,64]{2,1,0:T(8,128)(2,1)S(1)} %bitcast.36, bf16[2,160,144]{2,1,0:T(8,128)(2,1)S(1)} %copy-done.4, ...), custom_call_target="tpu_custom_call" | custom-call | tf_op jit(solution)/shard_map/pack/pallas_call | solution.py:374
  14.9 5.9 %all-to-all-start = ((bf16[8,192,128]{2,1,0:T(8,128)(2,1)}), bf16[8,192,128]{2,1,0:T(8,128)(2,1)S(1)}, u32[]{:S(2)}, u32[]{:S(2)}) async-start(bf16[8,192,128]{2,1,0:T(8,128)(2,1)} %get-tuple-element.10), calls=%async_computation | async-start | bytes 786432 | tf_op jit(solution)/shard_map/all_to_all | solution.py:391
  21.3 0.2 copy.26
  21.5 0.2 ne.70
  21.8 0.1 mul.88
  22.1 0.1 div.31
  22.4 0.1 rem.82
  22.7 0.1 squeeze.6
  23.3 4.1 %all-to-all-done = bf16[8,192,128]{2,1,0:T(8,128)(2,1)S(1)} async-done(((bf16[8,192,128]{2,1,0:T(8,128)(2,1)}), bf16[8,192,128]{2,1,0:T(8,128)(2,1)S(1)}, u32[]{:S(2)}, u32[]{:S(2)}) %all-to-all-start) | async-done | bytes 393248 | tf_op jit(solution)/shard_map/all_to_all | solution.py:391
  27.4 7.4 %all_gather.18.unit_ref = bf16[3072,128]{1,0:T(8,128)(2,1)S(1)} all-gather(bf16[1536,128]{1,0:T(8,128)(2,1)S(1)} %bitcast.37), channel_id=1, replica_groups=mesh['ylo'=2,'x'=4,'z'=8,'core'=2,'chan'=4] {'core'}, dimensions={0}, use_global_device_ids=true | all-gather | bytes 1179648 | tf_op jit(solution)/shard_map/all_gather | solution.py:392
  34.8 2.3 %place.1 = bf16[8,160,128]{2,1,0:T(8,128)(2,1)} custom-call(s32[1536]{0:T(1024)S(1)} %get-tuple-element.26.word_ref, s32[1536]{0:T(1024)S(1)} %get-tuple-element.25.beyond_ref, s32[5]{0:T(128)S(1)} %stack.23.me_ref, bf16[3072,128]{1,0:T(8,128)(2,1)S(1)} %all_gather.18.unit_ref), custom_call_target="tpu_custom_call" | custom-call | tf_op jit(solution)/shard_map/place/pallas_call | solution.py:394
  37.1 7.8 %all-to-all-start.1 = ((bf16[8,160,128]{2,1,0:T(8,128)(2,1)}), bf16[8,160,128]{2,1,0:T(8,128)(2,1)S(1)}, u32[]{:S(2)}, u32[]{:S(2)}) async-start(bf16[8,160,128]{2,1,0:T(8,128)(2,1)} %place.1), calls=%async_computation.1 | async-start | bytes 655360 | tf_op jit(solution)/shard_map/all_to_all | solution.py:403
  45.0 0.9 compare_convert_fusion.1.lift_ref
  45.8 12.7 %all-to-all-done.1.got_ref = bf16[8,160,128]{2,1,0:T(8,128)(2,1)S(1)} async-done(((bf16[8,160,128]{2,1,0:T(8,128)(2,1)}), bf16[8,160,128]{2,1,0:T(8,128)(2,1)S(1)}, u32[]{:S(2)}, u32[]{:S(2)}) %all-to-all-start.1) | async-done | bytes 327712 | tf_op jit(solution)/shard_map/all_to_all | solution.py:403
  58.6 0.8 join.1
  59.4 5.5 %all-to-all-start.2 = ((bf16[4,432,128]{2,1,0:T(8,128)(2,1)}), bf16[4,432,128]{2,1,0:T(8,128)(2,1)S(1)}, u32[]{:S(2)}, u32[]{:S(2)}) async-start(bf16[4,432,128]{2,1,0:T(8,128)(2,1)} %join.1), calls=%async_computation.2 | async-start | bytes 884736 | tf_op jit(solution)/shard_map/all_to_all | solution.py:413
  65.0 1.9 %compare_convert_fusion.window_ref = bf16[3,1584,256]{2,1,0:T(8,128)(2,1)} fusion(f32[256]{0:T(256)S(1)} %add_convert_fusion.2, f32[3,1584]{1,0:T(4,128)S(1)} %convolution_add_fusion), kind=kLoop, calls=%fused_computation | loop fusion | flops 2433024 | bytes 2453056 | tf_op jit(solution)/shard_map/convert_element_type | solution.py:422
  66.9 9.3 %all-to-all-done.2.pay_ref = bf16[4,432,128]{2,1,0:T(8,128)(2,1)S(1)} async-done(((bf16[4,432,128]{2,1,0:T(8,128)(2,1)}), bf16[4,432,128]{2,1,0:T(8,128)(2,1)S(1)}, u32[]{:S(2)}, u32[]{:S(2)}) %all-to-all-start.2) | async-done | bytes 442400 | tf_op jit(solution)/shard_map/all_to_all | solution.py:413
  76.2 1.7 %copy-done = bf16[72,64,256]{2,1,0:T(8,128)(2,1)S(1)} copy-done((bf16[72,64,256]{2,1,0:T(8,128)(2,1)S(1)}, bf16[72,64,256]{2,1,0:T(8,128)(2,1)}, u32[]{:S(2)}) %copy-start) | copy-done | bytes 2359320
  77.9 9.3 %tiles.1 = (bf16[3,36,64]{2,1,0:T(8,128)(2,1)}, bf16[3,64,144]{2,1,0:T(8,128)(2,1)}, bf16[2,1152,128]{2,1,0:T(8,128)(2,1)S(1)}) custom-call(s32[5]{0:T(128)S(1)} %stack.23.me_ref, bf16[4,432,128]{2,1,0:T(8,128)(2,1)S(1)} %all-to-all-done.2.pay_ref, bf16[3,1584,256]{2,1,0:T(8,128)(2,1)} %compare_convert_fusion.window_ref, ...), custom_call_target="tpu_custom_call" | custom-call | tf_op jit(solution)/shard_map/tiles/pallas_call | solution.py:424
  87.2 7.5 %all_to_all.30 = bf16[2,1152,128]{2,1,0:T(8,128)(2,1)S(1)} all-to-all(bf16[2,1152,128]{2,1,0:T(8,128)(2,1)S(1)} %get-tuple-element.14), channel_id=1, replica_groups=mesh['ylo'=2,'x'=4,'z'=8,'core'=2,'chan'=4] {'core'}, dimensions={0} | all-to-all | bytes 1179648 | tf_op jit(solution)/shard_map/all_to_all | solution.py:449
  94.9 13.9 %all_to_all.31 = bf16[32,36,128]{2,1,0:T(8,128)(2,1)S(1)} all-to-all(bf16[32,36,128]{2,1,0:T(8,128)(2,1)S(1)} %convert_element_type.62), channel_id=1, replica_groups=mesh['ylo'=2,'x'=4,'z'=8,'core'=2,'chan'=4] {'x','z'}, dimensions={0} | all-to-all | bytes 589824 | tf_op jit(solution)/shard_map/all_to_all | solution.py:451
  108.8 3.4 %all-gather.2 = bf16[2,36,128]{2,1,0:T(8,128)(2,1)S(1)} all-gather(bf16[1,36,128]{2,1,0:T(8,128)(2,1)S(1)} %bitcast.40), channel_id=3, replica_groups=mesh['ylo'=2,'x'=4,'z'=8,'core'=2,'chan'=4] {'ylo'}, dimensions={0}, use_global_device_ids=true | all-gather | bytes 27648 | tf_op jit(solution)/shard_map/all_gather | solution.py:453
  112.2 16.9 %all_to_all.32 = bf16[32,36,128]{2,1,0:T(8,128)(2,1)S(1)} all-to-all(bf16[32,36,128]{2,1,0:T(8,128)(2,1)S(1)} %broadcast_in_dim.9), channel_id=1, replica_groups=mesh['ylo'=2,'x'=4,'z'=8,'core'=2,'chan'=4] {'x','z'}, dimensions={0} | all-to-all | bytes 589824 | tf_op jit(solution)/shard_map/all_to_all | solution.py:455
  129.2 6.3 %all_gather.23 = bf16[2,1152,128]{2,1,0:T(8,128)(2,1)S(1)} all-gather(bf16[1,1152,128]{2,1,0:T(8,128)(2,1)S(1)} %all_gather_reshape.3), channel_id=1, replica_groups=mesh['ylo'=2,'x'=4,'z'=8,'core'=2,'chan'=4] {'core'}, dimensions={0}, use_global_device_ids=true | all-gather | bytes 884736 | tf_op jit(solution)/shard_map/all_gather | solution.py:456
  135.6 1.1 slice_multiply_fusion
  (55 shorter events, 2.2 us)
Async XLA Ops:
  7.2 13.6 %copy-start.12 = (s32[384,4,3]{0,1,2:T(4,128)S(1)}, s32[384,4,3]{0,1,2:T(4,128)}, u32[]{:S(2)}) copy-start(s32[384,4,3]{0,1,2:T(4,128)} %param.15) | copy-start | bytes 55300
  7.2 69.0 %all-gather.5.cloned.1.call-start = ((), (), s32[]{:S(2)}) async-start(), calls=%async_computation.6 | async-start | bytes 2654208 | tf_op jit(solution)/shard_map/all_gather | solution.py:390
  7.3 1.0 copy-start.1
  8.3 1.0 copy-start.2
  9.2 0.9 copy-start.4
  10.2 0.9 copy-start.5
  11.0 0.9 copy-start.6
  11.9 0.8 copy-start.8
  14.9 12.5 %all-to-all-start = ((bf16[8,192,128]{2,1,0:T(8,128)(2,1)}), bf16[8,192,128]{2,1,0:T(8,128)(2,1)S(1)}, u32[]{:S(2)}, u32[]{:S(2)}) async-start(bf16[8,192,128]{2,1,0:T(8,128)(2,1)} %get-tuple-element.10), calls=%async_computation | async-start | bytes 786432 | tf_op jit(solution)/shard_map/all_to_all | solution.py:391
  20.8 2.4 %copy-start.10 = (bf16[32,1728]{1,0:T(8,128)(2,1)S(1)}, bf16[32,1728]{1,0:T(8,128)(2,1)}, u32[]{:S(2)}) copy-start(bf16[32,1728]{1,0:T(8,128)(2,1)} %constant.130.clone) | copy-start | bytes 331780
  20.8 2.4 %copy-start.14 = (f32[1728]{0:T(1024)S(1)}, f32[1728]{0:T(1024)}, u32[]{:S(2)}) copy-start(f32[1728]{0:T(1024)} %constant.131.clone) | copy-start | bytes 20740
  37.1 21.5 %all-to-all-start.1 = ((bf16[8,160,128]{2,1,0:T(8,128)(2,1)}), bf16[8,160,128]{2,1,0:T(8,128)(2,1)S(1)}, u32[]{:S(2)}, u32[]{:S(2)}) async-start(bf16[8,160,128]{2,1,0:T(8,128)(2,1)} %place.1), calls=%async_computation.1 | async-start | bytes 655360 | tf_op jit(solution)/shard_map/all_to_all | solution.py:403
  44.9 19.9 %copy-start.11 = (bf16[32,1584]{1,0:T(8,128)(2,1)S(1)}, bf16[32,1584]{1,0:T(8,128)(2,1)}, u32[]{:S(2)}) copy-start(bf16[32,1584]{1,0:T(8,128)(2,1)} %constant.128.clone) | copy-start | bytes 304132
  45.0 19.9 %copy-start.13 = (f32[1584]{0:T(1024)S(1)}, f32[1584]{0:T(1024)}, u32[]{:S(2)}) copy-start(f32[1584]{0:T(1024)} %constant.129.clone) | copy-start | bytes 19012
  59.4 16.8 %all-to-all-start.2 = ((bf16[4,432,128]{2,1,0:T(8,128)(2,1)}), bf16[4,432,128]{2,1,0:T(8,128)(2,1)S(1)}, u32[]{:S(2)}, u32[]{:S(2)}) async-start(bf16[4,432,128]{2,1,0:T(8,128)(2,1)} %join.1), calls=%async_computation.2 | async-start | bytes 884736 | tf_op jit(solution)/shard_map/all_to_all | solution.py:413
  64.9 11.3 %copy-start.3 = (bf16[432,176]{1,0:T(8,128)(2,1)S(1)}, bf16[432,176]{1,0:T(8,128)(2,1)}, u32[]{:S(2)}) copy-start(bf16[432,176]{1,0:T(8,128)(2,1)} %constant.132.clone.down_ref) | copy-start | bytes 456196
  64.9 11.3 %copy-start.7 = (bf16[144,48]{1,0:T(8,128)(2,1)S(1)}, bf16[144,48]{1,0:T(8,128)(2,1)}, u32[]{:S(2)}) copy-start(bf16[144,48]{1,0:T(8,128)(2,1)} %constant.133.clone.rim_ref) | copy-start | bytes 41476
  64.9 11.3 %copy-start.9 = (bf16[48,64]{1,0:T(8,128)(2,1)S(1)}, bf16[48,64]{1,0:T(8,128)(2,1)}, u32[]{:S(2)}) copy-start(bf16[48,64]{1,0:T(8,128)(2,1)} %constant.134.clone.order_ref) | copy-start | bytes 18436
  76.2 1.7 %copy-start = (bf16[72,64,256]{2,1,0:T(8,128)(2,1)S(1)}, bf16[72,64,256]{2,1,0:T(8,128)(2,1)}, u32[]{:S(2)}) copy-start(bf16[72,64,256]{2,1,0:T(8,128)(2,1)} %all-gather.5.cloned.1.call-done) | copy-start | bytes 7077892
Sparse Core Ops, SparseCore 0:
  15.0 46.4 all-gather.4

commit v4 on v3

--- a/solution.py
+++ b/solution.py
@@ -32,9 +32,12 @@
 PAY_ROWS = X_HALF + C_HALF
 PACK_ROWS = 96
 UNIT = 16
-PRE_ROWS = 176
+PART = 40
+INNER = 4 * PART
+PRE_ROWS = INNER + 32
 DOWN_ROWS = 48
-SPREAD_ROWS = 192
+RIM_ROWS = 48
+RIM_TAPS = (0, 1, 2, 3, 6)
 
 
 def strip_cells(edge, depth):
@@ -47,29 +50,8 @@
     return [i * S + S - 1 - depth for i in range(S)]
 
 
-def pack_selectors():
-    rows = PACK_ROWS + 4 * UNIT
-    fields = np.zeros((2, rows, CELLS), np.float32)
-    coarse = np.zeros((2, rows, COARSE), np.float32)
-    for half in range(2):
-        for row in range(OWN_ROWS):
-            fields[half, row, 2 * row + half] = 1
-        for row in range(C_OWN):
-            coarse[half, OWN_ROWS + row, 2 * row + half] = 1
-        for edge in range(4):
-            base = PACK_ROWS + edge * UNIT
-            near, far = strip_cells(edge, 0), strip_cells(edge, 1)
-            for row in range(6):
-                fields[half, base + row, near[2 * row + half]] = 1
-                fields[half, base + 9 + row, far[2 * row + half]] = 1
-            for row in range(3):
-                at = 2 * row + half
-                if edge == 0:
-                    coarse[half, base + 6 + row, at] = 1
-                if edge == 2:
-                    coarse[half, base + 6 + row, at * HALF] = 1
-            fields[half, base + 15, near[11 - half]] = 1
-    return fields, coarse
+def cell_row(row, col):
+    return (row % 2 * 2 + col % 2) * PART + row // 2 * HALF + col // 2
 
 
 def own_at(cell):
@@ -94,12 +76,14 @@
             row, col = cell // S + a, cell % S + b
             inner_row, inner_col = 1 <= row <= S, 1 <= col <= S
             if inner_row and inner_col:
-                fixed[k, cell] = 1 + own_at((row - 1) * S + col - 1)
+                fixed[k, cell_row(cell // S, cell % S)] = 1 + own_at((row - 1) * S + col - 1)
             elif inner_row or inner_col:
                 edge = (2 if col == 0 else 3) if inner_row else (0 if row == 0 else 1)
                 at = row - 1 if inner_row else col - 1
                 for flip in range(2):
-                    varied[edge, :, flip, k, cell] = 1 + near_at(edge, 11 - at if flip else at, 0)
+                    varied[edge, :, flip, k, cell_row(cell // S, cell % S)] = 1 + near_at(
+                        edge, 11 - at if flip else at, 0
+                    )
         for slot, edge in enumerate((0, 2)):
             own = strip_cells(edge, 0)
             for facing in range(4):
@@ -114,20 +98,14 @@
                             at = own_at(own[11 - along if flip else along])
                         else:
                             continue
-                        varied[edge, facing, flip, k, CELLS + 16 * slot + j] = 1 + at
+                        varied[edge, facing, flip, k, INNER + 16 * slot + j] = 1 + at
     return fixed.reshape(-1), varied.reshape(32, -1)
 
 
-def spread_index():
-    fixed = np.zeros((9, SPREAD_ROWS), np.float32)
-    varied = np.zeros((4, 4, 2, 9, SPREAD_ROWS), np.float32)
-    for k in range(9):
+def rim_index():
+    varied = np.zeros((4, 4, 2, len(RIM_TAPS), RIM_ROWS), np.float32)
+    for slot, k in enumerate(RIM_TAPS):
         a, b = k // 3, k % 3
-        for cell in range(CELLS):
-            row, col = cell // S + 1 - a, cell % S + 1 - b
-            if row % 2 == 0 and col % 2 == 0 and 0 <= row < S and 0 <= col < S:
-                at = (row // 2) * HALF + col // 2
-                fixed[k, cell] = 1 + at // 2 + C_HALF * (at % 2)
         for edge in range(4):
             for flip in range(2):
                 for j in range(S):
@@ -135,10 +113,21 @@
                         at = (11 - j if flip else j) + 1 - tap
                         if live and at % 2 == 0 and 0 <= at < S:
                             at //= 2
-                            varied[edge, facing, flip, k, CELLS + edge * S + j] = (
+                            varied[edge, facing, flip, slot, edge * S + j] = (
                                 1 + C_OWN + 3 * edge + at // 2 + C_HALF * (at % 2)
                             )
-    return fixed.reshape(-1), varied.reshape(32, -1)
+    return np.zeros(len(RIM_TAPS) * RIM_ROWS, np.float32), varied.reshape(32, -1)
+
+
+def shift_selector():
+    chosen = np.zeros((2, 2, PART, 2 * C_HALF), np.float32)
+    for down in range(2):
+        for right in range(2):
+            for row in range(HALF - down):
+                for col in range(HALF - right):
+                    at = (row + down) * HALF + col + right
+                    chosen[down, right, row * HALF + col, at // 2 + C_HALF * (at % 2)] = 1
+    return chosen.reshape(INNER, 2 * C_HALF)
 
 
 def down_selector():
@@ -149,20 +138,27 @@
             if row == 0 and col == 0:
                 continue
             if row == 0:
-                at = CELLS + col - 1
+                at = INNER + col - 1
             elif col == 0:
-                at = CELLS + 16 + row - 1
+                at = INNER + 16 + row - 1
             else:
-                at = (row - 1) * S + col - 1
+                at = cell_row(row - 1, col - 1)
             chosen[k, cell, at] = 1
     return chosen.reshape(9 * DOWN_ROWS, PRE_ROWS)
 
 
 def rim_selector():
-    chosen = np.zeros((CELLS, 4 * S), np.float32)
+    chosen = np.zeros((INNER, RIM_ROWS), np.float32)
     for edge in range(4):
         for j, cell in enumerate(strip_cells(edge, 0)):
-            chosen[cell, edge * S + j] = 1
+            chosen[cell_row(cell // S, cell % S), edge * S + j] = 1
+    return chosen
+
+
+def cell_selector():
+    chosen = np.zeros((INNER, CELLS), np.float32)
+    for cell in range(CELLS):
+        chosen[cell_row(cell // S, cell % S), cell] = 1
     return chosen
 
 
@@ -181,25 +177,53 @@
     return lax.dot_general(left, right, (((1,), (1,)), ((), ())), preferred_element_type=F32)
 
 
-def pack_kernel(me_ref, fields_ref, cot_ref, self_ref, selc_ref, first_ref, down_ref, own_ref, unit_ref, half_ref, sem):
+def pack_selectors(half):
+    rows = PACK_ROWS + 4 * UNIT
+    row = lax.broadcasted_iota(jnp.int32, (rows, CELLS), 0)
+    at = lax.broadcasted_iota(jnp.int32, (rows, CELLS), 1)
+    edge, j = (row - PACK_ROWS) >> 4, (row - PACK_ROWS) & 15
+    deep = jnp.where(jnp.logical_and(j >= 9, j < 15), 1, 0)
+    along = jnp.where(j < 6, 2 * j + half, jnp.where(j < 15, 2 * (j - 9) + half, 11 - half))
+    start = jnp.where(edge == 0, S * deep, jnp.where(edge == 1, S * (S - 1 - deep), jnp.where(edge == 2, deep, S - 1 - deep)))
+    cell = start + along * jnp.where(edge < 2, 1, S)
+    cell = jnp.where(jnp.logical_or(j < 6, j >= 9), cell, -1)
+    cell = jnp.where(row < OWN_ROWS, 2 * row + half, jnp.where(row < PACK_ROWS, -1, cell))
+    fields = jnp.where(at == cell, 1.0, 0.0).astype(BF)
+    row, at, edge, j = row[:, :COARSE], at[:, :COARSE], edge[:, :COARSE], j[:, :COARSE]
+    cell = (2 * (j - 6) + half) * jnp.where(edge == 0, 1, HALF)
+    live = jnp.logical_and(jnp.logical_and(j >= 6, j < 9), jnp.logical_or(edge == 0, edge == 2))
+    cell = jnp.where(live, cell, -1)
+    own = jnp.where(row < OWN_ROWS + C_OWN, 2 * (row - OWN_ROWS) + half, -1)
+    cell = jnp.where(row < PACK_ROWS, own, cell)
+    return fields, jnp.where(at == cell, 1.0, 0.0).astype(BF)
+
+
+def pack_kernel(me_ref, fields_hbm, cot_hbm, first_ref, down_ref, own_ref, unit_ref, half_ref, fields_ref, cot_ref, sems):
+    loads = [
+        pltpu.make_async_copy(fields_hbm, fields_ref, sems.at[0]),
+        pltpu.make_async_copy(cot_hbm, cot_ref, sems.at[1]),
+    ]
+    for load in loads:
+        load.start()
+
     @pl.when(me_ref[3] == 0)
     def _():
-        pltpu.make_async_copy(first_ref, half_ref, sem).start()
+        pltpu.make_async_copy(first_ref, half_ref, sems.at[2]).start()
 
     @pl.when(me_ref[3] == 1)
     def _():
-        pltpu.make_async_copy(down_ref, half_ref, sem).start()
-
+        pltpu.make_async_copy(down_ref, half_ref, sems.at[2]).start()
+
+    chosen = [pack_selectors(h) for h in range(2)]
+    for load in loads:
+        load.wait()
     for t in range(TILES_HERE):
-        halves = [
-            (dot_nt(self_ref[h], fields_ref[t]) + dot_nn(selc_ref[h], cot_ref[t])).astype(BF)
-            for h in range(2)
-        ]
+        halves = [(dot_nt(f, fields_ref[t]) + dot_nn(c, cot_ref[t])).astype(BF) for f, c in chosen]
         for h in range(2):
             own_ref[t, :, h * CH : (h + 1) * CH] = halves[h][:PACK_ROWS]
             for copy in range(YX):
                 unit_ref[copy, t * 4 * UNIT : (t + 1) * 4 * UNIT, h * CH : (h + 1) * CH] = halves[h][PACK_ROWS:]
-    pltpu.make_async_copy(first_ref, half_ref, sem).wait()
+    pltpu.make_async_copy(first_ref, half_ref, sems.at[2]).wait()
 
 
 def edge_words(seam_table):
@@ -264,8 +288,8 @@
 
 
 def main_kernel(
-    me_ref, pay_ref, window_ref, lift_ref, down_ref, rim_ref, order_ref, weights_ref,
-    coarse_ref, gp_ref, grads_ref, xs, cs, wf, wd, wins, lifts, sems,
+    me_ref, pay_ref, window_ref, rim_at_ref, shift_ref, down_ref, rim_ref, order_ref, cell_ref, weights_ref,
+    coarse_ref, gp_ref, grads_ref, xs, cs, wf, wd, wins, ups, rims, downs, sems,
 ):
     copies = []
     for c in range(CHAN):
@@ -292,21 +316,31 @@
                 ]
     for t in range(TILES_HERE):
         xs[t, 2 * X_HALF :, :] = jnp.zeros((C - 2 * X_HALF, C), BF)
-    for k in range(9):
-        for t in range(TILES_HERE):
-            wins[k, t * PRE_ROWS : (t + 1) * PRE_ROWS, :] = dot_nn(
+    for t in range(TILES_HERE):
+        for k in range(9):
+            wins[t * PRE_ROWS : (t + 1) * PRE_ROWS, k * C : (k + 1) * C] = dot_nn(
                 window_ref[t, k * PRE_ROWS : (k + 1) * PRE_ROWS, :], xs[t]
             ).astype(BF)
-            lifts[k, t * SPREAD_ROWS : (t + 1) * SPREAD_ROWS, :] = dot_nn(
-                lift_ref[t, k * SPREAD_ROWS : (k + 1) * SPREAD_ROWS, :], cs[t]
-            ).astype(BF)
+        shifted = dot_nn(shift_ref[...], cs[t])
+        for s in range(4):
+            ups[s, t * PART : (t + 1) * PART, :] = shifted[s * PART : (s + 1) * PART]
+        near = dot_nn(rim_at_ref[t], cs[t]).astype(BF)
+        for s in range(len(RIM_TAPS)):
+            rims[s, t * RIM_ROWS : (t + 1) * RIM_ROWS, :] = near[s * RIM_ROWS : (s + 1) * RIM_ROWS]
     for copy in copies:
         copy.wait()
-    pre = dot_nn(wins[0], wf[0])
-    back = dot_nt(lifts[0], wd[0])
-    for k in range(1, 9):
-        pre = pre + dot_nn(wins[k], wf[k])
-        back = back + dot_nt(lifts[k], wd[k])
+    pre = dot_nn(wins[...], wf[...].reshape(9 * C, C))
+    ups_low = [ups[s].astype(BF) for s in range(4)]
+    blocks = (
+        dot_nt(ups_low[0], wd[4]),
+        dot_nt(ups_low[1], wd[3]) + dot_nt(ups_low[0], wd[5]),
+        dot_nt(ups_low[2], wd[1]) + dot_nt(ups_low[0], wd[7]),
+        dot_nt(ups_low[3], wd[0]) + dot_nt(ups_low[2], wd[2]) + dot_nt(ups_low[1], wd[6]) + dot_nt(ups_low[0], wd[8]),
+    )
+    rim = dot_nt(rims[0], wd[RIM_TAPS[0]])
+    for s in range(1, len(RIM_TAPS)):
+        rim = rim + dot_nt(rims[s], wd[RIM_TAPS[s]])
+    rim = rim.astype(BF)
     scale = np.float32(np.sqrt(2 / np.pi))
     squared = pre * pre
     bent = jnp.tanh(scale * (pre + np.float32(0.044715) * squared * pre))
@@ -314,23 +348,18 @@
     hidden = (pre * gate).astype(BF)
     slope = gate + 0.5 * pre * (1.0 - bent * bent) * scale * (1.0 + np.float32(3 * 0.044715) * squared)
 
-    down = [None] * TILES_HERE
     first_sum = None
     down_sum = None
     for t in range(TILES_HERE):
         own_hidden = hidden[t * PRE_ROWS : (t + 1) * PRE_ROWS]
-        coarse = None
         windows = dot_nn(down_ref[...], own_hidden).astype(BF)
         for k in range(9):
-            part = dot_nn(windows[k * DOWN_ROWS : (k + 1) * DOWN_ROWS], wd[k])
-            coarse = part if coarse is None else coarse + part
-        coarse_ref[t] = dot_nt(coarse.astype(BF), pick)[:COARSE].astype(BF)
-
-        rows = back[t * SPREAD_ROWS : (t + 1) * SPREAD_ROWS]
-        rims = rows[CELLS:].astype(BF)
-        grad_hidden = rows[:CELLS] + dot_nn(rim_ref[...], rims)
-        grad_pre = (grad_hidden * slope[t * PRE_ROWS : t * PRE_ROWS + CELLS]).astype(BF)
-        gp_ref[t] = dot_nt(pick, grad_pre).astype(BF)
+            downs[t * DOWN_ROWS : (t + 1) * DOWN_ROWS, k * C : (k + 1) * C] = windows[k * DOWN_ROWS : (k + 1) * DOWN_ROWS]
+
+        grad_hidden = jnp.concatenate([block[t * PART : (t + 1) * PART] for block in blocks], axis=0)
+        grad_hidden = grad_hidden + dot_nn(rim_ref[...], rim[t * RIM_ROWS : (t + 1) * RIM_ROWS])
+        grad_pre = (grad_hidden * slope[t * PRE_ROWS : t * PRE_ROWS + INNER]).astype(BF)
+        gp_ref[t] = dot_nn(dot_nt(pick, grad_pre).astype(BF), cell_ref[...]).astype(BF)
 
         x_own = dot_nt(pick, xs[t]).astype(BF)
         h_own = dot_nt(pick, own_hidden).astype(BF)
@@ -338,15 +367,18 @@
         first_parts, down_parts = [], []
         for k in range(9):
             first_parts.append(
-                dot_nt(x_own, window_ref[t, k * PRE_ROWS : k * PRE_ROWS + CELLS, :]).astype(BF)
+                dot_nt(x_own, window_ref[t, k * PRE_ROWS : k * PRE_ROWS + INNER, :]).astype(BF)
             )
             down_parts.append(
                 dot_nt(h_own, down_ref[k * DOWN_ROWS : (k + 1) * DOWN_ROWS, :]).astype(BF)
             )
-        first = dot_nn(jnp.concatenate(first_parts, axis=0), grad_pre)
-        first_sum = first if first_sum is None else first_sum + first
+        part = dot_nn(jnp.concatenate(first_parts, axis=0), grad_pre)
+        first_sum = part if first_sum is None else first_sum + part
         part = dot_nn(jnp.concatenate(down_parts, axis=0), up)
         down_sum = part if down_sum is None else down_sum + part
+    coarse = dot_nt(dot_nn(downs[...], wd[...].reshape(9 * C, C)).astype(BF), pick).astype(BF)
+    for t in range(TILES_HERE):
+        coarse_ref[t] = coarse[t * DOWN_ROWS : t * DOWN_ROWS + COARSE]
     for h in range(CORE):
         grads_ref[h, : 9 * CH, :] = first_sum[:, h * 128 : (h + 1) * 128].astype(BF)
         grads_ref[h, 9 * CH :, :] = down_sum[:, h * 128 : (h + 1) * 128].astype(BF)
@@ -356,8 +388,8 @@
     return [pl.BlockSpec(memory_space=pltpu.VMEM)] * count
 
 
-def anywhere(count):
-    return [pl.BlockSpec(memory_space=pl.ANY)] * count
+def hbm(count):
+    return [pl.BlockSpec(memory_space=pltpu.HBM)] * count
 
 
 def smem(count):
@@ -365,12 +397,38 @@
 
 
 LIMIT = pltpu.CompilerParams(vmem_limit_bytes=48 * 1024 * 1024)
+
+
+def tiles_call(me, payload, window, rim_at, weights):
+    constants = (shift_selector(), down_selector(), rim_selector(), order_selector(), cell_selector())
+    return pl.pallas_call(
+        main_kernel,
+        out_shape=(
+            jax.ShapeDtypeStruct((TILES_HERE, COARSE, CH), BF),
+            jax.ShapeDtypeStruct((TILES_HERE, CH, CELLS), BF),
+            jax.ShapeDtypeStruct((CORE, 18 * CH, 128), BF),
+        ),
+        in_specs=smem(1) + vmem(8) + hbm(1),
+        out_specs=tuple(vmem(3)),
+        scratch_shapes=[
+            pltpu.VMEM((TILES_HERE, C, C), BF),
+            pltpu.VMEM((TILES_HERE, 2 * C_HALF, C), BF),
+            pltpu.VMEM((9, C, C), BF),
+            pltpu.VMEM((9, C, C), BF),
+            pltpu.VMEM((TILES_HERE * PRE_ROWS, 9 * C), BF),
+            pltpu.VMEM((4, TILES_HERE * PART, C), F32),
+            pltpu.VMEM((len(RIM_TAPS), TILES_HERE * RIM_ROWS, C), BF),
+            pltpu.VMEM((TILES_HERE * DOWN_ROWS, 9 * C), BF),
+            pltpu.SemaphoreType.DMA((2 * CHAN,)),
+        ],
+        compiler_params=LIMIT,
+        name="tiles",
+    )(me, payload, window, rim_at, *(jnp.asarray(array, BF) for array in constants), weights)
 
 
 def shards(fields, seam_table, w_first, w_down, cotangent):
     coords = [lax.axis_index(axis) for axis in ("ylo", "x", "z", "core", "chan")]
     me = jnp.stack(coords).astype(jnp.int32)
-    sel_fields, sel_coarse = pack_selectors()
     own, units, half = pl.pallas_call(
         pack_kernel,
         out_shape=(
@@ -378,15 +436,16 @@
             jax.ShapeDtypeStruct((YX, TILES_HERE * 4 * UNIT, 128), BF),
             jax.ShapeDtypeStruct(w_first.shape, BF),
         ),
-        in_specs=smem(1) + vmem(4) + anywhere(2),
-        out_specs=tuple(vmem(2) + anywhere(1)),
-        scratch_shapes=[pltpu.SemaphoreType.DMA],
+        in_specs=smem(1) + hbm(4),
+        out_specs=tuple(vmem(2) + hbm(1)),
+        scratch_shapes=[
+            pltpu.VMEM((TILES_HERE, CH, CELLS), BF),
+            pltpu.VMEM((TILES_HERE, COARSE, CH), BF),
+            pltpu.SemaphoreType.DMA((3,)),
+        ],
         compiler_params=LIMIT,
         name="pack",
-    )(
-        me, fields, jnp.swapaxes(cotangent, 1, 2), jnp.asarray(sel_fields, BF), jnp.asarray(sel_coarse, BF),
-        w_first, w_down,
-    )
+    )(me, fields, jnp.swapaxes(cotangent, 1, 2), w_first, w_down)
     weights = lax.all_gather(half, ("chan", "core"), axis=0, tiled=False)
     units = lax.all_to_all(units, ("ylo", "x"), 0, 0).reshape(-1, 128)
     units = lax.all_gather(units, "core", axis=0, tiled=True)
@@ -417,34 +476,11 @@
     code = own_table[:, :, 1] * 2 + own_table[:, :, 2]
     chosen = (code[:, :, None] == jnp.arange(8, dtype=jnp.int32)).astype(BF).reshape(TILES_HERE, 32)
     one_hots = []
-    for (fixed, varied), depth in ((window_index(), C), (spread_index(), 2 * C_HALF)):
+    for (fixed, varied), depth in ((window_index(), C), (rim_index(), 2 * C_HALF)):
         at = jnp.dot(chosen, jnp.asarray(varied, BF), preferred_element_type=F32) + jnp.asarray(fixed, F32)
         one_hots.append((at[:, :, None] == jnp.arange(1, depth + 1, dtype=jnp.int32).astype(F32)).astype(BF))
 
-    coarse, grad_pre, grads = pl.pallas_call(
-        main_kernel,
-        out_shape=(
-            jax.ShapeDtypeStruct((TILES_HERE, COARSE, CH), BF),
-            jax.ShapeDtypeStruct((TILES_HERE, CH, CELLS), BF),
-            jax.ShapeDtypeStruct((CORE, 18 * CH, 128), BF),
-        ),
-        in_specs=smem(1) + vmem(6) + anywhere(1),
-        out_specs=tuple(vmem(3)),
-        scratch_shapes=[
-            pltpu.VMEM((TILES_HERE, C, C), BF),
-            pltpu.VMEM((TILES_HERE, 2 * C_HALF, C), BF),
-            pltpu.VMEM((9, C, C), BF),
-            pltpu.VMEM((9, C, C), BF),
-            pltpu.VMEM((9, TILES_HERE * PRE_ROWS, C), BF),
-            pltpu.VMEM((9, TILES_HERE * SPREAD_ROWS, C), BF),
-            pltpu.SemaphoreType.DMA((2 * CHAN,)),
-        ],
-        compiler_params=LIMIT,
-        name="tiles",
-    )(
-        me, payload, one_hots[0], one_hots[1], jnp.asarray(down_selector(), BF), jnp.asarray(rim_selector(), BF),
-        jnp.asarray(order_selector(), BF), weights,
-    )
+    coarse, grad_pre, grads = tiles_call(me, payload, one_hots[0], one_hots[1], weights)
 
     part = lax.all_to_all(grads, "core", 0, 0)
     part = (part[0].astype(F32) + part[1].astype(F32)).astype(BF).reshape(NX * NZ, 36, 128)

time: 144 us -> 142 us (0.986)
  local copies, waits for them, and re-layouts: 9.45 us -> 7.65 us
    unnamed x30 -> x28, local copies, waits for them, and re-layouts: 7.07 us -> 5.28 us
  transfers between devices with their start and end apart: 4 -> 4, of which waited for: 3 -> 3; matrix products, arithmetic and copies ran while one was open for 4% -> 3% of each run, Pallas kernels for 2% -> 2%
where the time goes in v4:
time: 142 us; the launch traced here: 141 us
  blocking collectives  55.4 us (39%)
  waiting for transfers between devices  26.8 us (19%)
  starting transfers between devices  19.3 us (14%)
  between operations  14.3 us (10%)
  Pallas kernels  14 us (10%)
  local copies, waits for them, and re-layouts  7.65 us (5%)
  other arithmetic  3.63 us (3%)
    all_to_all x1, blocking collectives, shards(): lax.all_to_all(jnp.broadcast_to(part[None], (NX * NZ, 36, 128)), ('x', 'z...  16.9 us
    all_to_all x1, blocking collectives, shards(): part = lax.all_to_all(part, ('x', 'z'), 0, 0)  13.9 us
    all_to_all x1, waiting for transfers between devices, shards(): got = lax.all_to_all(sends, 'z', 0, 0)  13.3 us
    all_to_all x1, waiting for transfers between devices, shards(): payload = lax.all_to_all(joined, 'chan', 0, 0)  9.16 us
    pallas_call x1, Pallas kernels, tiles_call(): pl.pallas_call(main_kernel, out_shape=(jax.ShapeDtypeStruct((TILES_HERE,...  8.69 us
    all_to_all x1, starting transfers between devices, shards(): got = lax.all_to_all(sends, 'z', 0, 0)  7.85 us
    all_gather x1, blocking collectives, shards(): units = lax.all_gather(units, 'core', axis=0, tiled=True)  7.66 us
    all_to_all x1, blocking collectives, shards(): part = lax.all_to_all(grads, 'core', 0, 0)  7.48 us
  transfers between devices with their start and end apart: 4, of which 3 were waited for; matrix products, arithmetic and copies ran while one was open for 3% of the time, Pallas kernels for 2%

profile of v4, /device:TPU:1, one launch (start us, length us, event | category | flops | bytes accessed | tf_op | source)
XLA Modules:
  0.0 141.2 jit_solution(15295496611265066839)
XLA Ops:
  7.3 1.0 copy-done.1
  8.3 1.0 copy-done.2
  9.2 0.9 copy-done.4
  10.1 0.8 copy-done.8
  10.9 2.2 %pack.1 = (bf16[3,96,128]{2,1,0:T(8,128)(2,1)S(1)}, bf16[8,192,128]{2,1,0:T(8,128)(2,1)}, bf16[9,64,256]{2,1,0:T(8,128)(2,1)}) custom-call(s32[5]{0:T(128)S(1)} %stack.23.me_ref, bf16[3,64,144]{2,1,0:T(8,128)(2,1)S(1)} %copy-done.4, bf16[3,36,64]{2,1,0:T(8,128)(2,1)S(1)} %bitcast.36, bf16[9,64,256]{2,1,0:T(8,128)(2,1)S(1)} %copy-done.1, ...), custom_call_target="tpu_custom_call" | custom-call | tf_op jit(solution)/shard_map/pack/pallas_call | solution.py:432
  13.1 5.9 %all-to-all-start = ((bf16[8,192,128]{2,1,0:T(8,128)(2,1)}), bf16[8,192,128]{2,1,0:T(8,128)(2,1)S(1)}, u32[]{:S(2)}, u32[]{:S(2)}) async-start(bf16[8,192,128]{2,1,0:T(8,128)(2,1)} %get-tuple-element.10), calls=%async_computation | async-start | bytes 786432 | tf_op jit(solution)/shard_map/all_to_all | solution.py:450
  19.4 0.2 copy.26
  19.6 0.2 ne.70
  19.8 0.1 copy.31
  20.0 0.1 mul.88
  20.2 0.1 div.31
  20.5 0.1 rem.82
  20.8 0.1 squeeze.6
  21.1 0.1 mul.84
  21.3 4.3 %all-to-all-done = bf16[8,192,128]{2,1,0:T(8,128)(2,1)S(1)} async-done(((bf16[8,192,128]{2,1,0:T(8,128)(2,1)}), bf16[8,192,128]{2,1,0:T(8,128)(2,1)S(1)}, u32[]{:S(2)}, u32[]{:S(2)}) %all-to-all-start) | async-done | bytes 393248 | tf_op jit(solution)/shard_map/all_to_all | solution.py:450
  25.6 7.7 %all_gather.18.unit_ref = bf16[3072,128]{1,0:T(8,128)(2,1)S(1)} all-gather(bf16[1536,128]{1,0:T(8,128)(2,1)S(1)} %bitcast.37), channel_id=1, replica_groups=mesh['ylo'=2,'x'=4,'z'=8,'core'=2,'chan'=4] {'core'}, dimensions={0}, use_global_device_ids=true | all-gather | bytes 1179648 | tf_op jit(solution)/shard_map/all_gather | solution.py:451
  33.3 2.3 %place.1 = bf16[8,160,128]{2,1,0:T(8,128)(2,1)} custom-call(s32[1536]{0:T(1024)S(1)} %get-tuple-element.26.word_ref, s32[1536]{0:T(1024)S(1)} %get-tuple-element.25.beyond_ref, s32[5]{0:T(128)S(1)} %stack.23.me_ref, bf16[3072,128]{1,0:T(8,128)(2,1)S(1)} %all_gather.18.unit_ref), custom_call_target="tpu_custom_call" | custom-call | tf_op jit(solution)/shard_map/place/pallas_call | solution.py:453
  35.6 7.8 %all-to-all-start.1 = ((bf16[8,160,128]{2,1,0:T(8,128)(2,1)}), bf16[8,160,128]{2,1,0:T(8,128)(2,1)S(1)}, u32[]{:S(2)}, u32[]{:S(2)}) async-start(bf16[8,160,128]{2,1,0:T(8,128)(2,1)} %place.1), calls=%async_computation.1 | async-start | bytes 655360 | tf_op jit(solution)/shard_map/all_to_all | solution.py:462
  43.6 0.2 compare_convert_fusion.1.rim_at_ref
  43.8 13.3 %all-to-all-done.1.got_ref = bf16[8,160,128]{2,1,0:T(8,128)(2,1)S(1)} async-done(((bf16[8,160,128]{2,1,0:T(8,128)(2,1)}), bf16[8,160,128]{2,1,0:T(8,128)(2,1)S(1)}, u32[]{:S(2)}, u32[]{:S(2)}) %all-to-all-start.1) | async-done | bytes 327712 | tf_op jit(solution)/shard_map/all_to_all | solution.py:462
  57.1 0.8 join.1
  57.9 5.5 %all-to-all-start.2 = ((bf16[4,432,128]{2,1,0:T(8,128)(2,1)}), bf16[4,432,128]{2,1,0:T(8,128)(2,1)S(1)}, u32[]{:S(2)}, u32[]{:S(2)}) async-start(bf16[4,432,128]{2,1,0:T(8,128)(2,1)} %join.1), calls=%async_computation.2 | async-start | bytes 884736 | tf_op jit(solution)/shard_map/all_to_all | solution.py:472
  63.6 2.0 %compare_convert_fusion.window_ref = bf16[3,1728,256]{2,1,0:T(8,128)(2,1)} fusion(f32[256]{0:T(256)S(1)} %add_convert_fusion.2, f32[3,1728]{1,0:T(4,128)S(1)} %convolution_add_fusion), kind=kLoop, calls=%fused_computation | loop fusion | flops 2654208 | bytes 2675968 | tf_op jit(solution)/shard_map/convert_element_type | solution.py:481
  65.6 9.2 %all-to-all-done.2.pay_ref = bf16[4,432,128]{2,1,0:T(8,128)(2,1)S(1)} async-done(((bf16[4,432,128]{2,1,0:T(8,128)(2,1)}), bf16[4,432,128]{2,1,0:T(8,128)(2,1)S(1)}, u32[]{:S(2)}, u32[]{:S(2)}) %all-to-all-start.2) | async-done | bytes 442400 | tf_op jit(solution)/shard_map/all_to_all | solution.py:472
  74.8 1.7 %copy-done = bf16[72,64,256]{2,1,0:T(8,128)(2,1)S(1)} copy-done((bf16[72,64,256]{2,1,0:T(8,128)(2,1)S(1)}, bf16[72,64,256]{2,1,0:T(8,128)(2,1)}, u32[]{:S(2)}) %copy-start) | copy-done | bytes 2359320
  76.4 8.7 %tiles.1 = (bf16[3,36,64]{2,1,0:T(8,128)(2,1)}, bf16[3,64,144]{2,1,0:T(8,128)(2,1)}, bf16[2,1152,128]{2,1,0:T(8,128)(2,1)S(1)}) custom-call(s32[5]{0:T(128)S(1)} %stack.23.me_ref, bf16[4,432,128]{2,1,0:T(8,128)(2,1)S(1)} %all-to-all-done.2.pay_ref, bf16[3,1728,256]{2,1,0:T(8,128)(2,1)} %compare_convert_fusion.window_ref, ...), custom_call_target="tpu_custom_call" | custom-call | tf_op jit(solution)/shard_map/tiles/pallas_call | solution.py:404
  85.1 7.5 %all_to_all.30 = bf16[2,1152,128]{2,1,0:T(8,128)(2,1)S(1)} all-to-all(bf16[2,1152,128]{2,1,0:T(8,128)(2,1)S(1)} %get-tuple-element.14), channel_id=1, replica_groups=mesh['ylo'=2,'x'=4,'z'=8,'core'=2,'chan'=4] {'core'}, dimensions={0} | all-to-all | bytes 1179648 | tf_op jit(solution)/shard_map/all_to_all | solution.py:485
  92.7 13.9 %all_to_all.31 = bf16[32,36,128]{2,1,0:T(8,128)(2,1)S(1)} all-to-all(bf16[32,36,128]{2,1,0:T(8,128)(2,1)S(1)} %convert_element_type.62), channel_id=1, replica_groups=mesh['ylo'=2,'x'=4,'z'=8,'core'=2,'chan'=4] {'x','z'}, dimensions={0} | all-to-all | bytes 589824 | tf_op jit(solution)/shard_map/all_to_all | solution.py:487
  106.7 3.3 %all-gather.2 = bf16[2,36,128]{2,1,0:T(8,128)(2,1)S(1)} all-gather(bf16[1,36,128]{2,1,0:T(8,128)(2,1)S(1)} %bitcast.40), channel_id=3, replica_groups=mesh['ylo'=2,'x'=4,'z'=8,'core'=2,'chan'=4] {'ylo'}, dimensions={0}, use_global_device_ids=true | all-gather | bytes 27648 | tf_op jit(solution)/shard_map/all_gather | solution.py:489
  110.0 16.9 %all_to_all.32 = bf16[32,36,128]{2,1,0:T(8,128)(2,1)S(1)} all-to-all(bf16[32,36,128]{2,1,0:T(8,128)(2,1)S(1)} %broadcast_in_dim.9), channel_id=1, replica_groups=mesh['ylo'=2,'x'=4,'z'=8,'core'=2,'chan'=4] {'x','z'}, dimensions={0} | all-to-all | bytes 589824 | tf_op jit(solution)/shard_map/all_to_all | solution.py:491
  126.9 6.2 %all_gather.23 = bf16[2,1152,128]{2,1,0:T(8,128)(2,1)S(1)} all-gather(bf16[1,1152,128]{2,1,0:T(8,128)(2,1)S(1)} %all_gather_reshape.3), channel_id=1, replica_groups=mesh['ylo'=2,'x'=4,'z'=8,'core'=2,'chan'=4] {'core'}, dimensions={0}, use_global_device_ids=true | all-gather | bytes 884736 | tf_op jit(solution)/shard_map/all_gather | solution.py:492
  133.3 1.1 slice_multiply_fusion
  (53 shorter events, 1.9 us)
Async XLA Ops:
  7.2 11.8 %copy-start.11 = (s32[384,4,3]{0,1,2:T(4,128)S(1)}, s32[384,4,3]{0,1,2:T(4,128)}, u32[]{:S(2)}) copy-start(s32[384,4,3]{0,1,2:T(4,128)} %param.15) | copy-start | bytes 55300
  7.2 67.5 %all-gather.5.cloned.1.call-start = ((), (), s32[]{:S(2)}) async-start(), calls=%async_computation.6 | async-start | bytes 2654208 | tf_op jit(solution)/shard_map/all_gather | solution.py:449
  7.3 1.0 copy-start.1
  8.3 1.0 copy-start.2
  9.2 0.9 copy-start.4
  10.1 0.8 copy-start.8
  13.1 12.5 %all-to-all-start = ((bf16[8,192,128]{2,1,0:T(8,128)(2,1)}), bf16[8,192,128]{2,1,0:T(8,128)(2,1)S(1)}, u32[]{:S(2)}, u32[]{:S(2)}) async-start(bf16[8,192,128]{2,1,0:T(8,128)(2,1)} %get-tuple-element.10), calls=%async_computation | async-start | bytes 786432 | tf_op jit(solution)/shard_map/all_to_all | solution.py:450
  25.6 17.9 %copy-start.12 = (bf16[32,240]{1,0:T(8,128)(2,1)S(1)}, bf16[32,240]{1,0:T(8,128)(2,1)}, u32[]{:S(2)}) copy-start(bf16[32,240]{1,0:T(8,128)(2,1)} %constant.128.clone) | copy-start | bytes 46084
  35.6 27.8 %copy-start.10 = (bf16[32,1728]{1,0:T(8,128)(2,1)S(1)}, bf16[32,1728]{1,0:T(8,128)(2,1)}, u32[]{:S(2)}) copy-start(bf16[32,1728]{1,0:T(8,128)(2,1)} %constant.126.clone) | copy-start | bytes 331780
  35.6 27.8 %copy-start.13 = (f32[1728]{0:T(1024)S(1)}, f32[1728]{0:T(1024)}, u32[]{:S(2)}) copy-start(f32[1728]{0:T(1024)} %constant.127.clone) | copy-start | bytes 20740
  35.6 21.5 %all-to-all-start.1 = ((bf16[8,160,128]{2,1,0:T(8,128)(2,1)}), bf16[8,160,128]{2,1,0:T(8,128)(2,1)S(1)}, u32[]{:S(2)}, u32[]{:S(2)}) async-start(bf16[8,160,128]{2,1,0:T(8,128)(2,1)} %place.1), calls=%async_computation.1 | async-start | bytes 655360 | tf_op jit(solution)/shard_map/all_to_all | solution.py:462
  57.9 16.8 %all-to-all-start.2 = ((bf16[4,432,128]{2,1,0:T(8,128)(2,1)}), bf16[4,432,128]{2,1,0:T(8,128)(2,1)S(1)}, u32[]{:S(2)}, u32[]{:S(2)}) async-start(bf16[4,432,128]{2,1,0:T(8,128)(2,1)} %join.1), calls=%async_computation.2 | async-start | bytes 884736 | tf_op jit(solution)/shard_map/all_to_all | solution.py:472
  63.5 11.2 %copy-start.3 = (bf16[432,192]{1,0:T(8,128)(2,1)S(1)}, bf16[432,192]{1,0:T(8,128)(2,1)}, u32[]{:S(2)}) copy-start(bf16[432,192]{1,0:T(8,128)(2,1)} %constant.131.clone.down_ref) | copy-start | bytes 497668
  63.5 11.2 %copy-start.5 = (bf16[160,144]{1,0:T(8,128)(2,1)S(1)}, bf16[160,144]{1,0:T(8,128)(2,1)}, u32[]{:S(2)}) copy-start(bf16[160,144]{1,0:T(8,128)(2,1)} %constant.134.clone.cell_ref) | copy-start | bytes 138244
  63.6 11.2 %copy-start.6 = (bf16[160,48]{1,0:T(8,128)(2,1)S(1)}, bf16[160,48]{1,0:T(8,128)(2,1)}, u32[]{:S(2)}) copy-start(bf16[160,48]{1,0:T(8,128)(2,1)} %constant.132.clone.rim_ref) | copy-start | bytes 46084
  63.6 11.2 %copy-start.7 = (bf16[160,64]{1,0:T(8,128)(2,1)S(1)}, bf16[160,64]{1,0:T(8,128)(2,1)}, u32[]{:S(2)}) copy-start(bf16[160,64]{1,0:T(8,128)(2,1)} %constant.130.clone.shift_ref) | copy-start | bytes 61444
  63.6 11.2 %copy-start.9 = (bf16[48,64]{1,0:T(8,128)(2,1)S(1)}, bf16[48,64]{1,0:T(8,128)(2,1)}, u32[]{:S(2)}) copy-start(bf16[48,64]{1,0:T(8,128)(2,1)} %constant.133.clone.order_ref) | copy-start | bytes 18436
  74.7 1.7 %copy-start = (bf16[72,64,256]{2,1,0:T(8,128)(2,1)S(1)}, bf16[72,64,256]{2,1,0:T(8,128)(2,1)}, u32[]{:S(2)}) copy-start(bf16[72,64,256]{2,1,0:T(8,128)(2,1)} %all-gather.5.cloned.1.call-done) | copy-start | bytes 7077892
Sparse Core Ops, SparseCore 0:
  13.2 46.5 all-gather.4

commit v5 on v4

--- a/solution.py
+++ b/solution.py
@@ -198,7 +198,7 @@
     return fields, jnp.where(at == cell, 1.0, 0.0).astype(BF)
 
 
-def pack_kernel(me_ref, fields_hbm, cot_hbm, first_ref, down_ref, own_ref, unit_ref, half_ref, fields_ref, cot_ref, sems):
+def pack_kernel(me_ref, fields_hbm, cot_hbm, first_ref, down_ref, own_ref, unit_ref, half_ref, fields_ref, cot_ref, held, sems):
     loads = [
         pltpu.make_async_copy(fields_hbm, fields_ref, sems.at[0]),
         pltpu.make_async_copy(cot_hbm, cot_ref, sems.at[1]),
@@ -208,13 +208,16 @@
 
     @pl.when(me_ref[3] == 0)
     def _():
-        pltpu.make_async_copy(first_ref, half_ref, sems.at[2]).start()
+        pltpu.make_async_copy(first_ref, held, sems.at[2]).start()
 
     @pl.when(me_ref[3] == 1)
     def _():
-        pltpu.make_async_copy(down_ref, half_ref, sems.at[2]).start()
+        pltpu.make_async_copy(down_ref, held, sems.at[2]).start()
 
     chosen = [pack_selectors(h) for h in range(2)]
+    pltpu.make_async_copy(first_ref, held, sems.at[2]).wait()
+    store = pltpu.make_async_copy(held, half_ref, sems.at[3])
+    store.start()
     for load in loads:
         load.wait()
     for t in range(TILES_HERE):
@@ -223,7 +226,7 @@
             own_ref[t, :, h * CH : (h + 1) * CH] = halves[h][:PACK_ROWS]
             for copy in range(YX):
                 unit_ref[copy, t * 4 * UNIT : (t + 1) * 4 * UNIT, h * CH : (h + 1) * CH] = halves[h][PACK_ROWS:]
-    pltpu.make_async_copy(first_ref, half_ref, sems.at[2]).wait()
+    store.wait()
 
 
 def edge_words(seam_table):
@@ -288,9 +291,14 @@
 
 
 def main_kernel(
-    me_ref, pay_ref, window_ref, rim_at_ref, shift_ref, down_ref, rim_ref, order_ref, cell_ref, weights_ref,
-    coarse_ref, gp_ref, grads_ref, xs, cs, wf, wd, wins, ups, rims, downs, sems,
+    me_ref, pay_ref, rim_at_ref, shift_ref, down_ref, rim_ref, order_ref, cell_ref, window_hbm, weights_ref,
+    coarse_ref, gp_ref, grads_ref, window_ref, xs, cs, wf, wd, wins, ups, rims, downs, sems,
 ):
+    window_copies = [
+        pltpu.make_async_copy(window_hbm.at[t], window_ref.at[t], sems.at[2 * CHAN + t]) for t in range(TILES_HERE)
+    ]
+    for copy in window_copies:
+        copy.start()
     copies = []
     for c in range(CHAN):
         for which, held in enumerate((wf, wd)):
@@ -317,6 +325,7 @@
     for t in range(TILES_HERE):
         xs[t, 2 * X_HALF :, :] = jnp.zeros((C - 2 * X_HALF, C), BF)
     for t in range(TILES_HERE):
+        window_copies[t].wait()
         for k in range(9):
             wins[t * PRE_ROWS : (t + 1) * PRE_ROWS, k * C : (k + 1) * C] = dot_nn(
                 window_ref[t, k * PRE_ROWS : (k + 1) * PRE_ROWS, :], xs[t]
@@ -397,6 +406,8 @@
 
 
 LIMIT = pltpu.CompilerParams(vmem_limit_bytes=48 * 1024 * 1024)
+WHOLE = pltpu.CompilerParams(vmem_limit_bytes=60 * 1024 * 1024)
+MOST = pltpu.CompilerParams(vmem_limit_bytes=52 * 1024 * 1024)
 
 
 def tiles_call(me, payload, window, rim_at, weights):
@@ -408,9 +419,10 @@
             jax.ShapeDtypeStruct((TILES_HERE, CH, CELLS), BF),
             jax.ShapeDtypeStruct((CORE, 18 * CH, 128), BF),
         ),
-        in_specs=smem(1) + vmem(8) + hbm(1),
+        in_specs=smem(1) + vmem(7) + hbm(2),
         out_specs=tuple(vmem(3)),
         scratch_shapes=[
+            pltpu.VMEM((TILES_HERE, 9 * PRE_ROWS, C), BF),
             pltpu.VMEM((TILES_HERE, C, C), BF),
             pltpu.VMEM((TILES_HERE, 2 * C_HALF, C), BF),
             pltpu.VMEM((9, C, C), BF),
@@ -419,11 +431,11 @@
             pltpu.VMEM((4, TILES_HERE * PART, C), F32),
             pltpu.VMEM((len(RIM_TAPS), TILES_HERE * RIM_ROWS, C), BF),
             pltpu.VMEM((TILES_HERE * DOWN_ROWS, 9 * C), BF),
-            pltpu.SemaphoreType.DMA((2 * CHAN,)),
+            pltpu.SemaphoreType.DMA((2 * CHAN + TILES_HERE,)),
         ],
-        compiler_params=LIMIT,
+        compiler_params=MOST,
         name="tiles",
-    )(me, payload, window, rim_at, *(jnp.asarray(array, BF) for array in constants), weights)
+    )(me, payload, rim_at, *(jnp.asarray(array, BF) for array in constants), window, weights)
 
 
 def shards(fields, seam_table, w_first, w_down, cotangent):
@@ -441,9 +453,10 @@
         scratch_shapes=[
             pltpu.VMEM((TILES_HERE, CH, CELLS), BF),
             pltpu.VMEM((TILES_HERE, COARSE, CH), BF),
-            pltpu.SemaphoreType.DMA((3,)),
+            pltpu.VMEM((9, CH, C), BF),
+            pltpu.SemaphoreType.DMA((4,)),
         ],
-        compiler_params=LIMIT,
+        compiler_params=WHOLE,
         name="pack",
     )(me, fields, jnp.swapaxes(cotangent, 1, 2), w_first, w_down)
     weights = lax.all_gather(half, ("chan", "core"), axis=0, tiled=False)

time: 142 us -> 138 us (0.972)
  local copies, waits for them, and re-layouts: 7.65 us -> 3.03 us
    unnamed x28 -> x22, local copies, waits for them, and re-layouts: 5.28 us -> 0.06 us
where the time goes in v5:
time: 138 us
  blocking collectives  55.4 us (40%)
  waiting for transfers between devices  26.8 us (19%)
  starting transfers between devices  19.3 us (14%)
  Pallas kernels  15.2 us (11%)
  between operations  14.3 us (10%)
  other arithmetic  3.61 us (3%)
  local copies, waits for them, and re-layouts  3.03 us (2%)
    all_to_all x1, blocking collectives, shards(): lax.all_to_all(jnp.broadcast_to(part[None], (NX * NZ, 36, 128)), ('x', 'z...  16.9 us
    all_to_all x1, blocking collectives, shards(): part = lax.all_to_all(part, ('x', 'z'), 0, 0)  13.9 us
    all_to_all x1, waiting for transfers between devices, shards(): got = lax.all_to_all(sends, 'z', 0, 0)  13.3 us
    all_to_all x1, waiting for transfers between devices, shards(): payload = lax.all_to_all(joined, 'chan', 0, 0)  9.18 us
    pallas_call x1, Pallas kernels, tiles_call(): pl.pallas_call(main_kernel, out_shape=(jax.ShapeDtypeStruct((TILES_HERE,...  8.8 us
    all_to_all x1, starting transfers between devices, shards(): got = lax.all_to_all(sends, 'z', 0, 0)  7.85 us
    all_gather x1, blocking collectives, shards(): units = lax.all_gather(units, 'core', axis=0, tiled=True)  7.66 us
    all_to_all x1, blocking collectives, shards(): part = lax.all_to_all(grads, 'core', 0, 0)  7.48 us
  transfers between devices with their start and end apart: 4, of which 3 were waited for; matrix products, arithmetic and copies ran while one was open for 3% of the time, Pallas kernels for 2%

profile of v5, /device:TPU:1, one launch (start us, length us, event | category | flops | bytes accessed | tf_op | source)
XLA Modules:
  0.0 137.8 jit_solution(7943583440800342370)
XLA Ops:
  7.2 0.7 stack.23.me_ref
  7.9 3.2 %pack.1 = (bf16[3,96,128]{2,1,0:T(8,128)(2,1)}, bf16[8,192,128]{2,1,0:T(8,128)(2,1)}, bf16[9,64,256]{2,1,0:T(8,128)(2,1)}) custom-call(s32[5]{0:T(128)} %stack.23.me_ref, bf16[3,64,144]{2,1,0:T(8,128)(2,1)} %fields_hbm.1, bf16[3,36,64]{2,1,0:T(8,128)(2,1)} %bitcast.40, bf16[9,64,256]{2,1,0:T(8,128)(2,1)} %first_ref.1, bf16[9,64,256]{2,1,0:T(8,128)(2,1)} %down_ref.2), custom_call_target="tpu_custom_call" | custom-call | tf_op jit(solution)/shard_map/pack/pallas_call | solution.py:444
  11.2 5.9 %all-to-all-start = ((bf16[8,192,128]{2,1,0:T(8,128)(2,1)}), bf16[8,192,128]{2,1,0:T(8,128)(2,1)S(1)}, u32[]{:S(2)}, u32[]{:S(2)}) async-start(bf16[8,192,128]{2,1,0:T(8,128)(2,1)} %get-tuple-element.10), calls=%async_computation | async-start | bytes 786432 | tf_op jit(solution)/shard_map/all_to_all | solution.py:463
  17.5 0.2 copy.26
  17.7 0.2 ne.70
  17.9 0.1 copy.31
  18.0 0.1 mul.88
  18.2 0.1 copy.28
  18.3 0.1 div.31
  18.5 0.1 copy.27
  18.6 0.1 rem.82
  18.7 0.1 copy.29
  18.9 0.1 squeeze.6
  19.0 0.1 copy.30
  19.2 0.1 mul.84
  19.4 4.3 %all-to-all-done = bf16[8,192,128]{2,1,0:T(8,128)(2,1)S(1)} async-done(((bf16[8,192,128]{2,1,0:T(8,128)(2,1)}), bf16[8,192,128]{2,1,0:T(8,128)(2,1)S(1)}, u32[]{:S(2)}, u32[]{:S(2)}) %all-to-all-start) | async-done | bytes 393248 | tf_op jit(solution)/shard_map/all_to_all | solution.py:463
  23.7 7.7 %all_gather.18.unit_ref = bf16[3072,128]{1,0:T(8,128)(2,1)S(1)} all-gather(bf16[1536,128]{1,0:T(8,128)(2,1)S(1)} %bitcast.36), channel_id=1, replica_groups=mesh['ylo'=2,'x'=4,'z'=8,'core'=2,'chan'=4] {'core'}, dimensions={0}, use_global_device_ids=true | all-gather | bytes 1179648 | tf_op jit(solution)/shard_map/all_gather | solution.py:464
  31.3 2.3 %place.1 = bf16[8,160,128]{2,1,0:T(8,128)(2,1)} custom-call(s32[1536]{0:T(1024)S(1)} %get-tuple-element.26.word_ref, s32[1536]{0:T(1024)S(1)} %get-tuple-element.25.beyond_ref, s32[5]{0:T(128)S(1)} %copy-done.6, bf16[3072,128]{1,0:T(8,128)(2,1)S(1)} %all_gather.18.unit_ref), custom_call_target="tpu_custom_call" | custom-call | tf_op jit(solution)/shard_map/place/pallas_call | solution.py:466
  33.6 7.8 %all-to-all-start.1 = ((bf16[8,160,128]{2,1,0:T(8,128)(2,1)}), bf16[8,160,128]{2,1,0:T(8,128)(2,1)S(1)}, u32[]{:S(2)}, u32[]{:S(2)}) async-start(bf16[8,160,128]{2,1,0:T(8,128)(2,1)} %place.1), calls=%async_computation.1 | async-start | bytes 655360 | tf_op jit(solution)/shard_map/all_to_all | solution.py:475
  41.6 0.2 compare_convert_fusion.1.rim_at_ref
  41.8 13.3 %all-to-all-done.1.got_ref = bf16[8,160,128]{2,1,0:T(8,128)(2,1)S(1)} async-done(((bf16[8,160,128]{2,1,0:T(8,128)(2,1)}), bf16[8,160,128]{2,1,0:T(8,128)(2,1)S(1)}, u32[]{:S(2)}, u32[]{:S(2)}) %all-to-all-start.1) | async-done | bytes 327712 | tf_op jit(solution)/shard_map/all_to_all | solution.py:475
  55.1 0.8 join.1
  55.9 5.5 %all-to-all-start.2 = ((bf16[4,432,128]{2,1,0:T(8,128)(2,1)}), bf16[4,432,128]{2,1,0:T(8,128)(2,1)S(1)}, u32[]{:S(2)}, u32[]{:S(2)}) async-start(bf16[4,432,128]{2,1,0:T(8,128)(2,1)} %join.1), calls=%async_computation.2 | async-start | bytes 884736 | tf_op jit(solution)/shard_map/all_to_all | solution.py:485
  61.7 1.9 %compare_convert_fusion.window_hbm = bf16[3,1728,256]{2,1,0:T(8,128)(2,1)} fusion(f32[256]{0:T(256)S(1)} %add_convert_fusion.2, f32[3,1728]{1,0:T(4,128)S(1)} %convolution_add_fusion), kind=kLoop, calls=%fused_computation | loop fusion | flops 2654208 | bytes 2675968 | tf_op jit(solution)/shard_map/convert_element_type | solution.py:494
  63.6 9.2 %all-to-all-done.2.pay_ref = bf16[4,432,128]{2,1,0:T(8,128)(2,1)S(1)} async-done(((bf16[4,432,128]{2,1,0:T(8,128)(2,1)}), bf16[4,432,128]{2,1,0:T(8,128)(2,1)S(1)}, u32[]{:S(2)}, u32[]{:S(2)}) %all-to-all-start.2) | async-done | bytes 442400 | tf_op jit(solution)/shard_map/all_to_all | solution.py:485
  72.8 8.8 %tiles.1 = (bf16[3,36,64]{2,1,0:T(8,128)(2,1)}, bf16[3,64,144]{2,1,0:T(8,128)(2,1)}, bf16[2,1152,128]{2,1,0:T(8,128)(2,1)S(1)}) custom-call(s32[5]{0:T(128)S(1)} %copy-done.6, bf16[4,432,128]{2,1,0:T(8,128)(2,1)S(1)} %all-to-all-done.2.pay_ref, bf16[3,240,64]{2,1,0:T(8,128)(2,1)S(1)} %compare_convert_fusion.1.rim_at_ref, bf16[160,64]{1,0:T(8,128)(2,1)S(1)} %copy-done.4, ...), custom_call_target="tpu_custom_call" | custom-call | tf_op jit(solution)/shard_map/tiles/pallas_call | solution.py:415
  81.6 7.5 %all_to_all.30 = bf16[2,1152,128]{2,1,0:T(8,128)(2,1)S(1)} all-to-all(bf16[2,1152,128]{2,1,0:T(8,128)(2,1)S(1)} %get-tuple-element.14), channel_id=1, replica_groups=mesh['ylo'=2,'x'=4,'z'=8,'core'=2,'chan'=4] {'core'}, dimensions={0} | all-to-all | bytes 1179648 | tf_op jit(solution)/shard_map/all_to_all | solution.py:498
  89.2 13.9 %all_to_all.31 = bf16[32,36,128]{2,1,0:T(8,128)(2,1)S(1)} all-to-all(bf16[32,36,128]{2,1,0:T(8,128)(2,1)S(1)} %convert_element_type.62), channel_id=1, replica_groups=mesh['ylo'=2,'x'=4,'z'=8,'core'=2,'chan'=4] {'x','z'}, dimensions={0} | all-to-all | bytes 589824 | tf_op jit(solution)/shard_map/all_to_all | solution.py:500
  103.2 3.3 %all-gather.2 = bf16[2,36,128]{2,1,0:T(8,128)(2,1)S(1)} all-gather(bf16[1,36,128]{2,1,0:T(8,128)(2,1)S(1)} %bitcast.39), channel_id=3, replica_groups=mesh['ylo'=2,'x'=4,'z'=8,'core'=2,'chan'=4] {'ylo'}, dimensions={0}, use_global_device_ids=true | all-gather | bytes 27648 | tf_op jit(solution)/shard_map/all_gather | solution.py:502
  106.5 16.9 %all_to_all.32 = bf16[32,36,128]{2,1,0:T(8,128)(2,1)S(1)} all-to-all(bf16[32,36,128]{2,1,0:T(8,128)(2,1)S(1)} %broadcast_in_dim.9), channel_id=1, replica_groups=mesh['ylo'=2,'x'=4,'z'=8,'core'=2,'chan'=4] {'x','z'}, dimensions={0} | all-to-all | bytes 589824 | tf_op jit(solution)/shard_map/all_to_all | solution.py:504
  123.4 6.2 %all_gather.23 = bf16[2,1152,128]{2,1,0:T(8,128)(2,1)S(1)} all-gather(bf16[1,1152,128]{2,1,0:T(8,128)(2,1)S(1)} %all_gather_reshape.3), channel_id=1, replica_groups=mesh['ylo'=2,'x'=4,'z'=8,'core'=2,'chan'=4] {'core'}, dimensions={0}, use_global_device_ids=true | all-gather | bytes 884736 | tf_op jit(solution)/shard_map/all_gather | solution.py:505
  129.8 1.1 slice_multiply_fusion
  (47 shorter events, 1.3 us)
Async XLA Ops:
  7.2 9.9 %copy-start.8 = (s32[384,4,3]{0,1,2:T(4,128)S(1)}, s32[384,4,3]{0,1,2:T(4,128)}, u32[]{:S(2)}) copy-start(s32[384,4,3]{0,1,2:T(4,128)} %param.15) | copy-start | bytes 55300
  7.2 65.6 %all-gather.5.cloned.1.call-start = ((), (), s32[]{:S(2)}) async-start(), calls=%async_computation.6 | async-start | bytes 2654208 | tf_op jit(solution)/shard_map/all_gather | solution.py:462
  11.2 12.5 %all-to-all-start = ((bf16[8,192,128]{2,1,0:T(8,128)(2,1)}), bf16[8,192,128]{2,1,0:T(8,128)(2,1)S(1)}, u32[]{:S(2)}, u32[]{:S(2)}) async-start(bf16[8,192,128]{2,1,0:T(8,128)(2,1)} %get-tuple-element.10), calls=%async_computation | async-start | bytes 786432 | tf_op jit(solution)/shard_map/all_to_all | solution.py:463
  18.3 13.0 %copy-start.6 = (s32[5]{0:T(128)S(1)}, s32[5]{0:T(128)}, u32[]{:S(2)}) copy-start(s32[5]{0:T(128)} %stack.23.me_ref) | copy-start | bytes 64
  23.6 17.9 %copy-start.9 = (bf16[32,240]{1,0:T(8,128)(2,1)S(1)}, bf16[32,240]{1,0:T(8,128)(2,1)}, u32[]{:S(2)}) copy-start(bf16[32,240]{1,0:T(8,128)(2,1)} %constant.128.clone) | copy-start | bytes 46084
  23.7 31.5 %copy-start.2 = (bf16[3,96,128]{2,1,0:T(8,128)(2,1)S(1)}, bf16[3,96,128]{2,1,0:T(8,128)(2,1)}, u32[]{:S(2)}) copy-start(bf16[3,96,128]{2,1,0:T(8,128)(2,1)} %get-tuple-element.11.own_ref) | copy-start | bytes 221188
  33.6 27.8 %copy-start.7 = (bf16[32,1728]{1,0:T(8,128)(2,1)S(1)}, bf16[32,1728]{1,0:T(8,128)(2,1)}, u32[]{:S(2)}) copy-start(bf16[32,1728]{1,0:T(8,128)(2,1)} %constant.126.clone) | copy-start | bytes 331780
  33.6 27.8 %copy-start.10 = (f32[1728]{0:T(1024)S(1)}, f32[1728]{0:T(1024)}, u32[]{:S(2)}) copy-start(f32[1728]{0:T(1024)} %constant.127.clone) | copy-start | bytes 20740
  33.6 21.5 %all-to-all-start.1 = ((bf16[8,160,128]{2,1,0:T(8,128)(2,1)}), bf16[8,160,128]{2,1,0:T(8,128)(2,1)S(1)}, u32[]{:S(2)}, u32[]{:S(2)}) async-start(bf16[8,160,128]{2,1,0:T(8,128)(2,1)} %place.1), calls=%async_computation.1 | async-start | bytes 655360 | tf_op jit(solution)/shard_map/all_to_all | solution.py:475
  55.9 16.8 %all-to-all-start.2 = ((bf16[4,432,128]{2,1,0:T(8,128)(2,1)}), bf16[4,432,128]{2,1,0:T(8,128)(2,1)S(1)}, u32[]{:S(2)}, u32[]{:S(2)}) async-start(bf16[4,432,128]{2,1,0:T(8,128)(2,1)} %join.1), calls=%async_computation.2 | async-start | bytes 884736 | tf_op jit(solution)/shard_map/all_to_all | solution.py:485
  61.6 11.2 %copy-start = (bf16[432,192]{1,0:T(8,128)(2,1)S(1)}, bf16[432,192]{1,0:T(8,128)(2,1)}, u32[]{:S(2)}) copy-start(bf16[432,192]{1,0:T(8,128)(2,1)} %constant.131.clone.down_ref) | copy-start | bytes 497668
  61.6 11.2 %copy-start.1 = (bf16[160,144]{1,0:T(8,128)(2,1)S(1)}, bf16[160,144]{1,0:T(8,128)(2,1)}, u32[]{:S(2)}) copy-start(bf16[160,144]{1,0:T(8,128)(2,1)} %constant.134.clone.cell_ref) | copy-start | bytes 138244
  61.6 11.2 %copy-start.3 = (bf16[160,48]{1,0:T(8,128)(2,1)S(1)}, bf16[160,48]{1,0:T(8,128)(2,1)}, u32[]{:S(2)}) copy-start(bf16[160,48]{1,0:T(8,128)(2,1)} %constant.132.clone.rim_ref) | copy-start | bytes 46084
  61.6 11.2 %copy-start.4 = (bf16[160,64]{1,0:T(8,128)(2,1)S(1)}, bf16[160,64]{1,0:T(8,128)(2,1)}, u32[]{:S(2)}) copy-start(bf16[160,64]{1,0:T(8,128)(2,1)} %constant.130.clone.shift_ref) | copy-start | bytes 61444
  61.6 11.2 %copy-start.5 = (bf16[48,64]{1,0:T(8,128)(2,1)S(1)}, bf16[48,64]{1,0:T(8,128)(2,1)}, u32[]{:S(2)}) copy-start(bf16[48,64]{1,0:T(8,128)(2,1)} %constant.133.clone.order_ref) | copy-start | bytes 18436
Sparse Core Ops, SparseCore 0:
  11.3 46.5 all-gather.4

commit v6 on v5

--- a/solution.py
+++ b/solution.py
@@ -198,35 +198,39 @@
     return fields, jnp.where(at == cell, 1.0, 0.0).astype(BF)
 
 
-def pack_kernel(me_ref, fields_hbm, cot_hbm, first_ref, down_ref, own_ref, unit_ref, half_ref, fields_ref, cot_ref, held, sems):
+def pack_kernel(fields_hbm, cot_hbm, first_ref, down_ref, own_ref, unit_hbm, half_ref, fields_ref, cot_ref, held, unit_ref, sems):
     loads = [
         pltpu.make_async_copy(fields_hbm, fields_ref, sems.at[0]),
         pltpu.make_async_copy(cot_hbm, cot_ref, sems.at[1]),
     ]
     for load in loads:
         load.start()
-
-    @pl.when(me_ref[3] == 0)
+    core = lax.axis_index("core")
+
+    @pl.when(core == 0)
     def _():
         pltpu.make_async_copy(first_ref, held, sems.at[2]).start()
 
-    @pl.when(me_ref[3] == 1)
+    @pl.when(core == 1)
     def _():
         pltpu.make_async_copy(down_ref, held, sems.at[2]).start()
 
     chosen = [pack_selectors(h) for h in range(2)]
-    pltpu.make_async_copy(first_ref, held, sems.at[2]).wait()
-    store = pltpu.make_async_copy(held, half_ref, sems.at[3])
-    store.start()
     for load in loads:
         load.wait()
     for t in range(TILES_HERE):
         halves = [(dot_nt(f, fields_ref[t]) + dot_nn(c, cot_ref[t])).astype(BF) for f, c in chosen]
         for h in range(2):
             own_ref[t, :, h * CH : (h + 1) * CH] = halves[h][:PACK_ROWS]
-            for copy in range(YX):
-                unit_ref[copy, t * 4 * UNIT : (t + 1) * 4 * UNIT, h * CH : (h + 1) * CH] = halves[h][PACK_ROWS:]
-    store.wait()
+            unit_ref[t * 4 * UNIT : (t + 1) * 4 * UNIT, h * CH : (h + 1) * CH] = halves[h][PACK_ROWS:]
+    pltpu.make_async_copy(first_ref, held, sems.at[2]).wait()
+    stores = [pltpu.make_async_copy(held, half_ref, sems.at[3])]
+    for copy in range(YX):
+        stores.append(pltpu.make_async_copy(unit_ref, unit_hbm.at[copy], sems.at[4 + copy]))
+    for store in stores:
+        store.start()
+    for store in stores:
+        store.wait()
 
 
 def edge_words(seam_table):
@@ -240,8 +244,8 @@
     return word.reshape(-1), beyond.reshape(-1)
 
 
-def place_kernel(word_ref, beyond_ref, me_ref, unit_ref, out_ref, sent):
-    ylo, x, z, core = me_ref[0], me_ref[1], me_ref[2], me_ref[3]
+def place_kernel(word_ref, beyond_ref, unit_ref, out_ref, sent):
+    ylo, x, z, core = (lax.axis_index(axis) for axis in TILE_AXES)
 
     def unit_at(word):
         keep = jnp.where((word >> 9) == z, 1.0, 0.0).astype(F32)
@@ -291,7 +295,7 @@
 
 
 def main_kernel(
-    me_ref, pay_ref, rim_at_ref, shift_ref, down_ref, rim_ref, order_ref, cell_ref, window_hbm, weights_ref,
+    pay_ref, rim_at_ref, shift_ref, down_ref, rim_ref, order_ref, cell_ref, window_hbm, weights_ref,
     coarse_ref, gp_ref, grads_ref, window_ref, xs, cs, wf, wd, wins, ups, rims, downs, sems,
 ):
     window_copies = [
@@ -309,7 +313,7 @@
             )
     for copy in copies:
         copy.start()
-    chan = me_ref[4]
+    chan = lax.axis_index("chan")
     pick = jnp.where(
         lax.broadcasted_iota(jnp.int32, (CH, C), 1) == lax.broadcasted_iota(jnp.int32, (CH, C), 0) + chan * CH, 1.0, 0.0
     ).astype(BF)
@@ -410,7 +414,7 @@
 MOST = pltpu.CompilerParams(vmem_limit_bytes=52 * 1024 * 1024)
 
 
-def tiles_call(me, payload, window, rim_at, weights):
+def tiles_call(payload, window, rim_at, weights):
     constants = (shift_selector(), down_selector(), rim_selector(), order_selector(), cell_selector())
     return pl.pallas_call(
         main_kernel,
@@ -419,7 +423,7 @@
             jax.ShapeDtypeStruct((TILES_HERE, CH, CELLS), BF),
             jax.ShapeDtypeStruct((CORE, 18 * CH, 128), BF),
         ),
-        in_specs=smem(1) + vmem(7) + hbm(2),
+        in_specs=vmem(7) + hbm(2),
         out_specs=tuple(vmem(3)),
         scratch_shapes=[
             pltpu.VMEM((TILES_HERE, 9 * PRE_ROWS, C), BF),
@@ -435,12 +439,11 @@
         ],
         compiler_params=MOST,
         name="tiles",
-    )(me, payload, rim_at, *(jnp.asarray(array, BF) for array in constants), window, weights)
+    )(payload, rim_at, *(jnp.asarray(array, BF) for array in constants), window, weights)
 
 
 def shards(fields, seam_table, w_first, w_down, cotangent):
-    coords = [lax.axis_index(axis) for axis in ("ylo", "x", "z", "core", "chan")]
-    me = jnp.stack(coords).astype(jnp.int32)
+    coords = [lax.axis_index(axis) for axis in ("ylo", "x", "z", "core")]
     own, units, half = pl.pallas_call(
         pack_kernel,
         out_shape=(
@@ -448,17 +451,18 @@
             jax.ShapeDtypeStruct((YX, TILES_HERE * 4 * UNIT, 128), BF),
             jax.ShapeDtypeStruct(w_first.shape, BF),
         ),
-        in_specs=smem(1) + hbm(4),
-        out_specs=tuple(vmem(2) + hbm(1)),
+        in_specs=hbm(4),
+        out_specs=tuple(vmem(1) + hbm(2)),
         scratch_shapes=[
             pltpu.VMEM((TILES_HERE, CH, CELLS), BF),
             pltpu.VMEM((TILES_HERE, COARSE, CH), BF),
             pltpu.VMEM((9, CH, C), BF),
-            pltpu.SemaphoreType.DMA((4,)),
+            pltpu.VMEM((TILES_HERE * 4 * UNIT, 128), BF),
+            pltpu.SemaphoreType.DMA((4 + YX,)),
         ],
         compiler_params=WHOLE,
         name="pack",
-    )(me, fields, jnp.swapaxes(cotangent, 1, 2), w_first, w_down)
+    )(fields, jnp.swapaxes(cotangent, 1, 2), w_first, w_down)
     weights = lax.all_gather(half, ("chan", "core"), axis=0, tiled=False)
     units = lax.all_to_all(units, ("ylo", "x"), 0, 0).reshape(-1, 128)
     units = lax.all_gather(units, "core", axis=0, tiled=True)
@@ -466,12 +470,12 @@
     sends = pl.pallas_call(
         place_kernel,
         out_shape=jax.ShapeDtypeStruct((NZ, SEND_ROWS, 128), BF),
-        in_specs=smem(3) + vmem(1),
+        in_specs=smem(2) + vmem(1),
         out_specs=vmem(1)[0],
         scratch_shapes=[pltpu.VMEM((NZ, SEND_ROWS, 128), F32)],
         compiler_params=LIMIT,
         name="place",
-    )(words, beyond, me, units)
+    )(words, beyond, units)
     got = lax.all_to_all(sends, "z", 0, 0)
     joined = pl.pallas_call(
         join_kernel,
@@ -493,15 +497,15 @@
         at = jnp.dot(chosen, jnp.asarray(varied, BF), preferred_element_type=F32) + jnp.asarray(fixed, F32)
         one_hots.append((at[:, :, None] == jnp.arange(1, depth + 1, dtype=jnp.int32).astype(F32)).astype(BF))
 
-    coarse, grad_pre, grads = tiles_call(me, payload, one_hots[0], one_hots[1], weights)
+    coarse, grad_pre, grads = tiles_call(payload, one_hots[0], one_hots[1], weights)
 
     part = lax.all_to_all(grads, "core", 0, 0)
-    part = (part[0].astype(F32) + part[1].astype(F32)).astype(BF).reshape(NX * NZ, 36, 128)
-    part = lax.all_to_all(part, ("x", "z"), 0, 0)
+    part = (part[0].astype(F32) + part[1].astype(F32)).astype(BF).reshape(YX, 144, 128)
+    part = lax.all_to_all(part, ("ylo", "x"), 0, 0)
     part = part.astype(F32).sum(0).astype(BF)
-    part = lax.all_gather(part, "ylo", axis=0, tiled=False)
-    part = (part[0].astype(F32) + part[1].astype(F32)).astype(BF)
-    part = lax.all_to_all(jnp.broadcast_to(part[None], (NX * NZ, 36, 128)), ("x", "z"), 0, 0)
+    part = lax.all_to_all(jnp.broadcast_to(part[None], (NZ, 144, 128)), "z", 0, 0)
+    part = part.astype(F32).sum(0).astype(BF)
+    part = lax.all_to_all(jnp.broadcast_to(part[None], (YX, 144, 128)), ("ylo", "x"), 0, 0)
     whole = lax.all_gather(part.reshape(18 * CH, 128), "core", axis=0, tiled=False)
     whole = jnp.concatenate([whole[0], whole[1]], axis=1).astype(F32).reshape(2, 9, CH, C)
     tiles = TILES_HERE * PLANE * CORE

time: 138 us -> 135 us (0.978)
  blocking collectives: 55.4 us -> 53.1 us
    all_gather x1 -> x0, blocking collectives: 3.25 us -> none  [shards(): part = lax.all_gather(part, 'ylo', axis=0, tiled=False)]
    all_to_all x2 -> x3, blocking collectives: 30.7 us -> 33.3 us  [the longest x1 12.8 us: shards(): lax.all_to_all(jnp.broadcast_to(part[None], (NZ, 144, 128)), 'z', 0, 0)]
where the time goes in v6:
time: 135 us
  blocking collectives  53.1 us (39%)
  waiting for transfers between devices  27.7 us (21%)
  starting transfers between devices  19.3 us (14%)
  Pallas kernels  14.3 us (11%)
  between operations  14.3 us (11%)
  other arithmetic  3.62 us (3%)
  local copies, waits for them, and re-layouts  2.26 us (2%)
    all_to_all x1, waiting for transfers between devices, shards(): got = lax.all_to_all(sends, 'z', 0, 0)  13.3 us
    all_to_all x1, blocking collectives, shards(): lax.all_to_all(jnp.broadcast_to(part[None], (NZ, 144, 128)), 'z', 0, 0)  12.8 us
    all_to_all x1, blocking collectives, shards(): part = lax.all_to_all(part, ('ylo', 'x'), 0, 0)  10.7 us
    all_to_all x1, waiting for transfers between devices, shards(): payload = lax.all_to_all(joined, 'chan', 0, 0)  10.1 us
    all_to_all x1, blocking collectives, shards(): lax.all_to_all(jnp.broadcast_to(part[None], (YX, 144, 128)), ('ylo', 'x')...  9.82 us
    pallas_call x1, Pallas kernels, tiles_call(): pl.pallas_call(main_kernel, out_shape=(jax.ShapeDtypeStruct((TILES_HERE,...  8.29 us
    all_gather x1, blocking collectives, shards(): units = lax.all_gather(units, 'core', axis=0, tiled=True)  7.67 us
    all_to_all x1, starting transfers between devices, shards(): got = lax.all_to_all(sends, 'z', 0, 0)  7.49 us
  transfers between devices with their start and end apart: 4, of which 3 were waited for; matrix products, arithmetic and copies ran while one was open for 3% of the time, Pallas kernels for 2%

profile of v6, /device:TPU:1, one launch (start us, length us, event | category | flops | bytes accessed | tf_op | source)
XLA Modules:
  0.0 134.8 jit_solution(5233382895786816424)
XLA Ops:
  7.2 2.9 %pack.1 = (bf16[3,96,128]{2,1,0:T(8,128)(2,1)}, bf16[8,192,128]{2,1,0:T(8,128)(2,1)}, bf16[9,64,256]{2,1,0:T(8,128)(2,1)}) custom-call(bf16[3,64,144]{2,1,0:T(8,128)(2,1)} %fields_hbm.1, bf16[3,36,64]{2,1,0:T(8,128)(2,1)} %bitcast.35, bf16[9,64,256]{2,1,0:T(8,128)(2,1)} %first_ref.1, bf16[9,64,256]{2,1,0:T(8,128)(2,1)} %down_ref.2), custom_call_target="tpu_custom_call" | custom-call | tf_op jit(solution)/shard_map/pack/pallas_call | solution.py:447
  10.1 5.9 %all-to-all-start = ((bf16[8,192,128]{2,1,0:T(8,128)(2,1)}), bf16[8,192,128]{2,1,0:T(8,128)(2,1)S(1)}, u32[]{:S(2)}, u32[]{:S(2)}) async-start(bf16[8,192,128]{2,1,0:T(8,128)(2,1)} %get-tuple-element.10), calls=%async_computation | async-start | bytes 786432 | tf_op jit(solution)/shard_map/all_to_all | solution.py:467
  16.4 0.2 copy.33
  16.6 0.2 ne.70
  16.8 0.1 copy.38
  17.0 0.1 mul.88
  17.1 0.1 copy.35
  17.2 0.1 div.31
  17.4 0.1 copy.34
  17.5 0.1 rem.82
  17.7 0.1 copy.36
  17.8 0.1 squeeze.6
  18.0 0.1 copy.37
  18.1 0.1 mul.84
  18.3 4.3 %all-to-all-done = bf16[8,192,128]{2,1,0:T(8,128)(2,1)S(1)} async-done(((bf16[8,192,128]{2,1,0:T(8,128)(2,1)}), bf16[8,192,128]{2,1,0:T(8,128)(2,1)S(1)}, u32[]{:S(2)}, u32[]{:S(2)}) %all-to-all-start) | async-done | bytes 393248 | tf_op jit(solution)/shard_map/all_to_all | solution.py:467
  22.6 7.7 %all_gather.12.unit_ref = bf16[3072,128]{1,0:T(8,128)(2,1)S(1)} all-gather(bf16[1536,128]{1,0:T(8,128)(2,1)S(1)} %bitcast.30), channel_id=1, replica_groups=mesh['ylo'=2,'x'=4,'z'=8,'core'=2,'chan'=4] {'core'}, dimensions={0}, use_global_device_ids=true | all-gather | bytes 1179648 | tf_op jit(solution)/shard_map/all_gather | solution.py:468
  30.3 2.3 %place.1 = bf16[8,160,128]{2,1,0:T(8,128)(2,1)} custom-call(s32[1536]{0:T(1024)S(1)} %get-tuple-element.26.word_ref, s32[1536]{0:T(1024)S(1)} %get-tuple-element.25.beyond_ref, bf16[3072,128]{1,0:T(8,128)(2,1)S(1)} %all_gather.12.unit_ref), custom_call_target="tpu_custom_call" | custom-call | tf_op jit(solution)/shard_map/place/pallas_call | solution.py:470
  32.6 7.5 %all-to-all-start.1 = ((bf16[8,160,128]{2,1,0:T(8,128)(2,1)}), bf16[8,160,128]{2,1,0:T(8,128)(2,1)S(1)}, u32[]{:S(2)}, u32[]{:S(2)}) async-start(bf16[8,160,128]{2,1,0:T(8,128)(2,1)} %place.1), calls=%async_computation.1 | async-start | bytes 655360 | tf_op jit(solution)/shard_map/all_to_all | solution.py:479
  40.2 0.2 compare_convert_fusion.1.rim_at_ref
  40.4 13.3 %all-to-all-done.1.got_ref = bf16[8,160,128]{2,1,0:T(8,128)(2,1)S(1)} async-done(((bf16[8,160,128]{2,1,0:T(8,128)(2,1)}), bf16[8,160,128]{2,1,0:T(8,128)(2,1)S(1)}, u32[]{:S(2)}, u32[]{:S(2)}) %all-to-all-start.1) | async-done | bytes 327712 | tf_op jit(solution)/shard_map/all_to_all | solution.py:479
  53.7 0.8 join.1
  54.5 5.8 %all-to-all-start.2 = ((bf16[4,432,128]{2,1,0:T(8,128)(2,1)}), bf16[4,432,128]{2,1,0:T(8,128)(2,1)S(1)}, u32[]{:S(2)}, u32[]{:S(2)}) async-start(bf16[4,432,128]{2,1,0:T(8,128)(2,1)} %join.1), calls=%async_computation.2 | async-start | bytes 884736 | tf_op jit(solution)/shard_map/all_to_all | solution.py:489
  60.4 0.1 convolution_add_fusion
  60.6 1.9 %compare_convert_fusion.window_hbm = bf16[3,1728,256]{2,1,0:T(8,128)(2,1)} fusion(f32[256]{0:T(256)S(1)} %add_convert_fusion.1, f32[3,1728]{1,0:T(4,128)S(1)} %convolution_add_fusion), kind=kLoop, calls=%fused_computation | loop fusion | flops 2654208 | bytes 2675968 | tf_op jit(solution)/shard_map/convert_element_type | solution.py:498
  62.5 10.1 %all-to-all-done.2.pay_ref = bf16[4,432,128]{2,1,0:T(8,128)(2,1)S(1)} async-done(((bf16[4,432,128]{2,1,0:T(8,128)(2,1)}), bf16[4,432,128]{2,1,0:T(8,128)(2,1)S(1)}, u32[]{:S(2)}, u32[]{:S(2)}) %all-to-all-start.2) | async-done | bytes 442400 | tf_op jit(solution)/shard_map/all_to_all | solution.py:489
  72.7 8.3 %tiles.1 = (bf16[3,36,64]{2,1,0:T(8,128)(2,1)}, bf16[3,64,144]{2,1,0:T(8,128)(2,1)}, bf16[2,1152,128]{2,1,0:T(8,128)(2,1)S(1)}) custom-call(bf16[4,432,128]{2,1,0:T(8,128)(2,1)S(1)} %all-to-all-done.2.pay_ref, bf16[3,240,64]{2,1,0:T(8,128)(2,1)S(1)} %compare_convert_fusion.1.rim_at_ref, bf16[160,64]{1,0:T(8,128)(2,1)S(1)} %copy-done.4, ...), custom_call_target="tpu_custom_call" | custom-call | tf_op jit(solution)/shard_map/tiles/pallas_call | solution.py:419
  81.0 6.3 %all_to_all.35 = bf16[2,1152,128]{2,1,0:T(8,128)(2,1)S(1)} all-to-all(bf16[2,1152,128]{2,1,0:T(8,128)(2,1)S(1)} %get-tuple-element.14), channel_id=1, replica_groups=mesh['ylo'=2,'x'=4,'z'=8,'core'=2,'chan'=4] {'core'}, dimensions={0} | all-to-all | bytes 1179648 | tf_op jit(solution)/shard_map/all_to_all | solution.py:502
  87.4 10.7 %all_to_all.36 = bf16[8,144,128]{2,1,0:T(8,128)(2,1)S(1)} all-to-all(bf16[8,144,128]{2,1,0:T(8,128)(2,1)S(1)} %bitcast.31), channel_id=1, replica_groups=mesh['ylo'=2,'x'=4,'z'=8,'core'=2,'chan'=4] {'ylo','x'}, dimensions={0} | all-to-all | bytes 589824 | tf_op jit(solution)/shard_map/all_to_all | solution.py:504
  98.2 12.8 %all_to_all.37 = bf16[8,144,128]{2,1,0:T(8,128)(2,1)S(1)} all-to-all(bf16[8,144,128]{2,1,0:T(8,128)(2,1)S(1)} %broadcast_in_dim.8), channel_id=1, replica_groups=mesh['ylo'=2,'x'=4,'z'=8,'core'=2,'chan'=4] {'z'}, dimensions={0} | all-to-all | bytes 589824 | tf_op jit(solution)/shard_map/all_to_all | solution.py:506
  111.1 9.8 %all_to_all.38 = bf16[8,144,128]{2,1,0:T(8,128)(2,1)S(1)} all-to-all(bf16[8,144,128]{2,1,0:T(8,128)(2,1)S(1)} %broadcast_in_dim.9), channel_id=1, replica_groups=mesh['ylo'=2,'x'=4,'z'=8,'core'=2,'chan'=4] {'ylo','x'}, dimensions={0} | all-to-all | bytes 589824 | tf_op jit(solution)/shard_map/all_to_all | solution.py:508
  120.9 5.8 %all_gather.15 = bf16[2,1152,128]{2,1,0:T(8,128)(2,1)S(1)} all-gather(bf16[1,1152,128]{2,1,0:T(8,128)(2,1)S(1)} %bitcast.32), channel_id=1, replica_groups=mesh['ylo'=2,'x'=4,'z'=8,'core'=2,'chan'=4] {'core'}, dimensions={0}, use_global_device_ids=true | all-gather | bytes 884736 | tf_op jit(solution)/shard_map/all_gather | solution.py:509
  126.9 1.1 slice_multiply_fusion
  (43 shorter events, 1.1 us)
Async XLA Ops:
  7.2 8.8 %copy-start.7 = (s32[384,4,3]{0,1,2:T(4,128)S(1)}, s32[384,4,3]{0,1,2:T(4,128)}, u32[]{:S(2)}) copy-start(s32[384,4,3]{0,1,2:T(4,128)} %param.15) | copy-start | bytes 55300
  7.2 65.5 %all-gather.3.cloned.1.call-start = ((), (), s32[]{:S(2)}) async-start(), calls=%async_computation.7 | async-start | bytes 2654208 | tf_op jit(solution)/shard_map/all_gather | solution.py:466
  10.1 12.5 %all-to-all-start = ((bf16[8,192,128]{2,1,0:T(8,128)(2,1)}), bf16[8,192,128]{2,1,0:T(8,128)(2,1)S(1)}, u32[]{:S(2)}, u32[]{:S(2)}) async-start(bf16[8,192,128]{2,1,0:T(8,128)(2,1)} %get-tuple-element.10), calls=%async_computation | async-start | bytes 786432 | tf_op jit(solution)/shard_map/all_to_all | solution.py:467
  22.6 17.5 %copy-start.8 = (bf16[32,240]{1,0:T(8,128)(2,1)S(1)}, bf16[32,240]{1,0:T(8,128)(2,1)}, u32[]{:S(2)}) copy-start(bf16[32,240]{1,0:T(8,128)(2,1)} %constant.127.clone) | copy-start | bytes 46084
  22.6 31.1 %copy-start.2 = (bf16[3,96,128]{2,1,0:T(8,128)(2,1)S(1)}, bf16[3,96,128]{2,1,0:T(8,128)(2,1)}, u32[]{:S(2)}) copy-start(bf16[3,96,128]{2,1,0:T(8,128)(2,1)} %get-tuple-element.11.own_ref) | copy-start | bytes 221188
  32.6 27.8 %copy-start.6 = (bf16[32,1728]{1,0:T(8,128)(2,1)S(1)}, bf16[32,1728]{1,0:T(8,128)(2,1)}, u32[]{:S(2)}) copy-start(bf16[32,1728]{1,0:T(8,128)(2,1)} %constant.125.clone) | copy-start | bytes 331780
  32.6 27.8 %copy-start.9 = (f32[1728]{0:T(1024)S(1)}, f32[1728]{0:T(1024)}, u32[]{:S(2)}) copy-start(f32[1728]{0:T(1024)} %constant.126.clone) | copy-start | bytes 20740
  32.6 21.1 %all-to-all-start.1 = ((bf16[8,160,128]{2,1,0:T(8,128)(2,1)}), bf16[8,160,128]{2,1,0:T(8,128)(2,1)S(1)}, u32[]{:S(2)}, u32[]{:S(2)}) async-start(bf16[8,160,128]{2,1,0:T(8,128)(2,1)} %place.1), calls=%async_computation.1 | async-start | bytes 655360 | tf_op jit(solution)/shard_map/all_to_all | solution.py:479
  54.5 18.1 %all-to-all-start.2 = ((bf16[4,432,128]{2,1,0:T(8,128)(2,1)}), bf16[4,432,128]{2,1,0:T(8,128)(2,1)S(1)}, u32[]{:S(2)}, u32[]{:S(2)}) async-start(bf16[4,432,128]{2,1,0:T(8,128)(2,1)} %join.1), calls=%async_computation.2 | async-start | bytes 884736 | tf_op jit(solution)/shard_map/all_to_all | solution.py:489
  60.5 12.1 %copy-start = (bf16[432,192]{1,0:T(8,128)(2,1)S(1)}, bf16[432,192]{1,0:T(8,128)(2,1)}, u32[]{:S(2)}) copy-start(bf16[432,192]{1,0:T(8,128)(2,1)} %constant.130.clone.down_ref) | copy-start | bytes 497668
  60.6 12.1 %copy-start.1 = (bf16[160,144]{1,0:T(8,128)(2,1)S(1)}, bf16[160,144]{1,0:T(8,128)(2,1)}, u32[]{:S(2)}) copy-start(bf16[160,144]{1,0:T(8,128)(2,1)} %constant.133.clone.cell_ref) | copy-start | bytes 138244
  60.6 12.1 %copy-start.3 = (bf16[160,48]{1,0:T(8,128)(2,1)S(1)}, bf16[160,48]{1,0:T(8,128)(2,1)}, u32[]{:S(2)}) copy-start(bf16[160,48]{1,0:T(8,128)(2,1)} %constant.131.clone.rim_ref) | copy-start | bytes 46084
  60.6 12.1 %copy-start.4 = (bf16[160,64]{1,0:T(8,128)(2,1)S(1)}, bf16[160,64]{1,0:T(8,128)(2,1)}, u32[]{:S(2)}) copy-start(bf16[160,64]{1,0:T(8,128)(2,1)} %constant.129.clone.shift_ref) | copy-start | bytes 61444
  60.6 12.1 %copy-start.5 = (bf16[48,64]{1,0:T(8,128)(2,1)S(1)}, bf16[48,64]{1,0:T(8,128)(2,1)}, u32[]{:S(2)}) copy-start(bf16[48,64]{1,0:T(8,128)(2,1)} %constant.132.clone.order_ref) | copy-start | bytes 18436
Sparse Core Ops, SparseCore 0:
  10.7 46.5 all-gather.2

commit v7 on v6

--- a/solution.py
+++ b/solution.py
@@ -173,6 +173,10 @@
     return lax.dot_general(left, right, (((1,), (0,)), ((), ())), preferred_element_type=F32)
 
 
+def dot_tn(left, right):
+    return lax.dot_general(left, right, (((0,), (0,)), ((), ())), preferred_element_type=F32)
+
+
 def dot_nt(left, right):
     return lax.dot_general(left, right, (((1,), (1,)), ((), ())), preferred_element_type=F32)
 
@@ -296,7 +300,7 @@
 
 def main_kernel(
     pay_ref, rim_at_ref, shift_ref, down_ref, rim_ref, order_ref, cell_ref, window_hbm, weights_ref,
-    coarse_ref, gp_ref, grads_ref, window_ref, xs, cs, wf, wd, wins, ups, rims, downs, sems,
+    coarse_ref, gp_ref, grads_ref, window_ref, xs, cs, wf, wd, wins, ups, rims, downs, gps, up, sems,
 ):
     window_copies = [
         pltpu.make_async_copy(window_hbm.at[t], window_ref.at[t], sems.at[2 * CHAN + t]) for t in range(TILES_HERE)
@@ -304,8 +308,8 @@
     for copy in window_copies:
         copy.start()
     copies = []
-    for c in range(CHAN):
-        for which, held in enumerate((wf, wd)):
+    for which, held in enumerate((wf, wd)):
+        for c in range(CHAN):
             copies.append(
                 pltpu.make_async_copy(
                     weights_ref.at[2 * c + which], held.at[:, pl.ds(c * CH, CH), :], sems.at[2 * c + which]
@@ -340,9 +344,11 @@
         near = dot_nn(rim_at_ref[t], cs[t]).astype(BF)
         for s in range(len(RIM_TAPS)):
             rims[s, t * RIM_ROWS : (t + 1) * RIM_ROWS, :] = near[s * RIM_ROWS : (s + 1) * RIM_ROWS]
-    for copy in copies:
+    for copy in copies[:CHAN]:
         copy.wait()
     pre = dot_nn(wins[...], wf[...].reshape(9 * C, C))
+    for copy in copies[CHAN:]:
+        copy.wait()
     ups_low = [ups[s].astype(BF) for s in range(4)]
     blocks = (
         dot_nt(ups_low[0], wd[4]),
@@ -361,40 +367,30 @@
     hidden = (pre * gate).astype(BF)
     slope = gate + 0.5 * pre * (1.0 - bent * bent) * scale * (1.0 + np.float32(3 * 0.044715) * squared)
 
-    first_sum = None
-    down_sum = None
     for t in range(TILES_HERE):
         own_hidden = hidden[t * PRE_ROWS : (t + 1) * PRE_ROWS]
         windows = dot_nn(down_ref[...], own_hidden).astype(BF)
         for k in range(9):
             downs[t * DOWN_ROWS : (t + 1) * DOWN_ROWS, k * C : (k + 1) * C] = windows[k * DOWN_ROWS : (k + 1) * DOWN_ROWS]
+        up[t * DOWN_ROWS : (t + 1) * DOWN_ROWS, :] = dot_nn(order_ref[...], cs[t]).astype(BF)
 
         grad_hidden = jnp.concatenate([block[t * PART : (t + 1) * PART] for block in blocks], axis=0)
         grad_hidden = grad_hidden + dot_nn(rim_ref[...], rim[t * RIM_ROWS : (t + 1) * RIM_ROWS])
         grad_pre = (grad_hidden * slope[t * PRE_ROWS : t * PRE_ROWS + INNER]).astype(BF)
+        gps[t * PRE_ROWS : t * PRE_ROWS + INNER, :] = grad_pre
+        gps[t * PRE_ROWS + INNER : (t + 1) * PRE_ROWS, :] = jnp.zeros((PRE_ROWS - INNER, C), BF)
         gp_ref[t] = dot_nn(dot_nt(pick, grad_pre).astype(BF), cell_ref[...]).astype(BF)
 
-        x_own = dot_nt(pick, xs[t]).astype(BF)
-        h_own = dot_nt(pick, own_hidden).astype(BF)
-        up = dot_nn(order_ref[...], cs[t]).astype(BF)
-        first_parts, down_parts = [], []
-        for k in range(9):
-            first_parts.append(
-                dot_nt(x_own, window_ref[t, k * PRE_ROWS : k * PRE_ROWS + INNER, :]).astype(BF)
-            )
-            down_parts.append(
-                dot_nt(h_own, down_ref[k * DOWN_ROWS : (k + 1) * DOWN_ROWS, :]).astype(BF)
-            )
-        part = dot_nn(jnp.concatenate(first_parts, axis=0), grad_pre)
-        first_sum = part if first_sum is None else first_sum + part
-        part = dot_nn(jnp.concatenate(down_parts, axis=0), up)
-        down_sum = part if down_sum is None else down_sum + part
+    lanes = pl.multiple_of((chan // 2) * 128, 128)
+    for k in range(9):
+        for base, left, right in ((0, wins, gps), (9 * CH, downs, up)):
+            both = dot_tn(left[:, pl.ds(k * C + lanes, 128)], right[...])
+            part = jnp.where(chan % 2 == 0, both[:CH], both[CH:]).astype(BF)
+            for h in range(CORE):
+                grads_ref[h, base + k * CH : base + (k + 1) * CH, :] = part[:, h * 128 : (h + 1) * 128]
     coarse = dot_nt(dot_nn(downs[...], wd[...].reshape(9 * C, C)).astype(BF), pick).astype(BF)
     for t in range(TILES_HERE):
         coarse_ref[t] = coarse[t * DOWN_ROWS : t * DOWN_ROWS + COARSE]
-    for h in range(CORE):
-        grads_ref[h, : 9 * CH, :] = first_sum[:, h * 128 : (h + 1) * 128].astype(BF)
-        grads_ref[h, 9 * CH :, :] = down_sum[:, h * 128 : (h + 1) * 128].astype(BF)
 
 
 def vmem(count):
@@ -435,6 +431,8 @@
             pltpu.VMEM((4, TILES_HERE * PART, C), F32),
             pltpu.VMEM((len(RIM_TAPS), TILES_HERE * RIM_ROWS, C), BF),
             pltpu.VMEM((TILES_HERE * DOWN_ROWS, 9 * C), BF),
+            pltpu.VMEM((TILES_HERE * PRE_ROWS, C), BF),
+            pltpu.VMEM((TILES_HERE * DOWN_ROWS, C), BF),
             pltpu.SemaphoreType.DMA((2 * CHAN + TILES_HERE,)),
         ],
         compiler_params=MOST,

time: 135 us -> 135 us (level)
  no operation moved by 1% of the time
where the time goes in v7:
time: 135 us
  blocking collectives  53.2 us (39%)
  waiting for transfers between devices  27.7 us (21%)
  starting transfers between devices  19.3 us (14%)
  between operations  14.3 us (11%)
  Pallas kernels  14.1 us (10%)
  other arithmetic  3.62 us (3%)
  local copies, waits for them, and re-layouts  2.26 us (2%)
    all_to_all x1, waiting for transfers between devices, shards(): got = lax.all_to_all(sends, 'z', 0, 0)  13.3 us
    all_to_all x1, blocking collectives, shards(): lax.all_to_all(jnp.broadcast_to(part[None], (NZ, 144, 128)), 'z', 0, 0)  12.8 us
    all_to_all x1, blocking collectives, shards(): part = lax.all_to_all(part, ('ylo', 'x'), 0, 0)  10.7 us
    all_to_all x1, waiting for transfers between devices, shards(): payload = lax.all_to_all(joined, 'chan', 0, 0)  10.1 us
    all_to_all x1, blocking collectives, shards(): lax.all_to_all(jnp.broadcast_to(part[None], (YX, 144, 128)), ('ylo', 'x')...  9.82 us
    pallas_call x1, Pallas kernels, tiles_call(): pl.pallas_call(main_kernel, out_shape=(jax.ShapeDtypeStruct((TILES_HERE,...  8.12 us
    all_gather x1, blocking collectives, shards(): units = lax.all_gather(units, 'core', axis=0, tiled=True)  7.67 us
    all_to_all x1, starting transfers between devices, shards(): got = lax.all_to_all(sends, 'z', 0, 0)  7.49 us
  transfers between devices with their start and end apart: 4, of which 3 were waited for; matrix products, arithmetic and copies ran while one was open for 3% of the time, Pallas kernels for 2%

profile of v7, /device:TPU:1, one launch (start us, length us, event | category | flops | bytes accessed | tf_op | source)
XLA Modules:
  0.0 134.7 jit_solution(10856425459636938473)
XLA Ops:
  7.2 2.9 %pack.1 = (bf16[3,96,128]{2,1,0:T(8,128)(2,1)}, bf16[8,192,128]{2,1,0:T(8,128)(2,1)}, bf16[9,64,256]{2,1,0:T(8,128)(2,1)}) custom-call(bf16[3,64,144]{2,1,0:T(8,128)(2,1)} %fields_hbm.1, bf16[3,36,64]{2,1,0:T(8,128)(2,1)} %bitcast.35, bf16[9,64,256]{2,1,0:T(8,128)(2,1)} %first_ref.1, bf16[9,64,256]{2,1,0:T(8,128)(2,1)} %down_ref.2), custom_call_target="tpu_custom_call" | custom-call | tf_op jit(solution)/shard_map/pack/pallas_call | solution.py:445
  10.1 5.9 %all-to-all-start = ((bf16[8,192,128]{2,1,0:T(8,128)(2,1)}), bf16[8,192,128]{2,1,0:T(8,128)(2,1)S(1)}, u32[]{:S(2)}, u32[]{:S(2)}) async-start(bf16[8,192,128]{2,1,0:T(8,128)(2,1)} %get-tuple-element.10), calls=%async_computation | async-start | bytes 786432 | tf_op jit(solution)/shard_map/all_to_all | solution.py:465
  16.4 0.2 copy.33
  16.6 0.2 ne.70
  16.8 0.1 copy.38
  17.0 0.1 mul.88
  17.1 0.1 copy.35
  17.2 0.1 div.31
  17.4 0.1 copy.34
  17.5 0.1 rem.82
  17.7 0.1 copy.36
  17.8 0.1 squeeze.6
  18.0 0.1 copy.37
  18.1 0.1 mul.84
  18.3 4.3 %all-to-all-done = bf16[8,192,128]{2,1,0:T(8,128)(2,1)S(1)} async-done(((bf16[8,192,128]{2,1,0:T(8,128)(2,1)}), bf16[8,192,128]{2,1,0:T(8,128)(2,1)S(1)}, u32[]{:S(2)}, u32[]{:S(2)}) %all-to-all-start) | async-done | bytes 393248 | tf_op jit(solution)/shard_map/all_to_all | solution.py:465
  22.6 7.7 %all_gather.12.unit_ref = bf16[3072,128]{1,0:T(8,128)(2,1)S(1)} all-gather(bf16[1536,128]{1,0:T(8,128)(2,1)S(1)} %bitcast.30), channel_id=1, replica_groups=mesh['ylo'=2,'x'=4,'z'=8,'core'=2,'chan'=4] {'core'}, dimensions={0}, use_global_device_ids=true | all-gather | bytes 1179648 | tf_op jit(solution)/shard_map/all_gather | solution.py:466
  30.3 2.3 %place.1 = bf16[8,160,128]{2,1,0:T(8,128)(2,1)} custom-call(s32[1536]{0:T(1024)S(1)} %get-tuple-element.26.word_ref, s32[1536]{0:T(1024)S(1)} %get-tuple-element.25.beyond_ref, bf16[3072,128]{1,0:T(8,128)(2,1)S(1)} %all_gather.12.unit_ref), custom_call_target="tpu_custom_call" | custom-call | tf_op jit(solution)/shard_map/place/pallas_call | solution.py:468
  32.6 7.5 %all-to-all-start.1 = ((bf16[8,160,128]{2,1,0:T(8,128)(2,1)}), bf16[8,160,128]{2,1,0:T(8,128)(2,1)S(1)}, u32[]{:S(2)}, u32[]{:S(2)}) async-start(bf16[8,160,128]{2,1,0:T(8,128)(2,1)} %place.1), calls=%async_computation.1 | async-start | bytes 655360 | tf_op jit(solution)/shard_map/all_to_all | solution.py:477
  40.2 0.2 compare_convert_fusion.1.rim_at_ref
  40.4 13.3 %all-to-all-done.1.got_ref = bf16[8,160,128]{2,1,0:T(8,128)(2,1)S(1)} async-done(((bf16[8,160,128]{2,1,0:T(8,128)(2,1)}), bf16[8,160,128]{2,1,0:T(8,128)(2,1)S(1)}, u32[]{:S(2)}, u32[]{:S(2)}) %all-to-all-start.1) | async-done | bytes 327712 | tf_op jit(solution)/shard_map/all_to_all | solution.py:477
  53.7 0.8 join.1
  54.5 5.8 %all-to-all-start.2 = ((bf16[4,432,128]{2,1,0:T(8,128)(2,1)}), bf16[4,432,128]{2,1,0:T(8,128)(2,1)S(1)}, u32[]{:S(2)}, u32[]{:S(2)}) async-start(bf16[4,432,128]{2,1,0:T(8,128)(2,1)} %join.1), calls=%async_computation.2 | async-start | bytes 884736 | tf_op jit(solution)/shard_map/all_to_all | solution.py:487
  60.4 0.1 convolution_add_fusion
  60.6 1.9 %compare_convert_fusion.window_hbm = bf16[3,1728,256]{2,1,0:T(8,128)(2,1)} fusion(f32[256]{0:T(256)S(1)} %add_convert_fusion.1, f32[3,1728]{1,0:T(4,128)S(1)} %convolution_add_fusion), kind=kLoop, calls=%fused_computation | loop fusion | flops 2654208 | bytes 2675968 | tf_op jit(solution)/shard_map/convert_element_type | solution.py:496
  62.5 10.1 %all-to-all-done.2.pay_ref = bf16[4,432,128]{2,1,0:T(8,128)(2,1)S(1)} async-done(((bf16[4,432,128]{2,1,0:T(8,128)(2,1)}), bf16[4,432,128]{2,1,0:T(8,128)(2,1)S(1)}, u32[]{:S(2)}, u32[]{:S(2)}) %all-to-all-start.2) | async-done | bytes 442400 | tf_op jit(solution)/shard_map/all_to_all | solution.py:487
  72.7 8.1 %tiles.1 = (bf16[3,36,64]{2,1,0:T(8,128)(2,1)}, bf16[3,64,144]{2,1,0:T(8,128)(2,1)}, bf16[2,1152,128]{2,1,0:T(8,128)(2,1)S(1)}) custom-call(bf16[4,432,128]{2,1,0:T(8,128)(2,1)S(1)} %all-to-all-done.2.pay_ref, bf16[3,240,64]{2,1,0:T(8,128)(2,1)S(1)} %compare_convert_fusion.1.rim_at_ref, bf16[160,64]{1,0:T(8,128)(2,1)S(1)} %copy-done.4, ...), custom_call_target="tpu_custom_call" | custom-call | tf_op jit(solution)/shard_map/tiles/pallas_call | solution.py:415
  80.8 6.3 %all_to_all.35 = bf16[2,1152,128]{2,1,0:T(8,128)(2,1)S(1)} all-to-all(bf16[2,1152,128]{2,1,0:T(8,128)(2,1)S(1)} %get-tuple-element.14), channel_id=1, replica_groups=mesh['ylo'=2,'x'=4,'z'=8,'core'=2,'chan'=4] {'core'}, dimensions={0} | all-to-all | bytes 1179648 | tf_op jit(solution)/shard_map/all_to_all | solution.py:500
  87.2 10.7 %all_to_all.36 = bf16[8,144,128]{2,1,0:T(8,128)(2,1)S(1)} all-to-all(bf16[8,144,128]{2,1,0:T(8,128)(2,1)S(1)} %bitcast.31), channel_id=1, replica_groups=mesh['ylo'=2,'x'=4,'z'=8,'core'=2,'chan'=4] {'ylo','x'}, dimensions={0} | all-to-all | bytes 589824 | tf_op jit(solution)/shard_map/all_to_all | solution.py:502
  98.1 12.8 %all_to_all.37 = bf16[8,144,128]{2,1,0:T(8,128)(2,1)S(1)} all-to-all(bf16[8,144,128]{2,1,0:T(8,128)(2,1)S(1)} %broadcast_in_dim.8), channel_id=1, replica_groups=mesh['ylo'=2,'x'=4,'z'=8,'core'=2,'chan'=4] {'z'}, dimensions={0} | all-to-all | bytes 589824 | tf_op jit(solution)/shard_map/all_to_all | solution.py:504
  110.9 9.8 %all_to_all.38 = bf16[8,144,128]{2,1,0:T(8,128)(2,1)S(1)} all-to-all(bf16[8,144,128]{2,1,0:T(8,128)(2,1)S(1)} %broadcast_in_dim.9), channel_id=1, replica_groups=mesh['ylo'=2,'x'=4,'z'=8,'core'=2,'chan'=4] {'ylo','x'}, dimensions={0} | all-to-all | bytes 589824 | tf_op jit(solution)/shard_map/all_to_all | solution.py:506
  120.8 5.8 %all_gather.15 = bf16[2,1152,128]{2,1,0:T(8,128)(2,1)S(1)} all-gather(bf16[1,1152,128]{2,1,0:T(8,128)(2,1)S(1)} %bitcast.32), channel_id=1, replica_groups=mesh['ylo'=2,'x'=4,'z'=8,'core'=2,'chan'=4] {'core'}, dimensions={0}, use_global_device_ids=true | all-gather | bytes 884736 | tf_op jit(solution)/shard_map/all_gather | solution.py:507
  126.7 1.1 slice_multiply_fusion
  (43 shorter events, 1.1 us)
Async XLA Ops:
  7.2 8.8 %copy-start.7 = (s32[384,4,3]{0,1,2:T(4,128)S(1)}, s32[384,4,3]{0,1,2:T(4,128)}, u32[]{:S(2)}) copy-start(s32[384,4,3]{0,1,2:T(4,128)} %param.15) | copy-start | bytes 55300
  7.2 65.5 %all-gather.3.cloned.1.call-start = ((), (), s32[]{:S(2)}) async-start(), calls=%async_computation.7 | async-start | bytes 2654208 | tf_op jit(solution)/shard_map/all_gather | solution.py:464
  10.1 12.5 %all-to-all-start = ((bf16[8,192,128]{2,1,0:T(8,128)(2,1)}), bf16[8,192,128]{2,1,0:T(8,128)(2,1)S(1)}, u32[]{:S(2)}, u32[]{:S(2)}) async-start(bf16[8,192,128]{2,1,0:T(8,128)(2,1)} %get-tuple-element.10), calls=%async_computation | async-start | bytes 786432 | tf_op jit(solution)/shard_map/all_to_all | solution.py:465
  22.6 17.5 %copy-start.8 = (bf16[32,240]{1,0:T(8,128)(2,1)S(1)}, bf16[32,240]{1,0:T(8,128)(2,1)}, u32[]{:S(2)}) copy-start(bf16[32,240]{1,0:T(8,128)(2,1)} %constant.127.clone) | copy-start | bytes 46084
  22.6 31.1 %copy-start.2 = (bf16[3,96,128]{2,1,0:T(8,128)(2,1)S(1)}, bf16[3,96,128]{2,1,0:T(8,128)(2,1)}, u32[]{:S(2)}) copy-start(bf16[3,96,128]{2,1,0:T(8,128)(2,1)} %get-tuple-element.11.own_ref) | copy-start | bytes 221188
  32.6 27.8 %copy-start.6 = (bf16[32,1728]{1,0:T(8,128)(2,1)S(1)}, bf16[32,1728]{1,0:T(8,128)(2,1)}, u32[]{:S(2)}) copy-start(bf16[32,1728]{1,0:T(8,128)(2,1)} %constant.125.clone) | copy-start | bytes 331780
  32.6 27.8 %copy-start.9 = (f32[1728]{0:T(1024)S(1)}, f32[1728]{0:T(1024)}, u32[]{:S(2)}) copy-start(f32[1728]{0:T(1024)} %constant.126.clone) | copy-start | bytes 20740
  32.6 21.1 %all-to-all-start.1 = ((bf16[8,160,128]{2,1,0:T(8,128)(2,1)}), bf16[8,160,128]{2,1,0:T(8,128)(2,1)S(1)}, u32[]{:S(2)}, u32[]{:S(2)}) async-start(bf16[8,160,128]{2,1,0:T(8,128)(2,1)} %place.1), calls=%async_computation.1 | async-start | bytes 655360 | tf_op jit(solution)/shard_map/all_to_all | solution.py:477
  54.5 18.1 %all-to-all-start.2 = ((bf16[4,432,128]{2,1,0:T(8,128)(2,1)}), bf16[4,432,128]{2,1,0:T(8,128)(2,1)S(1)}, u32[]{:S(2)}, u32[]{:S(2)}) async-start(bf16[4,432,128]{2,1,0:T(8,128)(2,1)} %join.1), calls=%async_computation.2 | async-start | bytes 884736 | tf_op jit(solution)/shard_map/all_to_all | solution.py:487
  60.5 12.1 %copy-start = (bf16[432,192]{1,0:T(8,128)(2,1)S(1)}, bf16[432,192]{1,0:T(8,128)(2,1)}, u32[]{:S(2)}) copy-start(bf16[432,192]{1,0:T(8,128)(2,1)} %constant.130.clone.down_ref) | copy-start | bytes 497668
  60.6 12.1 %copy-start.1 = (bf16[160,144]{1,0:T(8,128)(2,1)S(1)}, bf16[160,144]{1,0:T(8,128)(2,1)}, u32[]{:S(2)}) copy-start(bf16[160,144]{1,0:T(8,128)(2,1)} %constant.133.clone.cell_ref) | copy-start | bytes 138244
  60.6 12.1 %copy-start.3 = (bf16[160,48]{1,0:T(8,128)(2,1)S(1)}, bf16[160,48]{1,0:T(8,128)(2,1)}, u32[]{:S(2)}) copy-start(bf16[160,48]{1,0:T(8,128)(2,1)} %constant.131.clone.rim_ref) | copy-start | bytes 46084
  60.6 12.1 %copy-start.4 = (bf16[160,64]{1,0:T(8,128)(2,1)S(1)}, bf16[160,64]{1,0:T(8,128)(2,1)}, u32[]{:S(2)}) copy-start(bf16[160,64]{1,0:T(8,128)(2,1)} %constant.129.clone.shift_ref) | copy-start | bytes 61444
  60.6 12.1 %copy-start.5 = (bf16[48,64]{1,0:T(8,128)(2,1)S(1)}, bf16[48,64]{1,0:T(8,128)(2,1)}, u32[]{:S(2)}) copy-start(bf16[48,64]{1,0:T(8,128)(2,1)} %constant.132.clone.order_ref) | copy-start | bytes 18436
Sparse Core Ops, SparseCore 0:
  10.7 46.5 all-gather.2

commit v8 on v7

--- a/solution.py
+++ b/solution.py
@@ -344,11 +344,9 @@
         near = dot_nn(rim_at_ref[t], cs[t]).astype(BF)
         for s in range(len(RIM_TAPS)):
             rims[s, t * RIM_ROWS : (t + 1) * RIM_ROWS, :] = near[s * RIM_ROWS : (s + 1) * RIM_ROWS]
-    for copy in copies[:CHAN]:
+    for copy in copies:
         copy.wait()
     pre = dot_nn(wins[...], wf[...].reshape(9 * C, C))
-    for copy in copies[CHAN:]:
-        copy.wait()
     ups_low = [ups[s].astype(BF) for s in range(4)]
     blocks = (
         dot_nt(ups_low[0], wd[4]),
@@ -497,7 +495,8 @@
 
     coarse, grad_pre, grads = tiles_call(payload, one_hots[0], one_hots[1], weights)
 
-    part = lax.all_to_all(grads, "core", 0, 0)
+    part = lax.all_gather(grads, "core", axis=0, tiled=False)
+    part = lax.dynamic_index_in_dim(part, coords[3], 1, keepdims=False)
     part = (part[0].astype(F32) + part[1].astype(F32)).astype(BF).reshape(YX, 144, 128)
     part = lax.all_to_all(part, ("ylo", "x"), 0, 0)
     part = part.astype(F32).sum(0).astype(BF)

time: 135 us -> 145 us (1.074)
  waiting for transfers between devices: 27.7 us -> 39.4 us
  blocking collectives: 53.2 us -> 51.6 us
    all_gather x0 -> x1, waiting for transfers between devices: none -> 11.7 us  [shards(): part = lax.all_gather(grads, 'core', axis=0, tiled=False)]
    all_to_all x1 -> x0, blocking collectives: 6.33 us -> none  [shards(): part = lax.all_to_all(grads, 'core', 0, 0)]
    all_to_all x1, blocking collectives: 12.8 us -> 17.2 us  [shards(): lax.all_to_all(jnp.broadcast_to(part[None], (NZ, 144, 128)), 'z', 0, 0)]
  transfers between devices with their start and end apart: 4 -> 5, of which waited for: 3 -> 4; matrix products, arithmetic and copies ran while one was open for 3% -> 3% of each run, Pallas kernels for 2% -> 2%
where the time goes in v8:
time: 145 us
  blocking collectives  51.6 us (36%)
  waiting for transfers between devices  39.4 us (27%)
  starting transfers between devices  19.3 us (13%)
  between operations  14.3 us (10%)
  Pallas kernels  13 us (9%)
  other arithmetic  4.67 us (3%)
  local copies, waits for them, and re-layouts  2.26 us (2%)
    all_to_all x1, blocking collectives, shards(): lax.all_to_all(jnp.broadcast_to(part[None], (NZ, 144, 128)), 'z', 0, 0)  17.2 us
    all_to_all x1, waiting for transfers between devices, shards(): got = lax.all_to_all(sends, 'z', 0, 0)  13.3 us
    all_gather x1, waiting for transfers between devices, shards(): part = lax.all_gather(grads, 'core', axis=0, tiled=False)  11.7 us
    all_to_all x1, blocking collectives, shards(): part = lax.all_to_all(part, ('ylo', 'x'), 0, 0)  11.1 us
    all_to_all x1, waiting for transfers between devices, shards(): payload = lax.all_to_all(joined, 'chan', 0, 0)  10.1 us
    all_to_all x1, blocking collectives, shards(): lax.all_to_all(jnp.broadcast_to(part[None], (YX, 144, 128)), ('ylo', 'x')...  9.68 us
    all_gather x1, blocking collectives, shards(): units = lax.all_gather(units, 'core', axis=0, tiled=True)  7.54 us
    all_to_all x1, starting transfers between devices, shards(): got = lax.all_to_all(sends, 'z', 0, 0)  7.42 us
  transfers between devices with their start and end apart: 5, of which 4 were waited for; matrix products, arithmetic and copies ran while one was open for 3% of the time, Pallas kernels for 2%

profile of v8, /device:TPU:1, one launch (start us, length us, event | category | flops | bytes accessed | tf_op | source)
XLA Modules:
  0.0 144.7 jit_solution(6030387918214888994)
XLA Ops:
  7.2 2.9 %pack.1 = (bf16[3,96,128]{2,1,0:T(8,128)(2,1)}, bf16[8,192,128]{2,1,0:T(8,128)(2,1)}, bf16[9,64,256]{2,1,0:T(8,128)(2,1)}) custom-call(bf16[3,64,144]{2,1,0:T(8,128)(2,1)} %fields_hbm.1, bf16[3,36,64]{2,1,0:T(8,128)(2,1)} %bitcast.37, bf16[9,64,256]{2,1,0:T(8,128)(2,1)} %first_ref.1, bf16[9,64,256]{2,1,0:T(8,128)(2,1)} %down_ref.2), custom_call_target="tpu_custom_call" | custom-call | tf_op jit(solution)/shard_map/pack/pallas_call | solution.py:443
  10.1 5.9 %all-to-all-start = ((bf16[8,192,128]{2,1,0:T(8,128)(2,1)}), bf16[8,192,128]{2,1,0:T(8,128)(2,1)S(1)}, u32[]{:S(2)}, u32[]{:S(2)}) async-start(bf16[8,192,128]{2,1,0:T(8,128)(2,1)} %get-tuple-element.10), calls=%async_computation | async-start | bytes 786432 | tf_op jit(solution)/shard_map/all_to_all | solution.py:463
  16.4 0.2 copy.33
  16.6 0.2 ne.70
  16.8 0.1 copy.38
  17.0 0.1 mul.88
  17.1 0.1 copy.35
  17.2 0.1 div.31
  17.4 0.1 copy.34
  17.5 0.1 rem.82
  17.7 0.1 copy.36
  17.8 0.1 squeeze.8
  18.0 0.1 copy.37
  18.1 0.1 mul.84
  18.3 4.3 %all-to-all-done = bf16[8,192,128]{2,1,0:T(8,128)(2,1)S(1)} async-done(((bf16[8,192,128]{2,1,0:T(8,128)(2,1)}), bf16[8,192,128]{2,1,0:T(8,128)(2,1)S(1)}, u32[]{:S(2)}, u32[]{:S(2)}) %all-to-all-start) | async-done | bytes 393248 | tf_op jit(solution)/shard_map/all_to_all | solution.py:463
  22.6 7.5 %all_gather.18.unit_ref = bf16[3072,128]{1,0:T(8,128)(2,1)S(1)} all-gather(bf16[1536,128]{1,0:T(8,128)(2,1)S(1)} %bitcast.31), channel_id=1, replica_groups=mesh['ylo'=2,'x'=4,'z'=8,'core'=2,'chan'=4] {'core'}, dimensions={0}, use_global_device_ids=true | all-gather | bytes 1179648 | tf_op jit(solution)/shard_map/all_gather | solution.py:464
  30.1 2.3 %place.1 = bf16[8,160,128]{2,1,0:T(8,128)(2,1)} custom-call(s32[1536]{0:T(1024)S(1)} %get-tuple-element.26.word_ref, s32[1536]{0:T(1024)S(1)} %get-tuple-element.25.beyond_ref, bf16[3072,128]{1,0:T(8,128)(2,1)S(1)} %all_gather.18.unit_ref), custom_call_target="tpu_custom_call" | custom-call | tf_op jit(solution)/shard_map/place/pallas_call | solution.py:466
  32.5 7.4 %all-to-all-start.1 = ((bf16[8,160,128]{2,1,0:T(8,128)(2,1)}), bf16[8,160,128]{2,1,0:T(8,128)(2,1)S(1)}, u32[]{:S(2)}, u32[]{:S(2)}) async-start(bf16[8,160,128]{2,1,0:T(8,128)(2,1)} %place.1), calls=%async_computation.1 | async-start | bytes 655360 | tf_op jit(solution)/shard_map/all_to_all | solution.py:475
  40.0 0.2 compare_convert_fusion.1.rim_at_ref
  40.2 13.3 %all-to-all-done.1.got_ref = bf16[8,160,128]{2,1,0:T(8,128)(2,1)S(1)} async-done(((bf16[8,160,128]{2,1,0:T(8,128)(2,1)}), bf16[8,160,128]{2,1,0:T(8,128)(2,1)S(1)}, u32[]{:S(2)}, u32[]{:S(2)}) %all-to-all-start.1) | async-done | bytes 327712 | tf_op jit(solution)/shard_map/all_to_all | solution.py:475
  53.5 0.8 join.1
  54.3 5.9 %all-to-all-start.2 = ((bf16[4,432,128]{2,1,0:T(8,128)(2,1)}), bf16[4,432,128]{2,1,0:T(8,128)(2,1)S(1)}, u32[]{:S(2)}, u32[]{:S(2)}) async-start(bf16[4,432,128]{2,1,0:T(8,128)(2,1)} %join.1), calls=%async_computation.2 | async-start | bytes 884736 | tf_op jit(solution)/shard_map/all_to_all | solution.py:485
  60.5 1.9 %compare_convert_fusion.window_hbm = bf16[3,1728,256]{2,1,0:T(8,128)(2,1)} fusion(f32[256]{0:T(256)S(1)} %add_convert_fusion.1, f32[3,1728]{1,0:T(4,128)S(1)} %convolution_add_fusion), kind=kLoop, calls=%fused_computation | loop fusion | flops 2654208 | bytes 2675968 | tf_op jit(solution)/shard_map/convert_element_type | solution.py:494
  62.4 10.1 %all-to-all-done.2.pay_ref = bf16[4,432,128]{2,1,0:T(8,128)(2,1)S(1)} async-done(((bf16[4,432,128]{2,1,0:T(8,128)(2,1)}), bf16[4,432,128]{2,1,0:T(8,128)(2,1)S(1)}, u32[]{:S(2)}, u32[]{:S(2)}) %all-to-all-start.2) | async-done | bytes 442400 | tf_op jit(solution)/shard_map/all_to_all | solution.py:485
  72.6 7.0 %tiles.1 = (bf16[3,36,64]{2,1,0:T(8,128)(2,1)}, bf16[3,64,144]{2,1,0:T(8,128)(2,1)}, bf16[2,1152,128]{2,1,0:T(8,128)(2,1)}) custom-call(bf16[4,432,128]{2,1,0:T(8,128)(2,1)S(1)} %all-to-all-done.2.pay_ref, bf16[3,240,64]{2,1,0:T(8,128)(2,1)S(1)} %compare_convert_fusion.1.rim_at_ref, bf16[160,64]{1,0:T(8,128)(2,1)S(1)} %copy-done.4, ...), custom_call_target="tpu_custom_call" | custom-call | tf_op jit(solution)/shard_map/tiles/pallas_call | solution.py:413
  79.6 11.7 %all-gather.7.cloned.1.call-done = bf16[4,1152,128]{2,1,0:T(8,128)(2,1)} async-done(((bf16[2,1152,128]{2,1,0:T(8,128)(2,1)}), bf16[4,1152,128]{2,1,0:T(8,128)(2,1)}) %all-gather.7.cloned.1.call-update) | async-done | bytes 1179664 | tf_op jit(solution)/shard_map/all_gather | solution.py:498
  91.3 1.1 add_convert_fusion
  92.4 11.1 %all_to_all.30 = bf16[8,144,128]{2,1,0:T(8,128)(2,1)S(1)} all-to-all(bf16[8,144,128]{2,1,0:T(8,128)(2,1)S(1)} %bitcast.33), channel_id=1, replica_groups=mesh['ylo'=2,'x'=4,'z'=8,'core'=2,'chan'=4] {'ylo','x'}, dimensions={0} | all-to-all | bytes 589824 | tf_op jit(solution)/shard_map/all_to_all | solution.py:501
  103.6 17.2 %all_to_all.31 = bf16[8,144,128]{2,1,0:T(8,128)(2,1)S(1)} all-to-all(bf16[8,144,128]{2,1,0:T(8,128)(2,1)S(1)} %broadcast_in_dim.8), channel_id=1, replica_groups=mesh['ylo'=2,'x'=4,'z'=8,'core'=2,'chan'=4] {'z'}, dimensions={0} | all-to-all | bytes 589824 | tf_op jit(solution)/shard_map/all_to_all | solution.py:503
  120.9 9.7 %all_to_all.32 = bf16[8,144,128]{2,1,0:T(8,128)(2,1)S(1)} all-to-all(bf16[8,144,128]{2,1,0:T(8,128)(2,1)S(1)} %broadcast_in_dim.9), channel_id=1, replica_groups=mesh['ylo'=2,'x'=4,'z'=8,'core'=2,'chan'=4] {'ylo','x'}, dimensions={0} | all-to-all | bytes 589824 | tf_op jit(solution)/shard_map/all_to_all | solution.py:505
  130.6 6.1 %all_gather.23 = bf16[2,1152,128]{2,1,0:T(8,128)(2,1)S(1)} all-gather(bf16[1,1152,128]{2,1,0:T(8,128)(2,1)S(1)} %bitcast.32), channel_id=1, replica_groups=mesh['ylo'=2,'x'=4,'z'=8,'core'=2,'chan'=4] {'core'}, dimensions={0}, use_global_device_ids=true | all-gather | bytes 884736 | tf_op jit(solution)/shard_map/all_gather | solution.py:506
  136.8 1.1 slice_multiply_fusion
  (45 shorter events, 1.2 us)
Async XLA Ops:
  7.2 8.8 %copy-start.7 = (s32[384,4,3]{0,1,2:T(4,128)S(1)}, s32[384,4,3]{0,1,2:T(4,128)}, u32[]{:S(2)}) copy-start(s32[384,4,3]{0,1,2:T(4,128)} %param.15) | copy-start | bytes 55300
  7.2 65.4 %all-gather.5.cloned.1.call-start = ((), (), s32[]{:S(2)}) async-start(), calls=%async_computation.6 | async-start | bytes 2654208 | tf_op jit(solution)/shard_map/all_gather | solution.py:462
  10.1 12.5 %all-to-all-start = ((bf16[8,192,128]{2,1,0:T(8,128)(2,1)}), bf16[8,192,128]{2,1,0:T(8,128)(2,1)S(1)}, u32[]{:S(2)}, u32[]{:S(2)}) async-start(bf16[8,192,128]{2,1,0:T(8,128)(2,1)} %get-tuple-element.10), calls=%async_computation | async-start | bytes 786432 | tf_op jit(solution)/shard_map/all_to_all | solution.py:463
  30.1 9.8 %copy-start.8 = (bf16[32,240]{1,0:T(8,128)(2,1)S(1)}, bf16[32,240]{1,0:T(8,128)(2,1)}, u32[]{:S(2)}) copy-start(bf16[32,240]{1,0:T(8,128)(2,1)} %constant.131.clone) | copy-start | bytes 46084
  30.1 23.4 %copy-start.2 = (bf16[3,96,128]{2,1,0:T(8,128)(2,1)S(1)}, bf16[3,96,128]{2,1,0:T(8,128)(2,1)}, u32[]{:S(2)}) copy-start(bf16[3,96,128]{2,1,0:T(8,128)(2,1)} %get-tuple-element.11.own_ref) | copy-start | bytes 221188
  32.5 27.8 %copy-start.6 = (bf16[32,1728]{1,0:T(8,128)(2,1)S(1)}, bf16[32,1728]{1,0:T(8,128)(2,1)}, u32[]{:S(2)}) copy-start(bf16[32,1728]{1,0:T(8,128)(2,1)} %constant.129.clone) | copy-start | bytes 331780
  32.5 27.8 %copy-start.9 = (f32[1728]{0:T(1024)S(1)}, f32[1728]{0:T(1024)}, u32[]{:S(2)}) copy-start(f32[1728]{0:T(1024)} %constant.130.clone) | copy-start | bytes 20740
  32.5 21.0 %all-to-all-start.1 = ((bf16[8,160,128]{2,1,0:T(8,128)(2,1)}), bf16[8,160,128]{2,1,0:T(8,128)(2,1)S(1)}, u32[]{:S(2)}, u32[]{:S(2)}) async-start(bf16[8,160,128]{2,1,0:T(8,128)(2,1)} %place.1), calls=%async_computation.1 | async-start | bytes 655360 | tf_op jit(solution)/shard_map/all_to_all | solution.py:475
  54.3 18.2 %all-to-all-start.2 = ((bf16[4,432,128]{2,1,0:T(8,128)(2,1)}), bf16[4,432,128]{2,1,0:T(8,128)(2,1)S(1)}, u32[]{:S(2)}, u32[]{:S(2)}) async-start(bf16[4,432,128]{2,1,0:T(8,128)(2,1)} %join.1), calls=%async_computation.2 | async-start | bytes 884736 | tf_op jit(solution)/shard_map/all_to_all | solution.py:485
  60.3 31.1 %all-gather.7.cloned.1.call-start = ((), (), s32[]{:S(2)}) async-start(), calls=%async_computation.7 | async-start | bytes 1769472 | tf_op jit(solution)/shard_map/all_gather | solution.py:498
  60.4 12.1 %copy-start = (bf16[432,192]{1,0:T(8,128)(2,1)S(1)}, bf16[432,192]{1,0:T(8,128)(2,1)}, u32[]{:S(2)}) copy-start(bf16[432,192]{1,0:T(8,128)(2,1)} %constant.134.clone.down_ref) | copy-start | bytes 497668
  60.4 12.1 %copy-start.1 = (bf16[160,144]{1,0:T(8,128)(2,1)S(1)}, bf16[160,144]{1,0:T(8,128)(2,1)}, u32[]{:S(2)}) copy-start(bf16[160,144]{1,0:T(8,128)(2,1)} %constant.137.clone.cell_ref) | copy-start | bytes 138244
  60.4 12.1 %copy-start.3 = (bf16[160,48]{1,0:T(8,128)(2,1)S(1)}, bf16[160,48]{1,0:T(8,128)(2,1)}, u32[]{:S(2)}) copy-start(bf16[160,48]{1,0:T(8,128)(2,1)} %constant.135.clone.rim_ref) | copy-start | bytes 46084
  60.5 12.1 %copy-start.4 = (bf16[160,64]{1,0:T(8,128)(2,1)S(1)}, bf16[160,64]{1,0:T(8,128)(2,1)}, u32[]{:S(2)}) copy-start(bf16[160,64]{1,0:T(8,128)(2,1)} %constant.133.clone.shift_ref) | copy-start | bytes 61444
  60.5 12.1 %copy-start.5 = (bf16[48,64]{1,0:T(8,128)(2,1)S(1)}, bf16[48,64]{1,0:T(8,128)(2,1)}, u32[]{:S(2)}) copy-start(bf16[48,64]{1,0:T(8,128)(2,1)} %constant.136.clone.order_ref) | copy-start | bytes 18436
Sparse Core Ops, SparseCore 0:
  10.7 46.5 all-gather.4
  79.7 11.5 all-gather.6

commit v9 on v8

--- a/solution.py
+++ b/solution.py
@@ -495,8 +495,7 @@
 
     coarse, grad_pre, grads = tiles_call(payload, one_hots[0], one_hots[1], weights)
 
-    part = lax.all_gather(grads, "core", axis=0, tiled=False)
-    part = lax.dynamic_index_in_dim(part, coords[3], 1, keepdims=False)
+    part = lax.all_to_all(grads, "core", 0, 0)
     part = (part[0].astype(F32) + part[1].astype(F32)).astype(BF).reshape(YX, 144, 128)
     part = lax.all_to_all(part, ("ylo", "x"), 0, 0)
     part = part.astype(F32).sum(0).astype(BF)

time: 145 us -> 134 us (0.924)
  waiting for transfers between devices: 39.4 us -> 27.7 us
  blocking collectives: 51.6 us -> 53.2 us
    all_gather x1 -> x0, waiting for transfers between devices: 11.7 us -> none  [shards(): part = lax.all_gather(grads, 'core', axis=0, tiled=False)]
    all_to_all x0 -> x1, blocking collectives: none -> 6.33 us  [shards(): part = lax.all_to_all(grads, 'core', 0, 0)]
    all_to_all x1, blocking collectives: 17.2 us -> 12.8 us  [shards(): lax.all_to_all(jnp.broadcast_to(part[None], (NZ, 144, 128)), 'z', 0, 0)]
  transfers between devices with their start and end apart: 5 -> 4, of which waited for: 4 -> 3; matrix products, arithmetic and copies ran while one was open for 3% -> 3% of each run, Pallas kernels for 2% -> 2%
where the time goes in v9:
time: 134 us
  blocking collectives  53.2 us (40%)
  waiting for transfers between devices  27.7 us (21%)
  starting transfers between devices  19.3 us (14%)
  between operations  14.3 us (11%)
  Pallas kernels  13 us (10%)
  other arithmetic  3.62 us (3%)
  local copies, waits for them, and re-layouts  2.26 us (2%)
    all_to_all x1, waiting for transfers between devices, shards(): got = lax.all_to_all(sends, 'z', 0, 0)  13.3 us
    all_to_all x1, blocking collectives, shards(): lax.all_to_all(jnp.broadcast_to(part[None], (NZ, 144, 128)), 'z', 0, 0)  12.8 us
    all_to_all x1, blocking collectives, shards(): part = lax.all_to_all(part, ('ylo', 'x'), 0, 0)  10.7 us
    all_to_all x1, waiting for transfers between devices, shards(): payload = lax.all_to_all(joined, 'chan', 0, 0)  10.1 us
    all_to_all x1, blocking collectives, shards(): lax.all_to_all(jnp.broadcast_to(part[None], (YX, 144, 128)), ('ylo', 'x')...  9.82 us
    all_gather x1, blocking collectives, shards(): units = lax.all_gather(units, 'core', axis=0, tiled=True)  7.67 us
    all_to_all x1, starting transfers between devices, shards(): got = lax.all_to_all(sends, 'z', 0, 0)  7.49 us
    pallas_call x1, Pallas kernels, tiles_call(): pl.pallas_call(main_kernel, out_shape=(jax.ShapeDtypeStruct((TILES_HERE,...  7 us
  transfers between devices with their start and end apart: 4, of which 3 were waited for; matrix products, arithmetic and copies ran while one was open for 3% of the time, Pallas kernels for 2%

profile of v9, /device:TPU:1, one launch (start us, length us, event | category | flops | bytes accessed | tf_op | source)
XLA Modules:
  0.0 133.6 jit_solution(8022800007304150201)
XLA Ops:
  7.2 2.9 %pack.1 = (bf16[3,96,128]{2,1,0:T(8,128)(2,1)}, bf16[8,192,128]{2,1,0:T(8,128)(2,1)}, bf16[9,64,256]{2,1,0:T(8,128)(2,1)}) custom-call(bf16[3,64,144]{2,1,0:T(8,128)(2,1)} %fields_hbm.1, bf16[3,36,64]{2,1,0:T(8,128)(2,1)} %bitcast.35, bf16[9,64,256]{2,1,0:T(8,128)(2,1)} %first_ref.1, bf16[9,64,256]{2,1,0:T(8,128)(2,1)} %down_ref.2), custom_call_target="tpu_custom_call" | custom-call | tf_op jit(solution)/shard_map/pack/pallas_call | solution.py:443
  10.1 5.9 %all-to-all-start = ((bf16[8,192,128]{2,1,0:T(8,128)(2,1)}), bf16[8,192,128]{2,1,0:T(8,128)(2,1)S(1)}, u32[]{:S(2)}, u32[]{:S(2)}) async-start(bf16[8,192,128]{2,1,0:T(8,128)(2,1)} %get-tuple-element.10), calls=%async_computation | async-start | bytes 786432 | tf_op jit(solution)/shard_map/all_to_all | solution.py:463
  16.4 0.2 copy.33
  16.6 0.2 ne.70
  16.8 0.1 copy.38
  17.0 0.1 mul.88
  17.1 0.1 copy.35
  17.2 0.1 div.31
  17.4 0.1 copy.34
  17.5 0.1 rem.82
  17.7 0.1 copy.36
  17.8 0.1 squeeze.6
  18.0 0.1 copy.37
  18.1 0.1 mul.84
  18.3 4.3 %all-to-all-done = bf16[8,192,128]{2,1,0:T(8,128)(2,1)S(1)} async-done(((bf16[8,192,128]{2,1,0:T(8,128)(2,1)}), bf16[8,192,128]{2,1,0:T(8,128)(2,1)S(1)}, u32[]{:S(2)}, u32[]{:S(2)}) %all-to-all-start) | async-done | bytes 393248 | tf_op jit(solution)/shard_map/all_to_all | solution.py:463
  22.6 7.7 %all_gather.12.unit_ref = bf16[3072,128]{1,0:T(8,128)(2,1)S(1)} all-gather(bf16[1536,128]{1,0:T(8,128)(2,1)S(1)} %bitcast.30), channel_id=1, replica_groups=mesh['ylo'=2,'x'=4,'z'=8,'core'=2,'chan'=4] {'core'}, dimensions={0}, use_global_device_ids=true | all-gather | bytes 1179648 | tf_op jit(solution)/shard_map/all_gather | solution.py:464
  30.3 2.3 %place.1 = bf16[8,160,128]{2,1,0:T(8,128)(2,1)} custom-call(s32[1536]{0:T(1024)S(1)} %get-tuple-element.26.word_ref, s32[1536]{0:T(1024)S(1)} %get-tuple-element.25.beyond_ref, bf16[3072,128]{1,0:T(8,128)(2,1)S(1)} %all_gather.12.unit_ref), custom_call_target="tpu_custom_call" | custom-call | tf_op jit(solution)/shard_map/place/pallas_call | solution.py:466
  32.6 7.5 %all-to-all-start.1 = ((bf16[8,160,128]{2,1,0:T(8,128)(2,1)}), bf16[8,160,128]{2,1,0:T(8,128)(2,1)S(1)}, u32[]{:S(2)}, u32[]{:S(2)}) async-start(bf16[8,160,128]{2,1,0:T(8,128)(2,1)} %place.1), calls=%async_computation.1 | async-start | bytes 655360 | tf_op jit(solution)/shard_map/all_to_all | solution.py:475
  40.2 0.2 compare_convert_fusion.1.rim_at_ref
  40.4 13.3 %all-to-all-done.1.got_ref = bf16[8,160,128]{2,1,0:T(8,128)(2,1)S(1)} async-done(((bf16[8,160,128]{2,1,0:T(8,128)(2,1)}), bf16[8,160,128]{2,1,0:T(8,128)(2,1)S(1)}, u32[]{:S(2)}, u32[]{:S(2)}) %all-to-all-start.1) | async-done | bytes 327712 | tf_op jit(solution)/shard_map/all_to_all | solution.py:475
  53.7 0.8 join.1
  54.5 5.8 %all-to-all-start.2 = ((bf16[4,432,128]{2,1,0:T(8,128)(2,1)}), bf16[4,432,128]{2,1,0:T(8,128)(2,1)S(1)}, u32[]{:S(2)}, u32[]{:S(2)}) async-start(bf16[4,432,128]{2,1,0:T(8,128)(2,1)} %join.1), calls=%async_computation.2 | async-start | bytes 884736 | tf_op jit(solution)/shard_map/all_to_all | solution.py:485
  60.4 0.1 convolution_add_fusion
  60.6 1.9 %compare_convert_fusion.window_hbm = bf16[3,1728,256]{2,1,0:T(8,128)(2,1)} fusion(f32[256]{0:T(256)S(1)} %add_convert_fusion.1, f32[3,1728]{1,0:T(4,128)S(1)} %convolution_add_fusion), kind=kLoop, calls=%fused_computation | loop fusion | flops 2654208 | bytes 2675968 | tf_op jit(solution)/shard_map/convert_element_type | solution.py:494
  62.5 10.1 %all-to-all-done.2.pay_ref = bf16[4,432,128]{2,1,0:T(8,128)(2,1)S(1)} async-done(((bf16[4,432,128]{2,1,0:T(8,128)(2,1)}), bf16[4,432,128]{2,1,0:T(8,128)(2,1)S(1)}, u32[]{:S(2)}, u32[]{:S(2)}) %all-to-all-start.2) | async-done | bytes 442400 | tf_op jit(solution)/shard_map/all_to_all | solution.py:485
  72.7 7.0 %tiles.1 = (bf16[3,36,64]{2,1,0:T(8,128)(2,1)}, bf16[3,64,144]{2,1,0:T(8,128)(2,1)}, bf16[2,1152,128]{2,1,0:T(8,128)(2,1)S(1)}) custom-call(bf16[4,432,128]{2,1,0:T(8,128)(2,1)S(1)} %all-to-all-done.2.pay_ref, bf16[3,240,64]{2,1,0:T(8,128)(2,1)S(1)} %compare_convert_fusion.1.rim_at_ref, bf16[160,64]{1,0:T(8,128)(2,1)S(1)} %copy-done.4, ...), custom_call_target="tpu_custom_call" | custom-call | tf_op jit(solution)/shard_map/tiles/pallas_call | solution.py:413
  79.7 6.3 %all_to_all.35 = bf16[2,1152,128]{2,1,0:T(8,128)(2,1)S(1)} all-to-all(bf16[2,1152,128]{2,1,0:T(8,128)(2,1)S(1)} %get-tuple-element.14), channel_id=1, replica_groups=mesh['ylo'=2,'x'=4,'z'=8,'core'=2,'chan'=4] {'core'}, dimensions={0} | all-to-all | bytes 1179648 | tf_op jit(solution)/shard_map/all_to_all | solution.py:498
  86.1 10.7 %all_to_all.36 = bf16[8,144,128]{2,1,0:T(8,128)(2,1)S(1)} all-to-all(bf16[8,144,128]{2,1,0:T(8,128)(2,1)S(1)} %bitcast.31), channel_id=1, replica_groups=mesh['ylo'=2,'x'=4,'z'=8,'core'=2,'chan'=4] {'ylo','x'}, dimensions={0} | all-to-all | bytes 589824 | tf_op jit(solution)/shard_map/all_to_all | solution.py:500
  96.9 12.8 %all_to_all.37 = bf16[8,144,128]{2,1,0:T(8,128)(2,1)S(1)} all-to-all(bf16[8,144,128]{2,1,0:T(8,128)(2,1)S(1)} %broadcast_in_dim.8), channel_id=1, replica_groups=mesh['ylo'=2,'x'=4,'z'=8,'core'=2,'chan'=4] {'z'}, dimensions={0} | all-to-all | bytes 589824 | tf_op jit(solution)/shard_map/all_to_all | solution.py:502
  109.8 9.8 %all_to_all.38 = bf16[8,144,128]{2,1,0:T(8,128)(2,1)S(1)} all-to-all(bf16[8,144,128]{2,1,0:T(8,128)(2,1)S(1)} %broadcast_in_dim.9), channel_id=1, replica_groups=mesh['ylo'=2,'x'=4,'z'=8,'core'=2,'chan'=4] {'ylo','x'}, dimensions={0} | all-to-all | bytes 589824 | tf_op jit(solution)/shard_map/all_to_all | solution.py:504
  119.6 5.8 %all_gather.15 = bf16[2,1152,128]{2,1,0:T(8,128)(2,1)S(1)} all-gather(bf16[1,1152,128]{2,1,0:T(8,128)(2,1)S(1)} %bitcast.32), channel_id=1, replica_groups=mesh['ylo'=2,'x'=4,'z'=8,'core'=2,'chan'=4] {'core'}, dimensions={0}, use_global_device_ids=true | all-gather | bytes 884736 | tf_op jit(solution)/shard_map/all_gather | solution.py:505
  125.6 1.1 slice_multiply_fusion
  (43 shorter events, 1.1 us)
Async XLA Ops:
  7.2 8.8 %copy-start.7 = (s32[384,4,3]{0,1,2:T(4,128)S(1)}, s32[384,4,3]{0,1,2:T(4,128)}, u32[]{:S(2)}) copy-start(s32[384,4,3]{0,1,2:T(4,128)} %param.15) | copy-start | bytes 55300
  7.2 65.5 %all-gather.3.cloned.1.call-start = ((), (), s32[]{:S(2)}) async-start(), calls=%async_computation.7 | async-start | bytes 2654208 | tf_op jit(solution)/shard_map/all_gather | solution.py:462
  10.1 12.5 %all-to-all-start = ((bf16[8,192,128]{2,1,0:T(8,128)(2,1)}), bf16[8,192,128]{2,1,0:T(8,128)(2,1)S(1)}, u32[]{:S(2)}, u32[]{:S(2)}) async-start(bf16[8,192,128]{2,1,0:T(8,128)(2,1)} %get-tuple-element.10), calls=%async_computation | async-start | bytes 786432 | tf_op jit(solution)/shard_map/all_to_all | solution.py:463
  22.6 17.5 %copy-start.8 = (bf16[32,240]{1,0:T(8,128)(2,1)S(1)}, bf16[32,240]{1,0:T(8,128)(2,1)}, u32[]{:S(2)}) copy-start(bf16[32,240]{1,0:T(8,128)(2,1)} %constant.127.clone) | copy-start | bytes 46084
  22.6 31.1 %copy-start.2 = (bf16[3,96,128]{2,1,0:T(8,128)(2,1)S(1)}, bf16[3,96,128]{2,1,0:T(8,128)(2,1)}, u32[]{:S(2)}) copy-start(bf16[3,96,128]{2,1,0:T(8,128)(2,1)} %get-tuple-element.11.own_ref) | copy-start | bytes 221188
  32.6 27.8 %copy-start.6 = (bf16[32,1728]{1,0:T(8,128)(2,1)S(1)}, bf16[32,1728]{1,0:T(8,128)(2,1)}, u32[]{:S(2)}) copy-start(bf16[32,1728]{1,0:T(8,128)(2,1)} %constant.125.clone) | copy-start | bytes 331780
  32.6 27.8 %copy-start.9 = (f32[1728]{0:T(1024)S(1)}, f32[1728]{0:T(1024)}, u32[]{:S(2)}) copy-start(f32[1728]{0:T(1024)} %constant.126.clone) | copy-start | bytes 20740
  32.6 21.1 %all-to-all-start.1 = ((bf16[8,160,128]{2,1,0:T(8,128)(2,1)}), bf16[8,160,128]{2,1,0:T(8,128)(2,1)S(1)}, u32[]{:S(2)}, u32[]{:S(2)}) async-start(bf16[8,160,128]{2,1,0:T(8,128)(2,1)} %place.1), calls=%async_computation.1 | async-start | bytes 655360 | tf_op jit(solution)/shard_map/all_to_all | solution.py:475
  54.5 18.1 %all-to-all-start.2 = ((bf16[4,432,128]{2,1,0:T(8,128)(2,1)}), bf16[4,432,128]{2,1,0:T(8,128)(2,1)S(1)}, u32[]{:S(2)}, u32[]{:S(2)}) async-start(bf16[4,432,128]{2,1,0:T(8,128)(2,1)} %join.1), calls=%async_computation.2 | async-start | bytes 884736 | tf_op jit(solution)/shard_map/all_to_all | solution.py:485
  60.5 12.1 %copy-start = (bf16[432,192]{1,0:T(8,128)(2,1)S(1)}, bf16[432,192]{1,0:T(8,128)(2,1)}, u32[]{:S(2)}) copy-start(bf16[432,192]{1,0:T(8,128)(2,1)} %constant.130.clone.down_ref) | copy-start | bytes 497668
  60.6 12.1 %copy-start.1 = (bf16[160,144]{1,0:T(8,128)(2,1)S(1)}, bf16[160,144]{1,0:T(8,128)(2,1)}, u32[]{:S(2)}) copy-start(bf16[160,144]{1,0:T(8,128)(2,1)} %constant.133.clone.cell_ref) | copy-start | bytes 138244
  60.6 12.1 %copy-start.3 = (bf16[160,48]{1,0:T(8,128)(2,1)S(1)}, bf16[160,48]{1,0:T(8,128)(2,1)}, u32[]{:S(2)}) copy-start(bf16[160,48]{1,0:T(8,128)(2,1)} %constant.131.clone.rim_ref) | copy-start | bytes 46084
  60.6 12.1 %copy-start.4 = (bf16[160,64]{1,0:T(8,128)(2,1)S(1)}, bf16[160,64]{1,0:T(8,128)(2,1)}, u32[]{:S(2)}) copy-start(bf16[160,64]{1,0:T(8,128)(2,1)} %constant.129.clone.shift_ref) | copy-start | bytes 61444
  60.6 12.1 %copy-start.5 = (bf16[48,64]{1,0:T(8,128)(2,1)S(1)}, bf16[48,64]{1,0:T(8,128)(2,1)}, u32[]{:S(2)}) copy-start(bf16[48,64]{1,0:T(8,128)(2,1)} %constant.132.clone.order_ref) | copy-start | bytes 18436
Sparse Core Ops, SparseCore 0:
  10.7 46.5 all-gather.2

commit v10 on v9

--- a/solution.py
+++ b/solution.py
@@ -202,7 +202,7 @@
     return fields, jnp.where(at == cell, 1.0, 0.0).astype(BF)
 
 
-def pack_kernel(fields_hbm, cot_hbm, first_ref, down_ref, own_ref, unit_hbm, half_ref, fields_ref, cot_ref, held, unit_ref, sems):
+def pack_kernel(fields_hbm, cot_hbm, first_ref, down_ref, own_hbm, unit_hbm, half_ref, fields_ref, cot_ref, held, unit_ref, own_ref, sems):
     loads = [
         pltpu.make_async_copy(fields_hbm, fields_ref, sems.at[0]),
         pltpu.make_async_copy(cot_hbm, cot_ref, sems.at[1]),
@@ -231,6 +231,7 @@
     stores = [pltpu.make_async_copy(held, half_ref, sems.at[3])]
     for copy in range(YX):
         stores.append(pltpu.make_async_copy(unit_ref, unit_hbm.at[copy], sems.at[4 + copy]))
+    stores.append(pltpu.make_async_copy(own_ref, own_hbm, sems.at[4 + YX]))
     for store in stores:
         store.start()
     for store in stores:
@@ -300,7 +301,7 @@
 
 def main_kernel(
     pay_ref, rim_at_ref, shift_ref, down_ref, rim_ref, order_ref, cell_ref, window_hbm, weights_ref,
-    coarse_ref, gp_ref, grads_ref, window_ref, xs, cs, wf, wd, wins, ups, rims, downs, gps, up, sems,
+    coarse_ref, gp_ref, kept_ref, given_ref, window_ref, xs, cs, wf, wd, wins, ups, rims, downs, gps, up, sems,
 ):
     window_copies = [
         pltpu.make_async_copy(window_hbm.at[t], window_ref.at[t], sems.at[2 * CHAN + t]) for t in range(TILES_HERE)
@@ -317,7 +318,7 @@
             )
     for copy in copies:
         copy.start()
-    chan = lax.axis_index("chan")
+    chan, core = lax.axis_index("chan"), lax.axis_index("core")
     pick = jnp.where(
         lax.broadcasted_iota(jnp.int32, (CH, C), 1) == lax.broadcasted_iota(jnp.int32, (CH, C), 0) + chan * CH, 1.0, 0.0
     ).astype(BF)
@@ -384,8 +385,10 @@
         for base, left, right in ((0, wins, gps), (9 * CH, downs, up)):
             both = dot_tn(left[:, pl.ds(k * C + lanes, 128)], right[...])
             part = jnp.where(chan % 2 == 0, both[:CH], both[CH:]).astype(BF)
-            for h in range(CORE):
-                grads_ref[h, base + k * CH : base + (k + 1) * CH, :] = part[:, h * 128 : (h + 1) * 128]
+            left_half, right_half = part[:, :128], part[:, 128:]
+            rows = slice(base + k * CH, base + (k + 1) * CH)
+            kept_ref[rows, :] = jnp.where(core == 0, left_half, right_half)
+            given_ref[rows, :] = jnp.where(core == 0, right_half, left_half)
     coarse = dot_nt(dot_nn(downs[...], wd[...].reshape(9 * C, C)).astype(BF), pick).astype(BF)
     for t in range(TILES_HERE):
         coarse_ref[t] = coarse[t * DOWN_ROWS : t * DOWN_ROWS + COARSE]
@@ -415,10 +418,11 @@
         out_shape=(
             jax.ShapeDtypeStruct((TILES_HERE, COARSE, CH), BF),
             jax.ShapeDtypeStruct((TILES_HERE, CH, CELLS), BF),
-            jax.ShapeDtypeStruct((CORE, 18 * CH, 128), BF),
+            jax.ShapeDtypeStruct((18 * CH, 128), BF),
+            jax.ShapeDtypeStruct((18 * CH, 128), BF),
         ),
         in_specs=vmem(7) + hbm(2),
-        out_specs=tuple(vmem(3)),
+        out_specs=tuple(vmem(4)),
         scratch_shapes=[
             pltpu.VMEM((TILES_HERE, 9 * PRE_ROWS, C), BF),
             pltpu.VMEM((TILES_HERE, C, C), BF),
@@ -448,13 +452,14 @@
             jax.ShapeDtypeStruct(w_first.shape, BF),
         ),
         in_specs=hbm(4),
-        out_specs=tuple(vmem(1) + hbm(2)),
+        out_specs=tuple(hbm(3)),
         scratch_shapes=[
             pltpu.VMEM((TILES_HERE, CH, CELLS), BF),
             pltpu.VMEM((TILES_HERE, COARSE, CH), BF),
             pltpu.VMEM((9, CH, C), BF),
             pltpu.VMEM((TILES_HERE * 4 * UNIT, 128), BF),
-            pltpu.SemaphoreType.DMA((4 + YX,)),
+            pltpu.VMEM((TILES_HERE, PACK_ROWS, 128), BF),
+            pltpu.SemaphoreType.DMA((5 + YX,)),
         ],
         compiler_params=WHOLE,
         name="pack",
@@ -493,10 +498,10 @@
         at = jnp.dot(chosen, jnp.asarray(varied, BF), preferred_element_type=F32) + jnp.asarray(fixed, F32)
         one_hots.append((at[:, :, None] == jnp.arange(1, depth + 1, dtype=jnp.int32).astype(F32)).astype(BF))
 
-    coarse, grad_pre, grads = tiles_call(payload, one_hots[0], one_hots[1], weights)
-
-    part = lax.all_to_all(grads, "core", 0, 0)
-    part = (part[0].astype(F32) + part[1].astype(F32)).astype(BF).reshape(YX, 144, 128)
+    coarse, grad_pre, kept, given = tiles_call(payload, one_hots[0], one_hots[1], weights)
+
+    part = lax.ppermute(given, "core", [(0, 1), (1, 0)])
+    part = (kept.astype(F32) + part.astype(F32)).astype(BF).reshape(YX, 144, 128)
     part = lax.all_to_all(part, ("ylo", "x"), 0, 0)
     part = part.astype(F32).sum(0).astype(BF)
     part = lax.all_to_all(jnp.broadcast_to(part[None], (NZ, 144, 128)), "z", 0, 0)

time: 134 us -> 133 us (level)
  blocking collectives: 53.2 us -> 46.8 us
  starting transfers between devices: 19.3 us -> 23.7 us
    all_to_all x1 -> x0, blocking collectives: 6.33 us -> none  [shards(): part = lax.all_to_all(grads, 'core', 0, 0)]
    ppermute x0 -> x1, starting transfers between devices: none -> 4.4 us  [shards(): part = lax.ppermute(given, 'core', [(0, 1), (1, 0)])]
  transfers between devices with their start and end apart: 4 -> 5, of which waited for: 3 -> 4; matrix products, arithmetic and copies ran while one was open for 3% -> 3% of each run, Pallas kernels for 2% -> 2%
where the time goes in v10:
time: 133 us; the launch traced here: 132 us
  blocking collectives  46.8 us (35%)
  waiting for transfers between devices  28.9 us (22%)
  starting transfers between devices  23.7 us (18%)
  between operations  14.3 us (11%)
  Pallas kernels  12.4 us (9%)
  other arithmetic  3.61 us (3%)
  local copies, waits for them, and re-layouts  2.26 us (2%)
    all_to_all x1, waiting for transfers between devices, shards(): got = lax.all_to_all(sends, 'z', 0, 0)  13.3 us
    all_to_all x1, blocking collectives, shards(): lax.all_to_all(jnp.broadcast_to(part[None], (NZ, 144, 128)), 'z', 0, 0)  12.8 us
    all_to_all x1, blocking collectives, shards(): part = lax.all_to_all(part, ('ylo', 'x'), 0, 0)  10.7 us
    all_to_all x1, waiting for transfers between devices, shards(): payload = lax.all_to_all(joined, 'chan', 0, 0)  10.1 us
    all_to_all x1, blocking collectives, shards(): lax.all_to_all(jnp.broadcast_to(part[None], (YX, 144, 128)), ('ylo', 'x')...  9.82 us
    all_gather x1, blocking collectives, shards(): units = lax.all_gather(units, 'core', axis=0, tiled=True)  7.67 us
    all_to_all x1, starting transfers between devices, shards(): got = lax.all_to_all(sends, 'z', 0, 0)  7.42 us
    pallas_call x1, Pallas kernels, tiles_call(): pl.pallas_call(main_kernel, out_shape=(jax.ShapeDtypeStruct((TILES_HERE,...  7.01 us
  transfers between devices with their start and end apart: 5, of which 4 were waited for; matrix products, arithmetic and copies ran while one was open for 3% of the time, Pallas kernels for 2%

profile of v10, /device:TPU:1, one launch (start us, length us, event | category | flops | bytes accessed | tf_op | source)
XLA Modules:
  0.0 132.2 jit_solution(12979964123122070843)
XLA Ops:
  7.2 2.3 %pack.1 = (bf16[3,96,128]{2,1,0:T(8,128)(2,1)}, bf16[8,192,128]{2,1,0:T(8,128)(2,1)}, bf16[9,64,256]{2,1,0:T(8,128)(2,1)}) custom-call(bf16[3,64,144]{2,1,0:T(8,128)(2,1)} %fields_hbm.1, bf16[3,36,64]{2,1,0:T(8,128)(2,1)} %bitcast.35, bf16[9,64,256]{2,1,0:T(8,128)(2,1)} %first_ref.1, bf16[9,64,256]{2,1,0:T(8,128)(2,1)} %down_ref.2), custom_call_target="tpu_custom_call" | custom-call | tf_op jit(solution)/shard_map/pack/pallas_call | solution.py:447
  9.5 5.9 %all-to-all-start = ((bf16[8,192,128]{2,1,0:T(8,128)(2,1)}), bf16[8,192,128]{2,1,0:T(8,128)(2,1)S(1)}, u32[]{:S(2)}, u32[]{:S(2)}) async-start(bf16[8,192,128]{2,1,0:T(8,128)(2,1)} %get-tuple-element.11), calls=%async_computation | async-start | bytes 786432 | tf_op jit(solution)/shard_map/all_to_all | solution.py:468
  15.8 0.2 copy.33
  16.0 0.2 ne.70
  16.2 0.1 copy.38
  16.4 0.1 mul.88
  16.5 0.1 copy.35
  16.6 0.1 div.31
  16.8 0.1 copy.34
  16.9 0.1 rem.82
  17.1 0.1 copy.36
  17.2 0.1 squeeze.6
  17.4 0.1 copy.37
  17.5 0.1 mul.84
  17.7 4.3 %all-to-all-done = bf16[8,192,128]{2,1,0:T(8,128)(2,1)S(1)} async-done(((bf16[8,192,128]{2,1,0:T(8,128)(2,1)}), bf16[8,192,128]{2,1,0:T(8,128)(2,1)S(1)}, u32[]{:S(2)}, u32[]{:S(2)}) %all-to-all-start) | async-done | bytes 393248 | tf_op jit(solution)/shard_map/all_to_all | solution.py:468
  22.0 7.7 %all_gather.12.unit_ref = bf16[3072,128]{1,0:T(8,128)(2,1)S(1)} all-gather(bf16[1536,128]{1,0:T(8,128)(2,1)S(1)} %bitcast.30), channel_id=1, replica_groups=mesh['ylo'=2,'x'=4,'z'=8,'core'=2,'chan'=4] {'core'}, dimensions={0}, use_global_device_ids=true | all-gather | bytes 1179648 | tf_op jit(solution)/shard_map/all_gather | solution.py:469
  29.7 2.3 %place.1 = bf16[8,160,128]{2,1,0:T(8,128)(2,1)} custom-call(s32[1536]{0:T(1024)S(1)} %get-tuple-element.28.word_ref, s32[1536]{0:T(1024)S(1)} %get-tuple-element.27.beyond_ref, bf16[3072,128]{1,0:T(8,128)(2,1)S(1)} %all_gather.12.unit_ref), custom_call_target="tpu_custom_call" | custom-call | tf_op jit(solution)/shard_map/place/pallas_call | solution.py:471
  32.0 7.4 %all-to-all-start.1 = ((bf16[8,160,128]{2,1,0:T(8,128)(2,1)}), bf16[8,160,128]{2,1,0:T(8,128)(2,1)S(1)}, u32[]{:S(2)}, u32[]{:S(2)}) async-start(bf16[8,160,128]{2,1,0:T(8,128)(2,1)} %place.1), calls=%async_computation.1 | async-start | bytes 655360 | tf_op jit(solution)/shard_map/all_to_all | solution.py:480
  39.6 0.2 compare_convert_fusion.1.rim_at_ref
  39.7 13.3 %all-to-all-done.1.got_ref = bf16[8,160,128]{2,1,0:T(8,128)(2,1)S(1)} async-done(((bf16[8,160,128]{2,1,0:T(8,128)(2,1)}), bf16[8,160,128]{2,1,0:T(8,128)(2,1)S(1)}, u32[]{:S(2)}, u32[]{:S(2)}) %all-to-all-start.1) | async-done | bytes 327712 | tf_op jit(solution)/shard_map/all_to_all | solution.py:480
  53.1 0.8 join.1
  53.9 5.9 %all-to-all-start.2 = ((bf16[4,432,128]{2,1,0:T(8,128)(2,1)}), bf16[4,432,128]{2,1,0:T(8,128)(2,1)S(1)}, u32[]{:S(2)}, u32[]{:S(2)}) async-start(bf16[4,432,128]{2,1,0:T(8,128)(2,1)} %join.1), calls=%async_computation.2 | async-start | bytes 884736 | tf_op jit(solution)/shard_map/all_to_all | solution.py:490
  60.0 1.9 %compare_convert_fusion.window_hbm = bf16[3,1728,256]{2,1,0:T(8,128)(2,1)} fusion(f32[256]{0:T(256)S(1)} %add_convert_fusion.1, f32[3,1728]{1,0:T(4,128)S(1)} %convolution_add_fusion), kind=kLoop, calls=%fused_computation | loop fusion | flops 2654208 | bytes 2675968 | tf_op jit(solution)/shard_map/convert_element_type | solution.py:499
  61.9 10.1 %all-to-all-done.2.pay_ref = bf16[4,432,128]{2,1,0:T(8,128)(2,1)S(1)} async-done(((bf16[4,432,128]{2,1,0:T(8,128)(2,1)}), bf16[4,432,128]{2,1,0:T(8,128)(2,1)S(1)}, u32[]{:S(2)}, u32[]{:S(2)}) %all-to-all-start.2) | async-done | bytes 442400 | tf_op jit(solution)/shard_map/all_to_all | solution.py:490
  72.1 7.0 %tiles.1 = (bf16[3,36,64]{2,1,0:T(8,128)(2,1)}, bf16[3,64,144]{2,1,0:T(8,128)(2,1)}, bf16[1152,128]{1,0:T(8,128)(2,1)S(1)}, bf16[1152,128]{1,0:T(8,128)(2,1)S(1)}) custom-call(bf16[4,432,128]{2,1,0:T(8,128)(2,1)S(1)} %all-to-all-done.2.pay_ref, bf16[3,240,64]{2,1,0:T(8,128)(2,1)S(1)} %compare_convert_fusion.1.rim_at_ref, bf16[160,64]{1,0:T(8,128)(2,1)S(1)} %copy-done.4, ...), custom_call_target="tpu_custom_call" | custom-call | tf_op jit(solution)/shard_map/tiles/pallas_call | solution.py:416
  79.1 4.4 %collective-permute-start = (bf16[1152,128]{1,0:T(8,128)(2,1)S(1)}, bf16[1152,128]{1,0:T(8,128)(2,1)S(1)}, u32[]{:S(2)}, u32[]{:S(2)}) collective-permute-start(bf16[1152,128]{1,0:T(8,128)(2,1)S(1)} %get-tuple-element.16), channel_id=1, source_target_pairs={{0,4},{4,0},{1,5},{5,1},{2,6},{6,2},{3,7},{7,3},{8,12},{12,8},{9,1... | collective-permute-start | bytes 884744 | tf_op jit(solution)/shard_map/ppermute | solution.py:503
  83.5 1.2 collective-permute-done
  84.8 10.7 %all_to_all.30 = bf16[8,144,128]{2,1,0:T(8,128)(2,1)S(1)} all-to-all(bf16[8,144,128]{2,1,0:T(8,128)(2,1)S(1)} %bitcast.31), channel_id=1, replica_groups=mesh['ylo'=2,'x'=4,'z'=8,'core'=2,'chan'=4] {'ylo','x'}, dimensions={0} | all-to-all | bytes 589824 | tf_op jit(solution)/shard_map/all_to_all | solution.py:505
  95.6 12.8 %all_to_all.31 = bf16[8,144,128]{2,1,0:T(8,128)(2,1)S(1)} all-to-all(bf16[8,144,128]{2,1,0:T(8,128)(2,1)S(1)} %broadcast_in_dim.8), channel_id=1, replica_groups=mesh['ylo'=2,'x'=4,'z'=8,'core'=2,'chan'=4] {'z'}, dimensions={0} | all-to-all | bytes 589824 | tf_op jit(solution)/shard_map/all_to_all | solution.py:507
  108.5 9.8 %all_to_all.32 = bf16[8,144,128]{2,1,0:T(8,128)(2,1)S(1)} all-to-all(bf16[8,144,128]{2,1,0:T(8,128)(2,1)S(1)} %broadcast_in_dim.9), channel_id=1, replica_groups=mesh['ylo'=2,'x'=4,'z'=8,'core'=2,'chan'=4] {'ylo','x'}, dimensions={0} | all-to-all | bytes 589824 | tf_op jit(solution)/shard_map/all_to_all | solution.py:509
  118.3 5.8 %all_gather.15 = bf16[2,1152,128]{2,1,0:T(8,128)(2,1)S(1)} all-gather(bf16[1,1152,128]{2,1,0:T(8,128)(2,1)S(1)} %bitcast.32), channel_id=1, replica_groups=mesh['ylo'=2,'x'=4,'z'=8,'core'=2,'chan'=4] {'core'}, dimensions={0}, use_global_device_ids=true | all-gather | bytes 884736 | tf_op jit(solution)/shard_map/all_gather | solution.py:510
  124.3 1.1 slice_multiply_fusion
  (44 shorter events, 1.2 us)
Async XLA Ops:
  7.2 8.2 %copy-start.7 = (s32[384,4,3]{0,1,2:T(4,128)S(1)}, s32[384,4,3]{0,1,2:T(4,128)}, u32[]{:S(2)}) copy-start(s32[384,4,3]{0,1,2:T(4,128)} %param.15) | copy-start | bytes 55300
  7.2 64.9 %all-gather.3.cloned.1.call-start = ((), (), s32[]{:S(2)}) async-start(), calls=%async_computation.6 | async-start | bytes 2654208 | tf_op jit(solution)/shard_map/all_gather | solution.py:467
  9.5 12.5 %all-to-all-start = ((bf16[8,192,128]{2,1,0:T(8,128)(2,1)}), bf16[8,192,128]{2,1,0:T(8,128)(2,1)S(1)}, u32[]{:S(2)}, u32[]{:S(2)}) async-start(bf16[8,192,128]{2,1,0:T(8,128)(2,1)} %get-tuple-element.11), calls=%async_computation | async-start | bytes 786432 | tf_op jit(solution)/shard_map/all_to_all | solution.py:468
  22.0 17.5 %copy-start.8 = (bf16[32,240]{1,0:T(8,128)(2,1)S(1)}, bf16[32,240]{1,0:T(8,128)(2,1)}, u32[]{:S(2)}) copy-start(bf16[32,240]{1,0:T(8,128)(2,1)} %constant.127.clone) | copy-start | bytes 46084
  22.0 31.1 %copy-start.2 = (bf16[3,96,128]{2,1,0:T(8,128)(2,1)S(1)}, bf16[3,96,128]{2,1,0:T(8,128)(2,1)}, u32[]{:S(2)}) copy-start(bf16[3,96,128]{2,1,0:T(8,128)(2,1)} %get-tuple-element.12.own_ref) | copy-start | bytes 221188
  32.0 27.8 %copy-start.6 = (bf16[32,1728]{1,0:T(8,128)(2,1)S(1)}, bf16[32,1728]{1,0:T(8,128)(2,1)}, u32[]{:S(2)}) copy-start(bf16[32,1728]{1,0:T(8,128)(2,1)} %constant.125.clone) | copy-start | bytes 331780
  32.0 27.8 %copy-start.9 = (f32[1728]{0:T(1024)S(1)}, f32[1728]{0:T(1024)}, u32[]{:S(2)}) copy-start(f32[1728]{0:T(1024)} %constant.126.clone) | copy-start | bytes 20740
  32.0 21.0 %all-to-all-start.1 = ((bf16[8,160,128]{2,1,0:T(8,128)(2,1)}), bf16[8,160,128]{2,1,0:T(8,128)(2,1)S(1)}, u32[]{:S(2)}, u32[]{:S(2)}) async-start(bf16[8,160,128]{2,1,0:T(8,128)(2,1)} %place.1), calls=%async_computation.1 | async-start | bytes 655360 | tf_op jit(solution)/shard_map/all_to_all | solution.py:480
  53.9 18.2 %all-to-all-start.2 = ((bf16[4,432,128]{2,1,0:T(8,128)(2,1)}), bf16[4,432,128]{2,1,0:T(8,128)(2,1)S(1)}, u32[]{:S(2)}, u32[]{:S(2)}) async-start(bf16[4,432,128]{2,1,0:T(8,128)(2,1)} %join.1), calls=%async_computation.2 | async-start | bytes 884736 | tf_op jit(solution)/shard_map/all_to_all | solution.py:490
  59.9 12.1 %copy-start = (bf16[432,192]{1,0:T(8,128)(2,1)S(1)}, bf16[432,192]{1,0:T(8,128)(2,1)}, u32[]{:S(2)}) copy-start(bf16[432,192]{1,0:T(8,128)(2,1)} %constant.130.clone.down_ref) | copy-start | bytes 497668
  60.0 12.1 %copy-start.1 = (bf16[160,144]{1,0:T(8,128)(2,1)S(1)}, bf16[160,144]{1,0:T(8,128)(2,1)}, u32[]{:S(2)}) copy-start(bf16[160,144]{1,0:T(8,128)(2,1)} %constant.133.clone.cell_ref) | copy-start | bytes 138244
  60.0 12.1 %copy-start.3 = (bf16[160,48]{1,0:T(8,128)(2,1)S(1)}, bf16[160,48]{1,0:T(8,128)(2,1)}, u32[]{:S(2)}) copy-start(bf16[160,48]{1,0:T(8,128)(2,1)} %constant.131.clone.rim_ref) | copy-start | bytes 46084
  60.0 12.1 %copy-start.4 = (bf16[160,64]{1,0:T(8,128)(2,1)S(1)}, bf16[160,64]{1,0:T(8,128)(2,1)}, u32[]{:S(2)}) copy-start(bf16[160,64]{1,0:T(8,128)(2,1)} %constant.129.clone.shift_ref) | copy-start | bytes 61444
  60.0 12.1 %copy-start.5 = (bf16[48,64]{1,0:T(8,128)(2,1)S(1)}, bf16[48,64]{1,0:T(8,128)(2,1)}, u32[]{:S(2)}) copy-start(bf16[48,64]{1,0:T(8,128)(2,1)} %constant.132.clone.order_ref) | copy-start | bytes 18436
  79.1 5.6 %collective-permute-start = (bf16[1152,128]{1,0:T(8,128)(2,1)S(1)}, bf16[1152,128]{1,0:T(8,128)(2,1)S(1)}, u32[]{:S(2)}, u32[]{:S(2)}) collective-permute-start(bf16[1152,128]{1,0:T(8,128)(2,1)S(1)} %get-tuple-element.16), channel_id=1, source_target_pairs={{0,4},{4,0},{1,5},{5,1},{2,6},{6,2},{3,7},{7,3},{8,12},{12,8},{9,1... | collective-permute-start | bytes 884744 | tf_op jit(solution)/shard_map/ppermute | solution.py:503
Sparse Core Ops, SparseCore 0:
  10.7 46.5 all-gather.2

commit v11 on v10

--- a/solution.py
+++ b/solution.py
@@ -299,15 +299,7 @@
         out_ref[c] = whole
 
 
-def main_kernel(
-    pay_ref, rim_at_ref, shift_ref, down_ref, rim_ref, order_ref, cell_ref, window_hbm, weights_ref,
-    coarse_ref, gp_ref, kept_ref, given_ref, window_ref, xs, cs, wf, wd, wins, ups, rims, downs, gps, up, sems,
-):
-    window_copies = [
-        pltpu.make_async_copy(window_hbm.at[t], window_ref.at[t], sems.at[2 * CHAN + t]) for t in range(TILES_HERE)
-    ]
-    for copy in window_copies:
-        copy.start()
+def hold_kernel(weights_ref, wf, wd, sems):
     copies = []
     for which, held in enumerate((wf, wd)):
         for c in range(CHAN):
@@ -317,6 +309,19 @@
                 )
             )
     for copy in copies:
+        copy.start()
+    for copy in copies:
+        copy.wait()
+
+
+def main_kernel(
+    pay_ref, rim_at_ref, shift_ref, down_ref, rim_ref, order_ref, cell_ref, wf, wd, window_hbm,
+    coarse_ref, gp_ref, kept_ref, given_ref, window_ref, xs, cs, wins, ups, rims, downs, gps, up, sems,
+):
+    window_copies = [
+        pltpu.make_async_copy(window_hbm.at[t], window_ref.at[t], sems.at[t]) for t in range(TILES_HERE)
+    ]
+    for copy in window_copies:
         copy.start()
     chan, core = lax.axis_index("chan"), lax.axis_index("core")
     pick = jnp.where(
@@ -345,8 +350,6 @@
         near = dot_nn(rim_at_ref[t], cs[t]).astype(BF)
         for s in range(len(RIM_TAPS)):
             rims[s, t * RIM_ROWS : (t + 1) * RIM_ROWS, :] = near[s * RIM_ROWS : (s + 1) * RIM_ROWS]
-    for copy in copies:
-        copy.wait()
     pre = dot_nn(wins[...], wf[...].reshape(9 * C, C))
     ups_low = [ups[s].astype(BF) for s in range(4)]
     blocks = (
@@ -408,10 +411,20 @@
 
 LIMIT = pltpu.CompilerParams(vmem_limit_bytes=48 * 1024 * 1024)
 WHOLE = pltpu.CompilerParams(vmem_limit_bytes=60 * 1024 * 1024)
-MOST = pltpu.CompilerParams(vmem_limit_bytes=52 * 1024 * 1024)
+MOST = pltpu.CompilerParams(vmem_limit_bytes=50 * 1024 * 1024)
 
 
 def tiles_call(payload, window, rim_at, weights):
+    held = pl.pallas_call(
+        hold_kernel,
+        out_shape=(jax.ShapeDtypeStruct((9, C, C), BF), jax.ShapeDtypeStruct((9, C, C), BF)),
+        in_specs=hbm(1),
+        out_specs=tuple(vmem(2)),
+        scratch_shapes=[pltpu.SemaphoreType.DMA((2 * CHAN,))],
+        compiler_params=MOST,
+        cost_estimate=pl.CostEstimate(flops=0, bytes_accessed=2 * 18 * C * C * 2, transcendentals=0),
+        name="hold",
+    )(weights)
     constants = (shift_selector(), down_selector(), rim_selector(), order_selector(), cell_selector())
     return pl.pallas_call(
         main_kernel,
@@ -421,25 +434,23 @@
             jax.ShapeDtypeStruct((18 * CH, 128), BF),
             jax.ShapeDtypeStruct((18 * CH, 128), BF),
         ),
-        in_specs=vmem(7) + hbm(2),
+        in_specs=vmem(9) + hbm(1),
         out_specs=tuple(vmem(4)),
         scratch_shapes=[
             pltpu.VMEM((TILES_HERE, 9 * PRE_ROWS, C), BF),
             pltpu.VMEM((TILES_HERE, C, C), BF),
             pltpu.VMEM((TILES_HERE, 2 * C_HALF, C), BF),
-            pltpu.VMEM((9, C, C), BF),
-            pltpu.VMEM((9, C, C), BF),
             pltpu.VMEM((TILES_HERE * PRE_ROWS, 9 * C), BF),
             pltpu.VMEM((4, TILES_HERE * PART, C), F32),
             pltpu.VMEM((len(RIM_TAPS), TILES_HERE * RIM_ROWS, C), BF),
             pltpu.VMEM((TILES_HERE * DOWN_ROWS, 9 * C), BF),
             pltpu.VMEM((TILES_HERE * PRE_ROWS, C), BF),
             pltpu.VMEM((TILES_HERE * DOWN_ROWS, C), BF),
-            pltpu.SemaphoreType.DMA((2 * CHAN + TILES_HERE,)),
+            pltpu.SemaphoreType.DMA((TILES_HERE,)),
         ],
         compiler_params=MOST,
         name="tiles",
-    )(payload, rim_at, *(jnp.asarray(array, BF) for array in constants), window, weights)
+    )(payload, rim_at, *(jnp.asarray(array, BF) for array in constants), *held, window)
 
 
 def shards(fields, seam_table, w_first, w_down, cotangent):

time: 133 us -> 132 us (level)
  waiting for transfers between devices: 28.9 us -> 27.3 us
  Pallas kernels: 12.4 us -> 13.9 us
    pallas_call x0 -> x1, Pallas kernels: none -> 1.7 us  [tiles_call(): pl.pallas_call(hold_kernel, out_shape=(jax.ShapeDtypeStruct((9, C, C), BF...]
    all_to_all x1, waiting for transfers between devices: 10.1 us -> 8.47 us  [shards(): payload = lax.all_to_all(joined, 'chan', 0, 0)]
  transfers between devices with their start and end apart: 5 -> 5, of which waited for: 4 -> 4; matrix products, arithmetic and copies ran while one was open for 3% -> 3% of each run, Pallas kernels for 2% -> 4%
where the time goes in v11:
time: 132 us
  blocking collectives  46.7 us (35%)
  waiting for transfers between devices  27.3 us (21%)
  starting transfers between devices  23.7 us (18%)
  between operations  14.3 us (11%)
  Pallas kernels  13.9 us (11%)
  other arithmetic  3.61 us (3%)
  local copies, waits for them, and re-layouts  2.25 us (2%)
    all_to_all x1, waiting for transfers between devices, shards(): got = lax.all_to_all(sends, 'z', 0, 0)  13.3 us
    all_to_all x1, blocking collectives, shards(): lax.all_to_all(jnp.broadcast_to(part[None], (NZ, 144, 128)), 'z', 0, 0)  12.8 us
    all_to_all x1, blocking collectives, shards(): part = lax.all_to_all(part, ('ylo', 'x'), 0, 0)  10.7 us
    all_to_all x1, blocking collectives, shards(): lax.all_to_all(jnp.broadcast_to(part[None], (YX, 144, 128)), ('ylo', 'x')...  9.82 us
    all_to_all x1, waiting for transfers between devices, shards(): payload = lax.all_to_all(joined, 'chan', 0, 0)  8.47 us
    all_gather x1, blocking collectives, shards(): units = lax.all_gather(units, 'core', axis=0, tiled=True)  7.54 us
    all_to_all x1, starting transfers between devices, shards(): got = lax.all_to_all(sends, 'z', 0, 0)  7.42 us
    pallas_call x1, Pallas kernels, tiles_call(): pl.pallas_call(main_kernel, out_shape=(jax.ShapeDtypeStruct((TILES_HERE,...  6.76 us
  transfers between devices with their start and end apart: 5, of which 4 were waited for; matrix products, arithmetic and copies ran while one was open for 3% of the time, Pallas kernels for 4%

profile of v11, /device:TPU:1, one launch (start us, length us, event | category | flops | bytes accessed | tf_op | source)
XLA Modules:
  0.0 131.8 jit_solution(12568988244044717152)
XLA Ops:
  7.2 2.3 %pack.1 = (bf16[3,96,128]{2,1,0:T(8,128)(2,1)}, bf16[8,192,128]{2,1,0:T(8,128)(2,1)}, bf16[9,64,256]{2,1,0:T(8,128)(2,1)}) custom-call(bf16[3,64,144]{2,1,0:T(8,128)(2,1)} %fields_hbm.1, bf16[3,36,64]{2,1,0:T(8,128)(2,1)} %bitcast.35, bf16[9,64,256]{2,1,0:T(8,128)(2,1)} %first_ref.1, bf16[9,64,256]{2,1,0:T(8,128)(2,1)} %down_ref.2), custom_call_target="tpu_custom_call" | custom-call | tf_op jit(solution)/shard_map/pack/pallas_call | solution.py:458
  9.5 5.9 %all-to-all-start = ((bf16[8,192,128]{2,1,0:T(8,128)(2,1)}), bf16[8,192,128]{2,1,0:T(8,128)(2,1)S(1)}, u32[]{:S(2)}, u32[]{:S(2)}) async-start(bf16[8,192,128]{2,1,0:T(8,128)(2,1)} %get-tuple-element.13), calls=%async_computation | async-start | bytes 786432 | tf_op jit(solution)/shard_map/all_to_all | solution.py:479
  15.8 0.2 copy.33
  16.0 0.2 ne.70
  16.4 0.1 mul.88
  16.5 0.1 copy.35
  16.6 0.1 div.31
  16.8 0.1 copy.34
  16.9 0.1 rem.82
  17.1 0.1 copy.36
  17.2 0.1 squeeze.6
  17.4 0.1 copy.37
  17.5 0.1 mul.84
  17.7 4.3 %all-to-all-done = bf16[8,192,128]{2,1,0:T(8,128)(2,1)S(1)} async-done(((bf16[8,192,128]{2,1,0:T(8,128)(2,1)}), bf16[8,192,128]{2,1,0:T(8,128)(2,1)S(1)}, u32[]{:S(2)}, u32[]{:S(2)}) %all-to-all-start) | async-done | bytes 393248 | tf_op jit(solution)/shard_map/all_to_all | solution.py:479
  22.0 7.5 %all_gather.12.unit_ref = bf16[3072,128]{1,0:T(8,128)(2,1)S(1)} all-gather(bf16[1536,128]{1,0:T(8,128)(2,1)S(1)} %bitcast.30), channel_id=1, replica_groups=mesh['ylo'=2,'x'=4,'z'=8,'core'=2,'chan'=4] {'core'}, dimensions={0}, use_global_device_ids=true | all-gather | bytes 1179648 | tf_op jit(solution)/shard_map/all_gather | solution.py:480
  29.5 2.3 %place.1 = bf16[8,160,128]{2,1,0:T(8,128)(2,1)} custom-call(s32[1536]{0:T(1024)S(1)} %get-tuple-element.32.word_ref, s32[1536]{0:T(1024)S(1)} %get-tuple-element.31.beyond_ref, bf16[3072,128]{1,0:T(8,128)(2,1)S(1)} %all_gather.12.unit_ref), custom_call_target="tpu_custom_call" | custom-call | tf_op jit(solution)/shard_map/place/pallas_call | solution.py:482
  31.9 7.4 %all-to-all-start.1 = ((bf16[8,160,128]{2,1,0:T(8,128)(2,1)}), bf16[8,160,128]{2,1,0:T(8,128)(2,1)S(1)}, u32[]{:S(2)}, u32[]{:S(2)}) async-start(bf16[8,160,128]{2,1,0:T(8,128)(2,1)} %place.1), calls=%async_computation.1 | async-start | bytes 655360 | tf_op jit(solution)/shard_map/all_to_all | solution.py:491
  39.4 0.2 compare_convert_fusion.1.rim_at_ref
  39.6 13.3 %all-to-all-done.1.got_ref = bf16[8,160,128]{2,1,0:T(8,128)(2,1)S(1)} async-done(((bf16[8,160,128]{2,1,0:T(8,128)(2,1)}), bf16[8,160,128]{2,1,0:T(8,128)(2,1)S(1)}, u32[]{:S(2)}, u32[]{:S(2)}) %all-to-all-start.1) | async-done | bytes 327712 | tf_op jit(solution)/shard_map/all_to_all | solution.py:491
  52.9 0.8 join.1
  53.7 5.9 %all-to-all-start.2 = ((bf16[4,432,128]{2,1,0:T(8,128)(2,1)}), bf16[4,432,128]{2,1,0:T(8,128)(2,1)S(1)}, u32[]{:S(2)}, u32[]{:S(2)}) async-start(bf16[4,432,128]{2,1,0:T(8,128)(2,1)} %join.1), calls=%async_computation.2 | async-start | bytes 884736 | tf_op jit(solution)/shard_map/all_to_all | solution.py:501
  59.8 1.9 %compare_convert_fusion.window_hbm = bf16[3,1728,256]{2,1,0:T(8,128)(2,1)} fusion(f32[256]{0:T(256)S(1)} %add_convert_fusion.1, f32[3,1728]{1,0:T(4,128)S(1)} %convolution_add_fusion), kind=kLoop, calls=%fused_computation | loop fusion | flops 2654208 | bytes 2675968 | tf_op jit(solution)/shard_map/convert_element_type | solution.py:510
  61.8 1.7 %hold.1 = (bf16[9,256,256]{2,1,0:T(8,128)(2,1)S(1)}, bf16[9,256,256]{2,1,0:T(8,128)(2,1)S(1)}) custom-call(bf16[8,9,64,256]{3,2,1,0:T(8,128)(2,1)} %bitcast.29), custom_call_target="tpu_custom_call" | custom-call | bytes 4718592 | tf_op jit(solution)/shard_map/hold/pallas_call | solution.py:418
  63.5 8.5 %all-to-all-done.2.pay_ref = bf16[4,432,128]{2,1,0:T(8,128)(2,1)S(1)} async-done(((bf16[4,432,128]{2,1,0:T(8,128)(2,1)}), bf16[4,432,128]{2,1,0:T(8,128)(2,1)S(1)}, u32[]{:S(2)}, u32[]{:S(2)}) %all-to-all-start.2) | async-done | bytes 442400 | tf_op jit(solution)/shard_map/all_to_all | solution.py:501
  72.0 6.8 %tiles.1 = (bf16[3,36,64]{2,1,0:T(8,128)(2,1)}, bf16[3,64,144]{2,1,0:T(8,128)(2,1)}, bf16[1152,128]{1,0:T(8,128)(2,1)S(1)}, bf16[1152,128]{1,0:T(8,128)(2,1)S(1)}) custom-call(bf16[4,432,128]{2,1,0:T(8,128)(2,1)S(1)} %all-to-all-done.2.pay_ref, bf16[3,240,64]{2,1,0:T(8,128)(2,1)S(1)} %compare_convert_fusion.1.rim_at_ref, bf16[160,64]{1,0:T(8,128)(2,1)S(1)} %copy-done.4, ...), custom_call_target="tpu_custom_call" | custom-call | tf_op jit(solution)/shard_map/tiles/pallas_call | solution.py:429
  78.8 4.4 %collective-permute-start = (bf16[1152,128]{1,0:T(8,128)(2,1)S(1)}, bf16[1152,128]{1,0:T(8,128)(2,1)S(1)}, u32[]{:S(2)}, u32[]{:S(2)}) collective-permute-start(bf16[1152,128]{1,0:T(8,128)(2,1)S(1)} %get-tuple-element.20), channel_id=1, source_target_pairs={{0,4},{4,0},{1,5},{5,1},{2,6},{6,2},{3,7},{7,3},{8,12},{12,8},{9,1... | collective-permute-start | bytes 884744 | tf_op jit(solution)/shard_map/ppermute | solution.py:514
  83.2 1.2 collective-permute-done
  84.4 10.7 %all_to_all.30 = bf16[8,144,128]{2,1,0:T(8,128)(2,1)S(1)} all-to-all(bf16[8,144,128]{2,1,0:T(8,128)(2,1)S(1)} %bitcast.31), channel_id=1, replica_groups=mesh['ylo'=2,'x'=4,'z'=8,'core'=2,'chan'=4] {'ylo','x'}, dimensions={0} | all-to-all | bytes 589824 | tf_op jit(solution)/shard_map/all_to_all | solution.py:516
  95.2 12.8 %all_to_all.31 = bf16[8,144,128]{2,1,0:T(8,128)(2,1)S(1)} all-to-all(bf16[8,144,128]{2,1,0:T(8,128)(2,1)S(1)} %broadcast_in_dim.8), channel_id=1, replica_groups=mesh['ylo'=2,'x'=4,'z'=8,'core'=2,'chan'=4] {'z'}, dimensions={0} | all-to-all | bytes 589824 | tf_op jit(solution)/shard_map/all_to_all | solution.py:518
  108.1 9.8 %all_to_all.32 = bf16[8,144,128]{2,1,0:T(8,128)(2,1)S(1)} all-to-all(bf16[8,144,128]{2,1,0:T(8,128)(2,1)S(1)} %broadcast_in_dim.9), channel_id=1, replica_groups=mesh['ylo'=2,'x'=4,'z'=8,'core'=2,'chan'=4] {'ylo','x'}, dimensions={0} | all-to-all | bytes 589824 | tf_op jit(solution)/shard_map/all_to_all | solution.py:520
  117.9 5.8 %all_gather.15 = bf16[2,1152,128]{2,1,0:T(8,128)(2,1)S(1)} all-gather(bf16[1,1152,128]{2,1,0:T(8,128)(2,1)S(1)} %bitcast.32), channel_id=1, replica_groups=mesh['ylo'=2,'x'=4,'z'=8,'core'=2,'chan'=4] {'core'}, dimensions={0}, use_global_device_ids=true | all-gather | bytes 884736 | tf_op jit(solution)/shard_map/all_gather | solution.py:521
  123.9 1.1 slice_multiply_fusion
  (45 shorter events, 1.3 us)
Async XLA Ops:
  7.2 8.2 %copy-start.7 = (s32[384,4,3]{0,1,2:T(4,128)S(1)}, s32[384,4,3]{0,1,2:T(4,128)}, u32[]{:S(2)}) copy-start(s32[384,4,3]{0,1,2:T(4,128)} %param.15) | copy-start | bytes 55300
  7.2 54.6 %all-gather.3.cloned.1.call-start = ((), (), s32[]{:S(2)}) async-start(), calls=%async_computation.6 | async-start | bytes 2654208 | tf_op jit(solution)/shard_map/all_gather | solution.py:478
  9.5 12.5 %all-to-all-start = ((bf16[8,192,128]{2,1,0:T(8,128)(2,1)}), bf16[8,192,128]{2,1,0:T(8,128)(2,1)S(1)}, u32[]{:S(2)}, u32[]{:S(2)}) async-start(bf16[8,192,128]{2,1,0:T(8,128)(2,1)} %get-tuple-element.13), calls=%async_computation | async-start | bytes 786432 | tf_op jit(solution)/shard_map/all_to_all | solution.py:479
  29.5 9.8 %copy-start.8 = (bf16[32,240]{1,0:T(8,128)(2,1)S(1)}, bf16[32,240]{1,0:T(8,128)(2,1)}, u32[]{:S(2)}) copy-start(bf16[32,240]{1,0:T(8,128)(2,1)} %constant.127.clone) | copy-start | bytes 46084
  29.5 23.4 %copy-start.2 = (bf16[3,96,128]{2,1,0:T(8,128)(2,1)S(1)}, bf16[3,96,128]{2,1,0:T(8,128)(2,1)}, u32[]{:S(2)}) copy-start(bf16[3,96,128]{2,1,0:T(8,128)(2,1)} %get-tuple-element.14.own_ref) | copy-start | bytes 221188
  31.9 27.8 %copy-start.6 = (bf16[32,1728]{1,0:T(8,128)(2,1)S(1)}, bf16[32,1728]{1,0:T(8,128)(2,1)}, u32[]{:S(2)}) copy-start(bf16[32,1728]{1,0:T(8,128)(2,1)} %constant.125.clone) | copy-start | bytes 331780
  31.9 27.8 %copy-start.9 = (f32[1728]{0:T(1024)S(1)}, f32[1728]{0:T(1024)}, u32[]{:S(2)}) copy-start(f32[1728]{0:T(1024)} %constant.126.clone) | copy-start | bytes 20740
  31.9 21.0 %all-to-all-start.1 = ((bf16[8,160,128]{2,1,0:T(8,128)(2,1)}), bf16[8,160,128]{2,1,0:T(8,128)(2,1)S(1)}, u32[]{:S(2)}, u32[]{:S(2)}) async-start(bf16[8,160,128]{2,1,0:T(8,128)(2,1)} %place.1), calls=%async_computation.1 | async-start | bytes 655360 | tf_op jit(solution)/shard_map/all_to_all | solution.py:491
  53.7 18.2 %all-to-all-start.2 = ((bf16[4,432,128]{2,1,0:T(8,128)(2,1)}), bf16[4,432,128]{2,1,0:T(8,128)(2,1)S(1)}, u32[]{:S(2)}, u32[]{:S(2)}) async-start(bf16[4,432,128]{2,1,0:T(8,128)(2,1)} %join.1), calls=%async_computation.2 | async-start | bytes 884736 | tf_op jit(solution)/shard_map/all_to_all | solution.py:501
  61.8 10.2 %copy-start = (bf16[432,192]{1,0:T(8,128)(2,1)S(1)}, bf16[432,192]{1,0:T(8,128)(2,1)}, u32[]{:S(2)}) copy-start(bf16[432,192]{1,0:T(8,128)(2,1)} %constant.130.clone.down_ref) | copy-start | bytes 497668
  61.8 10.2 %copy-start.1 = (bf16[160,144]{1,0:T(8,128)(2,1)S(1)}, bf16[160,144]{1,0:T(8,128)(2,1)}, u32[]{:S(2)}) copy-start(bf16[160,144]{1,0:T(8,128)(2,1)} %constant.133.clone.cell_ref) | copy-start | bytes 138244
  61.8 10.2 %copy-start.3 = (bf16[160,48]{1,0:T(8,128)(2,1)S(1)}, bf16[160,48]{1,0:T(8,128)(2,1)}, u32[]{:S(2)}) copy-start(bf16[160,48]{1,0:T(8,128)(2,1)} %constant.131.clone.rim_ref) | copy-start | bytes 46084
  61.8 10.2 %copy-start.4 = (bf16[160,64]{1,0:T(8,128)(2,1)S(1)}, bf16[160,64]{1,0:T(8,128)(2,1)}, u32[]{:S(2)}) copy-start(bf16[160,64]{1,0:T(8,128)(2,1)} %constant.129.clone.shift_ref) | copy-start | bytes 61444
  61.8 10.2 %copy-start.5 = (bf16[48,64]{1,0:T(8,128)(2,1)S(1)}, bf16[48,64]{1,0:T(8,128)(2,1)}, u32[]{:S(2)}) copy-start(bf16[48,64]{1,0:T(8,128)(2,1)} %constant.132.clone.order_ref) | copy-start | bytes 18436
  78.8 5.6 %collective-permute-start = (bf16[1152,128]{1,0:T(8,128)(2,1)S(1)}, bf16[1152,128]{1,0:T(8,128)(2,1)S(1)}, u32[]{:S(2)}, u32[]{:S(2)}) collective-permute-start(bf16[1152,128]{1,0:T(8,128)(2,1)S(1)} %get-tuple-element.20), channel_id=1, source_target_pairs={{0,4},{4,0},{1,5},{5,1},{2,6},{6,2},{3,7},{7,3},{8,12},{12,8},{9,1... | collective-permute-start | bytes 884744 | tf_op jit(solution)/shard_map/ppermute | solution.py:514
Sparse Core Ops, SparseCore 0:
  10.7 46.5 all-gather.2

commit v12 on v11

--- a/solution.py
+++ b/solution.py
@@ -315,14 +315,9 @@
 
 
 def main_kernel(
-    pay_ref, rim_at_ref, shift_ref, down_ref, rim_ref, order_ref, cell_ref, wf, wd, window_hbm,
-    coarse_ref, gp_ref, kept_ref, given_ref, window_ref, xs, cs, wins, ups, rims, downs, gps, up, sems,
+    pay_ref, rim_at_ref, shift_ref, down_ref, rim_ref, order_ref, cell_ref, wf, wd, window_ref,
+    coarse_ref, gp_ref, kept_ref, given_ref, xs, cs, wins, ups, rims, downs, gps, up,
 ):
-    window_copies = [
-        pltpu.make_async_copy(window_hbm.at[t], window_ref.at[t], sems.at[t]) for t in range(TILES_HERE)
-    ]
-    for copy in window_copies:
-        copy.start()
     chan, core = lax.axis_index("chan"), lax.axis_index("core")
     pick = jnp.where(
         lax.broadcasted_iota(jnp.int32, (CH, C), 1) == lax.broadcasted_iota(jnp.int32, (CH, C), 0) + chan * CH, 1.0, 0.0
@@ -339,7 +334,6 @@
     for t in range(TILES_HERE):
         xs[t, 2 * X_HALF :, :] = jnp.zeros((C - 2 * X_HALF, C), BF)
     for t in range(TILES_HERE):
-        window_copies[t].wait()
         for k in range(9):
             wins[t * PRE_ROWS : (t + 1) * PRE_ROWS, k * C : (k + 1) * C] = dot_nn(
                 window_ref[t, k * PRE_ROWS : (k + 1) * PRE_ROWS, :], xs[t]
@@ -411,7 +405,7 @@
 
 LIMIT = pltpu.CompilerParams(vmem_limit_bytes=48 * 1024 * 1024)
 WHOLE = pltpu.CompilerParams(vmem_limit_bytes=60 * 1024 * 1024)
-MOST = pltpu.CompilerParams(vmem_limit_bytes=50 * 1024 * 1024)
+MOST = pltpu.CompilerParams(vmem_limit_bytes=40 * 1024 * 1024)
 
 
 def tiles_call(payload, window, rim_at, weights):
@@ -434,10 +428,9 @@
             jax.ShapeDtypeStruct((18 * CH, 128), BF),
             jax.ShapeDtypeStruct((18 * CH, 128), BF),
         ),
-        in_specs=vmem(9) + hbm(1),
+        in_specs=vmem(10),
         out_specs=tuple(vmem(4)),
         scratch_shapes=[
-            pltpu.VMEM((TILES_HERE, 9 * PRE_ROWS, C), BF),
             pltpu.VMEM((TILES_HERE, C, C), BF),
             pltpu.VMEM((TILES_HERE, 2 * C_HALF, C), BF),
             pltpu.VMEM((TILES_HERE * PRE_ROWS, 9 * C), BF),
@@ -446,7 +439,6 @@
             pltpu.VMEM((TILES_HERE * DOWN_ROWS, 9 * C), BF),
             pltpu.VMEM((TILES_HERE * PRE_ROWS, C), BF),
             pltpu.VMEM((TILES_HERE * DOWN_ROWS, C), BF),
-            pltpu.SemaphoreType.DMA((TILES_HERE,)),
         ],
         compiler_params=MOST,
         name="tiles",

time: 132 us -> 135 us (1.023)
  local copies, waits for them, and re-layouts: 2.25 us -> 10.2 us
  Pallas kernels: 13.9 us -> 10.9 us
    unnamed x20 -> x30, local copies, waits for them, and re-layouts: 0.04 us -> 7.95 us
    pallas_call x1, Pallas kernels: 6.76 us -> 5.24 us  [tiles_call(): pl.pallas_call(main_kernel, out_shape=(jax.ShapeDtypeStruct((TILES_HERE,...]
    pallas_call x1, Pallas kernels: 1.7 us -> 0.24 us  [tiles_call(): pl.pallas_call(hold_kernel, out_shape=(jax.ShapeDtypeStruct((9, C, C), BF...]
  transfers between devices with their start and end apart: 5 -> 5, of which waited for: 4 -> 4; matrix products, arithmetic and copies ran while one was open for 3% -> 3% of each run, Pallas kernels for 4% -> 3%
where the time goes in v12:
time: 135 us; the launch traced here: 134 us
  blocking collectives  46.7 us (35%)
  waiting for transfers between devices  26.1 us (19%)
  starting transfers between devices  23.6 us (17%)
  between operations  14.3 us (11%)
  Pallas kernels  10.9 us (8%)
  local copies, waits for them, and re-layouts  10.2 us (8%)
  other arithmetic  2.55 us (2%)
    all_to_all x1, waiting for transfers between devices, shards(): got = lax.all_to_all(sends, 'z', 0, 0)  13.3 us
    all_to_all x1, blocking collectives, shards(): lax.all_to_all(jnp.broadcast_to(part[None], (NZ, 144, 128)), 'z', 0, 0)  12.8 us
    all_to_all x1, blocking collectives, shards(): part = lax.all_to_all(part, ('ylo', 'x'), 0, 0)  10.7 us
    all_to_all x1, blocking collectives, shards(): lax.all_to_all(jnp.broadcast_to(part[None], (YX, 144, 128)), ('ylo', 'x')...  9.82 us
    unnamed x30, local copies, waits for them, and re-layouts  7.95 us
    all_gather x1, blocking collectives, shards(): units = lax.all_gather(units, 'core', axis=0, tiled=True)  7.54 us
    all_to_all x1, starting transfers between devices, shards(): got = lax.all_to_all(sends, 'z', 0, 0)  7.42 us
    all_to_all x1, waiting for transfers between devices, shards(): payload = lax.all_to_all(joined, 'chan', 0, 0)  7.23 us
  transfers between devices with their start and end apart: 5, of which 4 were waited for; matrix products, arithmetic and copies ran while one was open for 3% of the time, Pallas kernels for 3%

profile of v12, /device:TPU:1, one launch (start us, length us, event | category | flops | bytes accessed | tf_op | source)
XLA Modules:
  0.0 134.5 jit_solution(9295132033616401320)
XLA Ops:
  7.2 2.3 %pack.1 = (bf16[3,96,128]{2,1,0:T(8,128)(2,1)}, bf16[8,192,128]{2,1,0:T(8,128)(2,1)}, bf16[9,64,256]{2,1,0:T(8,128)(2,1)}) custom-call(bf16[3,64,144]{2,1,0:T(8,128)(2,1)} %fields_hbm.1, bf16[3,36,64]{2,1,0:T(8,128)(2,1)} %bitcast.35, bf16[9,64,256]{2,1,0:T(8,128)(2,1)} %first_ref.1, bf16[9,64,256]{2,1,0:T(8,128)(2,1)} %down_ref.2), custom_call_target="tpu_custom_call" | custom-call | tf_op jit(solution)/shard_map/pack/pallas_call | solution.py:450
  9.5 5.9 %all-to-all-start = ((bf16[8,192,128]{2,1,0:T(8,128)(2,1)}), bf16[8,192,128]{2,1,0:T(8,128)(2,1)S(1)}, u32[]{:S(2)}, u32[]{:S(2)}) async-start(bf16[8,192,128]{2,1,0:T(8,128)(2,1)} %get-tuple-element.13), calls=%async_computation | async-start | bytes 786432 | tf_op jit(solution)/shard_map/all_to_all | solution.py:471
  15.8 0.2 copy.33
  16.0 0.2 ne.70
  16.4 0.1 mul.88
  16.6 0.1 div.31
  17.7 4.3 %all-to-all-done = bf16[8,192,128]{2,1,0:T(8,128)(2,1)S(1)} async-done(((bf16[8,192,128]{2,1,0:T(8,128)(2,1)}), bf16[8,192,128]{2,1,0:T(8,128)(2,1)S(1)}, u32[]{:S(2)}, u32[]{:S(2)}) %all-to-all-start) | async-done | bytes 393248 | tf_op jit(solution)/shard_map/all_to_all | solution.py:471
  22.0 7.5 %all_gather.12.unit_ref = bf16[3072,128]{1,0:T(8,128)(2,1)S(1)} all-gather(bf16[1536,128]{1,0:T(8,128)(2,1)S(1)} %bitcast.30), channel_id=1, replica_groups=mesh['ylo'=2,'x'=4,'z'=8,'core'=2,'chan'=4] {'core'}, dimensions={0}, use_global_device_ids=true | all-gather | bytes 1179648 | tf_op jit(solution)/shard_map/all_gather | solution.py:472
  29.5 2.3 %place.1 = bf16[8,160,128]{2,1,0:T(8,128)(2,1)} custom-call(s32[1536]{0:T(1024)S(1)} %get-tuple-element.32.word_ref, s32[1536]{0:T(1024)S(1)} %get-tuple-element.31.beyond_ref, bf16[3072,128]{1,0:T(8,128)(2,1)S(1)} %all_gather.12.unit_ref), custom_call_target="tpu_custom_call" | custom-call | tf_op jit(solution)/shard_map/place/pallas_call | solution.py:474
  31.9 7.4 %all-to-all-start.1 = ((bf16[8,160,128]{2,1,0:T(8,128)(2,1)}), bf16[8,160,128]{2,1,0:T(8,128)(2,1)S(1)}, u32[]{:S(2)}, u32[]{:S(2)}) async-start(bf16[8,160,128]{2,1,0:T(8,128)(2,1)} %place.1), calls=%async_computation.1 | async-start | bytes 655360 | tf_op jit(solution)/shard_map/all_to_all | solution.py:483
  39.4 0.2 compare_convert_fusion.1.rim_at_ref
  39.6 13.3 %all-to-all-done.1.got_ref = bf16[8,160,128]{2,1,0:T(8,128)(2,1)S(1)} async-done(((bf16[8,160,128]{2,1,0:T(8,128)(2,1)}), bf16[8,160,128]{2,1,0:T(8,128)(2,1)S(1)}, u32[]{:S(2)}, u32[]{:S(2)}) %all-to-all-start.1) | async-done | bytes 327712 | tf_op jit(solution)/shard_map/all_to_all | solution.py:483
  52.9 0.8 join.1
  53.7 5.9 %all-to-all-start.2 = ((bf16[4,432,128]{2,1,0:T(8,128)(2,1)}), bf16[4,432,128]{2,1,0:T(8,128)(2,1)S(1)}, u32[]{:S(2)}, u32[]{:S(2)}) async-start(bf16[4,432,128]{2,1,0:T(8,128)(2,1)} %join.1), calls=%async_computation.2 | async-start | bytes 884736 | tf_op jit(solution)/shard_map/all_to_all | solution.py:493
  59.8 0.9 compare_convert_fusion.window_ref
  60.7 1.7 %copy-done = bf16[72,64,256]{2,1,0:T(8,128)(2,1)S(1)} copy-done((bf16[72,64,256]{2,1,0:T(8,128)(2,1)S(1)}, bf16[72,64,256]{2,1,0:T(8,128)(2,1)}, u32[]{:S(2)}) %copy-start) | copy-done | bytes 2359320
  62.4 0.2 hold.1
  62.7 1.0 copy-done.1
  63.7 1.0 copy-done.3
  64.7 7.2 %all-to-all-done.2.pay_ref = bf16[4,432,128]{2,1,0:T(8,128)(2,1)S(1)} async-done(((bf16[4,432,128]{2,1,0:T(8,128)(2,1)}), bf16[4,432,128]{2,1,0:T(8,128)(2,1)S(1)}, u32[]{:S(2)}, u32[]{:S(2)}) %all-to-all-start.2) | async-done | bytes 442400 | tf_op jit(solution)/shard_map/all_to_all | solution.py:493
  72.0 1.3 copy-done.2
  73.2 1.3 copy-done.4
  74.5 0.9 copy-done.6
  75.4 0.8 copy-done.9
  76.2 5.2 %tiles.1 = (bf16[3,36,64]{2,1,0:T(8,128)(2,1)}, bf16[3,64,144]{2,1,0:T(8,128)(2,1)}, bf16[1152,128]{1,0:T(8,128)(2,1)S(1)}, bf16[1152,128]{1,0:T(8,128)(2,1)S(1)}) custom-call(bf16[4,432,128]{2,1,0:T(8,128)(2,1)S(1)} %all-to-all-done.2.pay_ref, bf16[3,240,64]{2,1,0:T(8,128)(2,1)S(1)} %compare_convert_fusion.1.rim_at_ref, bf16[160,64]{1,0:T(8,128)(2,1)S(1)} %copy-done.9, ...), custom_call_target="tpu_custom_call" | custom-call | tf_op jit(solution)/shard_map/tiles/pallas_call | solution.py:423
  81.4 4.4 %collective-permute-start = (bf16[1152,128]{1,0:T(8,128)(2,1)S(1)}, bf16[1152,128]{1,0:T(8,128)(2,1)S(1)}, u32[]{:S(2)}, u32[]{:S(2)}) collective-permute-start(bf16[1152,128]{1,0:T(8,128)(2,1)S(1)} %get-tuple-element.20), channel_id=1, source_target_pairs={{0,4},{4,0},{1,5},{5,1},{2,6},{6,2},{3,7},{7,3},{8,12},{12,8},{9,1... | collective-permute-start | bytes 884744 | tf_op jit(solution)/shard_map/ppermute | solution.py:506
  85.8 1.2 collective-permute-done
  87.1 10.7 %all_to_all.30 = bf16[8,144,128]{2,1,0:T(8,128)(2,1)S(1)} all-to-all(bf16[8,144,128]{2,1,0:T(8,128)(2,1)S(1)} %bitcast.31), channel_id=1, replica_groups=mesh['ylo'=2,'x'=4,'z'=8,'core'=2,'chan'=4] {'ylo','x'}, dimensions={0} | all-to-all | bytes 589824 | tf_op jit(solution)/shard_map/all_to_all | solution.py:508
  97.9 12.8 %all_to_all.31 = bf16[8,144,128]{2,1,0:T(8,128)(2,1)S(1)} all-to-all(bf16[8,144,128]{2,1,0:T(8,128)(2,1)S(1)} %broadcast_in_dim.8), channel_id=1, replica_groups=mesh['ylo'=2,'x'=4,'z'=8,'core'=2,'chan'=4] {'z'}, dimensions={0} | all-to-all | bytes 589824 | tf_op jit(solution)/shard_map/all_to_all | solution.py:510
  110.7 9.8 %all_to_all.32 = bf16[8,144,128]{2,1,0:T(8,128)(2,1)S(1)} all-to-all(bf16[8,144,128]{2,1,0:T(8,128)(2,1)S(1)} %broadcast_in_dim.9), channel_id=1, replica_groups=mesh['ylo'=2,'x'=4,'z'=8,'core'=2,'chan'=4] {'ylo','x'}, dimensions={0} | all-to-all | bytes 589824 | tf_op jit(solution)/shard_map/all_to_all | solution.py:512
  120.6 5.8 %all_gather.15 = bf16[2,1152,128]{2,1,0:T(8,128)(2,1)S(1)} all-gather(bf16[1,1152,128]{2,1,0:T(8,128)(2,1)S(1)} %bitcast.32), channel_id=1, replica_groups=mesh['ylo'=2,'x'=4,'z'=8,'core'=2,'chan'=4] {'core'}, dimensions={0}, use_global_device_ids=true | all-gather | bytes 884736 | tf_op jit(solution)/shard_map/all_gather | solution.py:513
  126.5 1.1 slice_multiply_fusion
  (55 shorter events, 2.3 us)
Async XLA Ops:
  7.2 8.2 %copy-start.12 = (s32[384,4,3]{0,1,2:T(4,128)S(1)}, s32[384,4,3]{0,1,2:T(4,128)}, u32[]{:S(2)}) copy-start(s32[384,4,3]{0,1,2:T(4,128)} %param.15) | copy-start | bytes 55300
  7.2 53.5 %all-gather.3.cloned.1.call-start = ((), (), s32[]{:S(2)}) async-start(), calls=%async_computation.6 | async-start | bytes 2654208 | tf_op jit(solution)/shard_map/all_gather | solution.py:470
  9.5 12.5 %all-to-all-start = ((bf16[8,192,128]{2,1,0:T(8,128)(2,1)}), bf16[8,192,128]{2,1,0:T(8,128)(2,1)S(1)}, u32[]{:S(2)}, u32[]{:S(2)}) async-start(bf16[8,192,128]{2,1,0:T(8,128)(2,1)} %get-tuple-element.13), calls=%async_computation | async-start | bytes 786432 | tf_op jit(solution)/shard_map/all_to_all | solution.py:471
  29.5 9.8 %copy-start.13 = (bf16[32,240]{1,0:T(8,128)(2,1)S(1)}, bf16[32,240]{1,0:T(8,128)(2,1)}, u32[]{:S(2)}) copy-start(bf16[32,240]{1,0:T(8,128)(2,1)} %constant.127.clone) | copy-start | bytes 46084
  29.5 23.4 %copy-start.7 = (bf16[3,96,128]{2,1,0:T(8,128)(2,1)S(1)}, bf16[3,96,128]{2,1,0:T(8,128)(2,1)}, u32[]{:S(2)}) copy-start(bf16[3,96,128]{2,1,0:T(8,128)(2,1)} %get-tuple-element.14.own_ref) | copy-start | bytes 221188
  31.9 27.8 %copy-start.11 = (bf16[32,1728]{1,0:T(8,128)(2,1)S(1)}, bf16[32,1728]{1,0:T(8,128)(2,1)}, u32[]{:S(2)}) copy-start(bf16[32,1728]{1,0:T(8,128)(2,1)} %constant.125.clone) | copy-start | bytes 331780
  31.9 27.8 %copy-start.14 = (f32[1728]{0:T(1024)S(1)}, f32[1728]{0:T(1024)}, u32[]{:S(2)}) copy-start(f32[1728]{0:T(1024)} %constant.126.clone) | copy-start | bytes 20740
  31.9 21.0 %all-to-all-start.1 = ((bf16[8,160,128]{2,1,0:T(8,128)(2,1)}), bf16[8,160,128]{2,1,0:T(8,128)(2,1)S(1)}, u32[]{:S(2)}, u32[]{:S(2)}) async-start(bf16[8,160,128]{2,1,0:T(8,128)(2,1)} %place.1), calls=%async_computation.1 | async-start | bytes 655360 | tf_op jit(solution)/shard_map/all_to_all | solution.py:483
  53.7 18.2 %all-to-all-start.2 = ((bf16[4,432,128]{2,1,0:T(8,128)(2,1)}), bf16[4,432,128]{2,1,0:T(8,128)(2,1)S(1)}, u32[]{:S(2)}, u32[]{:S(2)}) async-start(bf16[4,432,128]{2,1,0:T(8,128)(2,1)} %join.1), calls=%async_computation.2 | async-start | bytes 884736 | tf_op jit(solution)/shard_map/all_to_all | solution.py:493
  60.7 1.7 %copy-start = (bf16[72,64,256]{2,1,0:T(8,128)(2,1)S(1)}, bf16[72,64,256]{2,1,0:T(8,128)(2,1)}, u32[]{:S(2)}) copy-start(bf16[72,64,256]{2,1,0:T(8,128)(2,1)} %all-gather.3.cloned.1.call-done) | copy-start | bytes 7077892
  62.4 9.6 %copy-start.5 = (bf16[432,192]{1,0:T(8,128)(2,1)S(1)}, bf16[432,192]{1,0:T(8,128)(2,1)}, u32[]{:S(2)}) copy-start(bf16[432,192]{1,0:T(8,128)(2,1)} %constant.130.clone.down_ref) | copy-start | bytes 497668
  62.4 9.6 %copy-start.8 = (bf16[160,48]{1,0:T(8,128)(2,1)S(1)}, bf16[160,48]{1,0:T(8,128)(2,1)}, u32[]{:S(2)}) copy-start(bf16[160,48]{1,0:T(8,128)(2,1)} %constant.131.clone.rim_ref) | copy-start | bytes 46084
  62.4 9.6 %copy-start.10 = (bf16[48,64]{1,0:T(8,128)(2,1)S(1)}, bf16[48,64]{1,0:T(8,128)(2,1)}, u32[]{:S(2)}) copy-start(bf16[48,64]{1,0:T(8,128)(2,1)} %constant.132.clone.order_ref) | copy-start | bytes 18436
  62.7 1.1 copy-start.1
  63.7 1.0 copy-start.3
  72.0 1.3 copy-start.2
  73.2 1.3 copy-start.4
  74.5 0.9 copy-start.6
  75.4 0.8 copy-start.9
  81.4 5.6 %collective-permute-start = (bf16[1152,128]{1,0:T(8,128)(2,1)S(1)}, bf16[1152,128]{1,0:T(8,128)(2,1)S(1)}, u32[]{:S(2)}, u32[]{:S(2)}) collective-permute-start(bf16[1152,128]{1,0:T(8,128)(2,1)S(1)} %get-tuple-element.20), channel_id=1, source_target_pairs={{0,4},{4,0},{1,5},{5,1},{2,6},{6,2},{3,7},{7,3},{8,12},{12,8},{9,1... | collective-permute-start | bytes 884744 | tf_op jit(solution)/shard_map/ppermute | solution.py:506
Sparse Core Ops, SparseCore 0:
  10.7 46.5 all-gather.2
